TPU v7x, 256 devices: a whole 4x4x8 slice. The times are simulated.
256 devices in a mesh: dp: 32 (over z, x), expert: 8 (over y, core).
Axes of the slice: x: 4, y: 4, z: 8, core: 2. Of those that a mesh axis runs over, the one named last changes fastest.
Arguments:
- tokens: bfloat16 [4096, 4096], P('dp'), may hold values from -6 to 6
- expert_ids: int32 [4096, 8], P('dp'), may hold values from 0 to 63, all different within a row; in each aligned block of 128 rows (0 to 127, 128 to 255, ...) at most 20 rows name the same one
- gates: float32 [4096, 8], P('dp'), may hold values from 0.02 to 0.25
- w_gate: bfloat16 [64, 1536, 4096], P('dp', 'expert'), may hold values from -0.09375 to 0.09375
- w_up: bfloat16 [64, 1536, 4096], P('dp', 'expert'), may hold values from -0.09375 to 0.09375
- w_down: bfloat16 [64, 1536, 4096], P('dp', 'expert'), may hold values from -0.15625 to 0.15625
- gate_scale: float32 [64, 1536], P('dp', 'expert'), may hold values from 0.5 to 2
- up_scale: float32 [64, 1536], P('dp', 'expert'), may hold values from 0.5 to 2
- down_scale: float32 [64, 4096], P('dp'), may hold values from 0.5 to 2
- kv_rows: bfloat16 [4096, 1024], P('dp', 'expert'), may hold values from -6 to 6
- page_slots: int32 [128], replicated, may hold values from 0 to 127, each once
Outputs:
- moe_out: bfloat16 [4096, 4096], P('dp', 'expert')
- kv_cache: bfloat16 [128, 32, 1024], P('dp', None, 'expert')
Inputs may be any that keep to these rules, and one draw needn't show every extreme that they name: `expert_ids`: in the 128 rows of one index of dp, no expert is named by more than 20 rows. `page_slots`: each cache page is named once; cache page c lies on index c // 4 of dp.
All inputs are finite; a program needn't handle non-finite values.
Results may differ from a plain program's by a relative error of at most 0.02.
Values may be sent and summed in bfloat16 or wider, within the bound.
No kernel may reach another device: no remote copies, remote signals or barrier semaphores. Data moves between devices by JAX's collectives and lax.ppermute only.
A program may use at most 128 MiB of HBM per device.

v0:
```python
import jax
import jax.numpy as jnp
from jax import lax
from jax.sharding import PartitionSpec as P

PAGE = 32


def on_device(
    tokens,
    expert_ids,
    gates,
    w_gate,
    w_up,
    w_down,
    gate_scale,
    up_scale,
    down_scale,
    kv_rows,
    page_slots,
):
    n_data = lax.axis_size("dp")
    n_group = lax.axis_size("expert")
    data_index = lax.axis_index("dp")
    tok_count = tokens.shape[0]
    picks = expert_ids.shape[1]
    local_experts = w_gate.shape[0]
    all_experts = local_experts * n_data
    width = tokens.shape[1]
    columns = width // n_group
    capacity = (tok_count * picks * 5 + 4 * all_experts - 1) // (4 * all_experts)
    flat_ids = expert_ids.reshape(-1)
    onehot = (flat_ids[:, None] == jnp.arange(all_experts, dtype=jnp.int32)[None, :]).astype(
        jnp.int32
    )
    ranks = jnp.cumsum(onehot, axis=0) - 1
    position = jnp.sum(ranks * onehot, axis=1)
    slot = flat_ids * capacity + position
    token_of = jnp.arange(tok_count * picks, dtype=jnp.int32) // picks
    slot_token = (
        jnp.full((all_experts * capacity,), tok_count, dtype=jnp.int32).at[slot].set(token_of)
    )
    padded = jnp.concatenate([tokens, jnp.zeros((1, tokens.shape[1]), tokens.dtype)], axis=0)
    arrived = lax.all_to_all(
        padded[slot_token].reshape(n_data, local_experts * capacity, tokens.shape[1]),
        "dp",
        split_axis=0,
        concat_axis=0,
        tiled=True,
    )
    arrived = arrived.reshape(n_data, local_experts, capacity, width)
    gate_act = jnp.einsum("secd,ehd->sech", arrived, w_gate, preferred_element_type=jnp.float32)
    up_act = jnp.einsum("secd,ehd->sech", arrived, w_up, preferred_element_type=jnp.float32)
    gate_act = gate_act * gate_scale[None, :, None, :]
    up_act = up_act * up_scale[None, :, None, :]
    hidden = (jax.nn.silu(gate_act) * up_act).astype(jnp.bfloat16)
    partial_value = jnp.einsum("sech,ehd->secd", hidden, w_down, preferred_element_type=jnp.float32)
    partial_value = (partial_value * down_scale[None, :, None, :]).astype(jnp.bfloat16)
    slot_pairs = slot.reshape(tok_count, picks)
    summed = lax.psum_scatter(partial_value, "expert", scatter_dimension=3, tiled=True).astype(
        jnp.float32
    )
    returned = lax.all_to_all(
        summed.reshape(n_data, local_experts * capacity, columns).astype(jnp.bfloat16),
        "dp",
        split_axis=0,
        concat_axis=0,
        tiled=True,
    ).astype(jnp.float32)
    returned = returned.reshape(all_experts * capacity, columns)
    chosen = returned[slot_pairs]
    mixed = jnp.sum(gates[:, :, None] * chosen, axis=1)
    moe_out = mixed.astype(jnp.bfloat16)
    pages_local = tok_count // PAGE
    kv_cols = kv_rows.shape[1]
    pages = kv_rows.reshape(pages_local, PAGE, kv_cols)
    own_slots = lax.dynamic_slice_in_dim(page_slots, data_index * pages_local, pages_local, 0)
    owner = own_slots // pages_local
    target = owner[None, :] == jnp.arange(n_data, dtype=jnp.int32)[:, None]
    outgoing = jnp.where(target[:, :, None, None], pages[None], jnp.zeros_like(pages[None]))
    incoming = lax.all_to_all(outgoing, "dp", split_axis=0, concat_axis=0, tiled=True)
    incoming = incoming.reshape(n_data * pages_local, PAGE * kv_cols)
    wanted = data_index * pages_local + jnp.arange(pages_local, dtype=jnp.int32)
    selector = (page_slots[None, :] == wanted[:, None]).astype(jnp.bfloat16)
    kv_cache = jnp.dot(selector, incoming, preferred_element_type=jnp.float32).astype(jnp.bfloat16)
    kv_cache = kv_cache.reshape(pages_local, PAGE, kv_cols)
    return (moe_out, kv_cache)


def solution(mesh):
    placed = (
        P("dp", None),
        P("dp", None),
        P("dp", None),
        P("dp", "expert", None),
        P("dp", "expert", None),
        P("dp", "expert", None),
        P("dp", "expert"),
        P("dp", "expert"),
        P("dp", None),
        P("dp", "expert"),
        P(),
    )
    return jax.shard_map(
        on_device,
        mesh=mesh,
        in_specs=placed,
        out_specs=(P("dp", "expert"), P("dp", None, "expert")),
        check_vma=False,
    )
```

profile of v0, /device:TPU:1, one launch (start us, length us, event | category | flops | bytes accessed | tf_op | source)
XLA Modules:
  0.0 476.2 jit_solution(17568854269729146190)
XLA Ops:
  7.2 0.0 copy-start
  7.2 0.0 reduce-scatter.2.cloned.1.call-start
  7.2 0.9 copy.25
  8.2 0.1 eq.59
  8.3 0.1 eq.55
  8.4 0.7 fusion.39
  9.1 30.8 %reduce-window.6 = s32[64,8,128]{2,1,0:T(8,128)S(1)} reduce-window(s32[64,8,128]{2,1,0:T(8,128)} %fusion.39, s32[]{:T(128)} %constant.52.clone.1), window={size=1x1x128 pad=0_0x0_0x127_0}, to_apply=%region_0.0 | reduce-window | flops 8323072 | bytes 524292 | tf_op jit(solution)/shard_map/reduce-window
  39.9 0.8 slice.12
  40.7 1.1 copy.28
  41.9 0.1 copy.29
  41.9 0.1 add_add_fusion
  42.1 0.1 fusion.38
  42.1 0.1 reduce_sum.24
  42.3 0.1 mul.73
  42.4 4.3 scatter_custom_fusion
  46.7 2.3 concatenate.3
  49.1 20.2 %gather_fusion = bf16[1280,4096]{1,0:T(8,128)(2,1)} fusion(bf16[129,4096]{1,0:T(8,128)(2,1)} %concatenate.3, s32[2048]{0:T(1024)S(1)} %pad_clamp_fusion), kind=kCustom, calls=%fused_computation | custom fusion | bytes 20976640 | tf_op jit(solution)/shard_map/gather | solution.py:45
  69.2 240.4 %all_to_all.15 = bf16[32,40,4096]{2,1,0:T(8,128)(2,1)} all-to-all(bf16[32,40,4096]{2,1,0:T(8,128)(2,1)} %bitcast.80), channel_id=1, replica_groups=mesh['dp'=32,'expert'=8] {'dp'}, dimensions={0} | all-to-all | bytes 20971520 | tf_op jit(solution)/shard_map/all_to_all | solution.py:44
  309.6 0.0 copy-start.5
  309.6 13.6 %copy.30 = bf16[32,40,4096]{2,0,1:T(8,128)(2,1)} copy(bf16[32,40,4096]{2,1,0:T(8,128)(2,1)} %all_to_all.15) | data formatting | bytes 20971520 | tf_op jit(solution)/shard_map/all_to_all | solution.py:44
  323.2 0.0 copy-done.5
  323.2 0.0 copy-start.4
  323.2 0.0 copy-start.6
  323.2 8.8 %fusion.19 = f32[32,2,20,192]{3,0,2,1:T(8,128)} fusion(bf16[32,2,20,4096]{3,0,2,1:T(8,128)(2,1)} %bitcast.81, bf16[2,192,4096]{2,1,0:T(8,128)(2,1)} %param.14, f32[2,192]{1,0:T(2,128)S(1)} %copy-done.5), kind=kOutput, calls=%fused_computation.17 | convolution fusion | flops 2013511680 | bytes 14616064 | tf_op jit(solution)/shard_map/secd,ehd->sech/dot_general | solution.py:52
  332.0 0.0 copy-done
  332.0 0.0 copy-done.4
  332.0 0.0 copy-done.6
  332.0 16.8 %fusion = bf16[32,2,20,4096]{3,0,2,1:T(8,128)(2,1)} fusion(f32[2,4096]{1,0:T(2,128)S(1)} %copy-done.4, bf16[2,192,4096]{2,1,0:T(8,128)(2,1)S(1)} %copy-done, bf16[32,2,20,4096]{3,0,2,1:T(8,128)(2,1)} %bitcast.82, bf16[2,192,4096]{2,1,0:T(8,128)(2,1)} %param.15, f32[32,2,20,192]{3,0,2,1:T(8,128)} %fusion.19, f32[2,192]{1,0:T(2,128)S(1)} %copy-done.6), kind=kOutput, calls=%fused_computation.4 | convolution fusion | flops 4038737920 | bytes 28280320 | tf_op jit(solution)/shard_map/sech,ehd->secd/dot_general | solution.py:57
  348.8 0.0 copy-start.3
  348.8 0.0 reduce-scatter.2.cloned.1.call-update
  348.8 0.6 copy-done.3
  349.5 0.1 and_select_fusion
  349.6 0.0 copy-done.1
  349.6 1.3 broadcast_select_fusion
  350.8 6.5 %all-to-all-start.2 = ((bf16[32,4,32,128]{3,2,1,0:T(8,128)(2,1)}), bf16[32,4,32,128]{3,2,1,0:T(8,128)(2,1)}, u32[]{:S(2)}, u32[]{:S(2)}) async-start(bf16[32,4,32,128]{3,2,1,0:T(8,128)(2,1)} %broadcast_select_fusion), calls=%async_computation.3 | async-start | bytes 2097152 | tf_op jit(solution)/shard_map/all_to_all | solution.py:81
  357.3 55.4 %reduce-scatter.2.cloned.1.call-done = bf16[32,2,20,512]{3,0,2,1:T(8,128)(2,1)} async-done(((bf16[32,2,20,4096]{3,0,2,1:T(8,128)(2,1)}), bf16[32,2,20,512]{3,0,2,1:T(8,128)(2,1)}) %reduce-scatter.2.cloned.1.call-update) | async-done | bytes 1310736 | tf_op jit(solution)/shard_map/reduce_scatter | solution.py:60
  412.8 3.1 copy.31
  415.9 0.0 all-to-all-done.2
  415.9 9.7 %all-to-all-start.1 = ((bf16[32,40,512]{2,1,0:T(8,128)(2,1)}), bf16[32,40,512]{2,1,0:T(8,128)(2,1)}, u32[]{:S(2)}, u32[]{:S(2)}) async-start(bf16[32,40,512]{2,1,0:T(8,128)(2,1)} %copy.31), calls=%async_computation.2 | async-start | bytes 2621440 | tf_op jit(solution)/shard_map/all_to_all | solution.py:63
  425.5 0.1 reshape.121
  425.6 0.0 copy-done.2
  425.6 0.1 copy.24
  425.8 1.6 fusion.32
  427.4 0.6 copy.44
  428.0 28.2 %all-to-all-done.1 = bf16[32,40,512]{2,1,0:T(8,128)(2,1)} async-done(((bf16[32,40,512]{2,1,0:T(8,128)(2,1)}), bf16[32,40,512]{2,1,0:T(8,128)(2,1)}, u32[]{:S(2)}, u32[]{:S(2)}) %all-to-all-start.1) | async-done | bytes 1310752 | tf_op jit(solution)/shard_map/all_to_all | solution.py:63
  456.2 3.2 bitcast_convert_fusion
  459.4 7.0 %gather_fusion.1 = f32[1024,512]{1,0:T(8,128)} fusion(f32[1280,512]{1,0:T(8,128)} %bitcast_convert_fusion, s32[1024]{0:T(1024)S(1)} %broadcast_clamp_fusion), kind=kCustom, calls=%fused_computation.1 | custom fusion | bytes 4198400 | tf_op jit(solution)/shard_map/gather | solution.py:71
  466.5 2.9 fusion.6
  (12 shorter events, 0.1 us)
Async XLA Ops:
  7.2 324.9 %copy-start = (bf16[2,192,4096]{2,1,0:T(8,128)(2,1)S(1)}, bf16[2,192,4096]{2,1,0:T(8,128)(2,1)}, u32[]{:S(2)}) copy-start(bf16[2,192,4096]{2,1,0:T(8,128)(2,1)} %param.16) | copy-start | bytes 9437188
  7.2 405.6 %reduce-scatter.2.cloned.1.call-start = ((), (), s32[]{:S(2)}) async-start(), calls=%async_computation.4 | async-start | bytes 11796480 | tf_op jit(solution)/shard_map/reduce_scatter | solution.py:60
  309.6 13.6 %copy-start.5 = (f32[2,192]{1,0:T(2,128)S(1)}, f32[2,192]{1,0:T(2,128)}, u32[]{:S(2)}) copy-start(f32[2,192]{1,0:T(2,128)} %param.17) | copy-start | bytes 4612
  323.2 8.8 %copy-start.4 = (f32[2,4096]{1,0:T(2,128)S(1)}, f32[2,4096]{1,0:T(2,128)}, u32[]{:S(2)}) copy-start(f32[2,4096]{1,0:T(2,128)} %param.19) | copy-start | bytes 98308
  323.2 8.8 %copy-start.6 = (f32[2,192]{1,0:T(2,128)S(1)}, f32[2,192]{1,0:T(2,128)}, u32[]{:S(2)}) copy-start(f32[2,192]{1,0:T(2,128)} %param.18) | copy-start | bytes 4612
  348.8 0.7 copy-start.3
  348.8 0.8 copy-start.1
  350.8 65.0 %all-to-all-start.2 = ((bf16[32,4,32,128]{3,2,1,0:T(8,128)(2,1)}), bf16[32,4,32,128]{3,2,1,0:T(8,128)(2,1)}, u32[]{:S(2)}, u32[]{:S(2)}) async-start(bf16[32,4,32,128]{3,2,1,0:T(8,128)(2,1)} %broadcast_select_fusion), calls=%async_computation.3 | async-start | bytes 2097152 | tf_op jit(solution)/shard_map/all_to_all | solution.py:81
  412.8 12.9 %copy-start.2 = (f32[128,8]{0,1:T(8,128)S(1)}, f32[128,8]{0,1:T(8,128)}, u32[]{:S(2)}) copy-start(f32[128,8]{0,1:T(8,128)} %param.13) | copy-start | bytes 12292
  415.9 40.4 %all-to-all-start.1 = ((bf16[32,40,512]{2,1,0:T(8,128)(2,1)}), bf16[32,40,512]{2,1,0:T(8,128)(2,1)}, u32[]{:S(2)}, u32[]{:S(2)}) async-start(bf16[32,40,512]{2,1,0:T(8,128)(2,1)} %copy.31), calls=%async_computation.2 | async-start | bytes 2621440 | tf_op jit(solution)/shard_map/all_to_all | solution.py:63
Sparse Core Ops, SparseCore 0:
  349.0 63.7 reduce-scatter.1
where the time goes:
time: 481 us; the launch traced here: 476 us
  blocking collectives  240 us (50%)
  waiting for transfers between devices  83.7 us (17%)
  local copies, waits for them, and re-layouts  55.3 us (11%)
  other arithmetic  39.3 us (8%)
  matrix products  27.2 us (6%)
  starting transfers between devices  16.2 us (3%)
  between operations  14.2 us (3%)
    all_to_all x1, blocking collectives, on_device(): lax.all_to_all(padded[slot_token].reshape(n_data, local_experts * capacit...  240 us
    reduce_scatter x1, waiting for transfers between devices, on_device(): lax.psum_scatter(partial_value, 'expert', scatter_dimension=3, tiled=True)  55.4 us
    another operation x2, other arithmetic  30.9 us
    all_to_all x1, waiting for transfers between devices, on_device(): lax.all_to_all(summed.reshape(n_data, local_experts * capacity, columns)....  28.2 us
    gather x1, local copies, waits for them, and re-layouts, on_device(): padded[slot_token]  20.2 us
    dot_general x1, matrix products, on_device(): jnp.einsum('sech,ehd->secd', hidden, w_down, preferred_element_type=jnp.f...  16.8 us
    all_to_all x1, local copies, waits for them, and re-layouts, on_device(): lax.all_to_all(padded[slot_token].reshape(n_data, local_experts * capacit...  13.6 us
    all_to_all x1, starting transfers between devices, on_device(): lax.all_to_all(summed.reshape(n_data, local_experts * capacity, columns)....  9.66 us
  transfers between devices with their start and end apart: 3, of which 2 were waited for; matrix products, arithmetic and copies ran while one was open for 1% of the time, Pallas kernels for 0%

commit v1 on v0

v1 whole, which is shorter than its diff:
```python
import functools

import jax
import jax.numpy as jnp
import numpy as np
from jax import lax
from jax.experimental import pallas as pl
from jax.experimental.pallas import tpu as pltpu
from jax.sharding import Mesh
from jax.sharding import PartitionSpec as P

BF = jnp.bfloat16
F32 = jnp.float32
PAGE = 32
ROWS = 8
DP = ("z", "x")
MOVES = ((0, False), (0, True), (1, False), (1, True), (3, False), (3, True), (2, False), (2, True))


def dot(a, b):
    return lax.dot_general(a, b, (((1,), (0,)), ((), ())), preferred_element_type=F32)


def dot_nt(a, b):
    return lax.dot_general(a, b, (((1,), (1,)), ((), ())), preferred_element_type=F32)


def dot_tn(a, b):
    return lax.dot_general(a, b, (((0,), (0,)), ((), ())), preferred_element_type=F32)


def iota(shape, dim):
    return lax.broadcasted_iota(jnp.int32, shape, dim)


def ones(cond, dtype=BF):
    return jnp.where(cond, 1.0, 0.0).astype(dtype)


def slot_codes(ids_t, parity, n_dst, none):
    picks, tok = ids_t.shape
    expert = 2 * iota((n_dst, tok), 0) + parity
    named = jnp.zeros((n_dst, tok), F32)
    for k in range(picks):
        named = named + ones(ids_t[k : k + 1, :] == expert, F32)
    earlier = ones(iota((tok, tok), 0) < iota((tok, tok), 1))
    place = dot(named.astype(BF), earlier)
    code = jnp.where(named > 0, place, none)
    spread = ones((iota((n_dst * ROWS, n_dst), 0) // ROWS) == iota((n_dst * ROWS, n_dst), 1))
    return dot(spread, code.astype(BF)), spread


def selections(code):
    row = iota(code.shape, 0) % ROWS
    slot = row.astype(F32)
    low = row < 4
    return (
        code == slot,
        code == slot + 8.0,
        (code == slot + 16.0) & low,
        (code == slot + 12.0) & jnp.logical_not(low),
    )


def route_kernel(n_dst, place_ref, ids_ref, tok_hbm, kv_ref, out_ref, tok_ref, sem):
    quarter = tok_ref.shape[1]
    half = quarter // 2
    cols = pl.ds(pl.multiple_of(place_ref[0] * quarter, quarter), quarter)
    copy = pltpu.make_async_copy(tok_hbm.at[:, cols], tok_ref, sem)
    copy.start()
    code, _ = slot_codes(ids_ref[...], place_ref[1], n_dst, 200.0)
    first, second, low, high = selections(code)
    n, t = code.shape
    row, col = iota((n, t), 0), iota((n, t), 1)
    piece = (col == (row % ROWS) * PAGE + row // ROWS) & (row % ROWS < t // PAGE)
    out_ref[:, 2 * quarter + half :] = dot(ones(piece), kv_ref[...]).astype(BF)
    copy.wait()
    tok = tok_ref[...]
    out_ref[:, :quarter] = dot(ones(first), tok).astype(BF)
    out_ref[:, quarter : 2 * quarter] = dot(ones(second), tok).astype(BF)
    out_ref[:, 2 * quarter : 2 * quarter + half] = (
        dot(ones(low), tok[:, :half]) + dot(ones(high), tok[:, half:])
    ).astype(BF)


def weights_kernel(place_ref, wg_ref, wu_ref, wd_ref, *refs):
    outs, sems = refs[:-1], refs[-1]
    y, core = place_ref[0], place_ref[1]
    quarter = outs[2].shape[1]
    copies = []
    for i, (by, other) in enumerate(MOVES):
        to_y = lax.rem(y + by, 4)
        to_core = 1 - core if other else core
        cols = pl.ds(pl.multiple_of(to_y * quarter, quarter), quarter)
        copies.append((wd_ref.at[to_core, :, cols], outs[2 + i]))
    copies += [(wg_ref.at[1 - core], outs[0]), (wu_ref.at[1 - core], outs[1])]
    copies = [pltpu.make_async_copy(a, b, sems.at[i]) for i, (a, b) in enumerate(copies)]
    for c in copies:
        c.start()
    for c in copies:
        c.wait()


def unpack_kernel(in_ref, slots_ref, p_ref, q_ref, kv_ref):
    n = in_ref.shape[0]
    quarter = p_ref.shape[1]
    half = quarter // 2
    p_ref[...] = in_ref[:, :quarter]
    q_ref[:n] = in_ref[:, quarter : 2 * quarter]
    m = n // 2
    row, col = iota((m, n), 0), iota((m, n), 1)
    at = (row // 4) * ROWS + row % 4
    mixed = in_ref[:, 2 * quarter : 2 * quarter + half]
    q_ref[n:, :half] = dot(ones(col == at), mixed).astype(BF)
    q_ref[n:, half:] = dot(ones(col == at + 4), mixed).astype(BF)
    pages = slots_ref.shape[1]
    row, col = iota((pages, n), 0), iota((pages, n), 1)
    held = col % ROWS < 4
    spread = ones(held & (row == (col // ROWS) * 4 + col % ROWS))
    slots = jnp.broadcast_to(slots_ref[...].astype(F32), (8, pages)).astype(BF)
    slots = jnp.where(held[0:1], dot(slots, spread)[0:1], -2.0)
    row = iota((n, n), 0)
    wanted = jnp.where(row % ROWS < 4, (row // ROWS) * 4 + row % ROWS, -1).astype(F32)
    kv_ref[...] = dot(ones(slots == wanted), in_ref[:, 2 * quarter + half :]).astype(BF)


def up_kernel(
    place_ref, own_ref, left_ref, right_ref, far_ref, wg_ref, wg2_ref, wu_ref, wu2_ref, s_ref, out_ref, g_ref, u_ref
):
    k = pl.program_id(0)

    def step(x_ref, first):
        x = x_ref[...]
        g = dot_nt(x, jnp.concatenate([wg_ref[0], wg2_ref[...]], axis=0))
        u = dot_nt(x, jnp.concatenate([wu_ref[0], wu2_ref[...]], axis=0))
        if first:
            g_ref[...], u_ref[...] = g, u
        else:
            g_ref[...] += g
            u_ref[...] += u

    for i, ref in enumerate((own_ref, left_ref, right_ref, far_ref)):
        pl.when(k == i)(functools.partial(step, ref, i == 0))

    @pl.when(k == 3)
    def _():
        g = g_ref[...] * s_ref[0:1, :]
        u = u_ref[...] * s_ref[1:2, :]
        out_ref[...] = (g / (1.0 + jnp.exp(-g)) * u).astype(BF)


def down_sum(refs):
    acc = None
    for i in range(4):
        w = jnp.concatenate([refs[4 + 2 * i][...], refs[5 + 2 * i][...]], axis=0)
        part = dot(refs[i][...], w)
        acc = part if acc is None else acc + part
    return (acc * refs[12][0]).astype(BF)


def down_kernel(place_ref, *refs):
    refs[13][...] = down_sum(refs)


def down_pack_kernel(place_ref, *refs):
    y = down_sum(refs)
    kv_ref, out_ref = refs[13:]
    n, quarter = kv_ref.shape[0], y.shape[1]
    half = quarter // 2
    out_ref[:, :quarter] = y[:n]
    rest = y[n:]
    m = n // 2
    row, col = iota((n, m), 0), iota((n, m), 1)
    hit = col == (row // ROWS) * 4 + row % 4
    low = row % ROWS < 4
    out_ref[:, quarter : quarter + half] = (
        dot(ones(hit & low), rest[:, :half]) + dot(ones(hit & jnp.logical_not(low)), rest[:, half:])
    ).astype(BF)
    out_ref[:, quarter + half :] = kv_ref[...]


def combine_kernel(n_dst, place_ref, ids_ref, gates_ref, p_ref, q_ref, keep_ref, send_ref, kv_ref):
    parity = place_ref[1]
    ids, gates = ids_ref[...], gates_ref[...]
    code, spread = slot_codes(ids, parity, n_dst, 200.0)
    picks, tok = ids.shape
    expert = 2 * iota((n_dst, tok), 0) + parity
    gate = jnp.zeros((n_dst, tok), F32)
    for k in range(picks):
        gate = gate + jnp.where(ids[k : k + 1, :] == expert, gates[k : k + 1, :], 0.0)
    top = gate.astype(BF)
    rest = (gate - top.astype(F32)).astype(BF)
    top, rest = dot(spread, top), dot(spread, rest)
    first, second, low, high = selections(code)

    def mix(where, rows):
        return dot_tn(jnp.where(where, top, 0.0).astype(BF), rows) + dot_tn(
            jnp.where(where, rest, 0.0).astype(BF), rows
        )

    quarter = p_ref.shape[1]
    half = quarter // 2
    mixed = q_ref[:, quarter : quarter + half]
    sums = []
    for where, lo in ((low, 0), (high, half)):
        cols = slice(lo, lo + half)
        sums.append(mix(first, p_ref[:, cols]) + mix(second, q_ref[:, cols]) + mix(where, mixed))
    even = parity == 0
    keep_ref[...] = jnp.where(even, sums[0], sums[1])
    send_ref[...] = jnp.where(even, sums[1], sums[0])
    n = q_ref.shape[0]
    row, col = iota((tok, n), 0), iota((tok, n), 1)
    kv_ref[...] = dot(ones(col == (row % PAGE) * ROWS + row // PAGE), q_ref[:, quarter + half :]).astype(BF)


def sds(*shape, dtype=BF):
    return jax.ShapeDtypeStruct(shape, dtype)


def whole(*shape):
    return pl.BlockSpec(shape, lambda *a: (0,) * len(shape))


PARAMS = pltpu.CompilerParams(vmem_limit_bytes=62 * 1024 * 1024)


def on_device(
    tokens, expert_ids, gates, w_gate, w_up, w_down, gate_scale, up_scale, down_scale, kv_rows, page_slots
):
    y, core = lax.axis_index("y"), lax.axis_index("core")
    n_dp = lax.axis_size("z") * lax.axis_size("x")
    n_y, n_core = lax.axis_size("y"), lax.axis_size("core")
    tok, width = tokens.shape
    quarter = width // n_y
    half = quarter // 2
    experts, hid = w_gate.shape[:2]
    kv_cols = kv_rows.shape[1]
    rows = n_dp * ROWS
    place = jnp.stack([y, core]).astype(jnp.int32)
    ids_t, gates_t = expert_ids.T, gates.T
    picks = ids_t.shape[0]

    payload = 2 * quarter + half + kv_cols
    hbm = pl.BlockSpec(memory_space=pltpu.HBM)
    vmem = pl.BlockSpec(memory_space=pltpu.VMEM)
    smem = pl.BlockSpec(memory_space=pltpu.SMEM)
    with jax.named_scope("route"):
        outgoing = pl.pallas_call(
            functools.partial(route_kernel, n_dp),
            in_specs=[smem, vmem, hbm, vmem],
            out_specs=vmem,
            out_shape=sds(rows, payload),
            scratch_shapes=[pltpu.VMEM((tok, quarter), BF), pltpu.SemaphoreType.DMA],
            compiler_params=PARAMS,
        )(place, ids_t, tokens, kv_rows)

    def exchange(v):
        return lax.all_to_all(v.reshape(n_dp, ROWS, v.shape[-1]), DP, 0, 0, tiled=True).reshape(v.shape)

    with jax.named_scope("dispatch"):
        arrived = exchange(outgoing)

    swap = [(0, 1), (1, 0)]
    with jax.named_scope("weights"):
        parts = pl.pallas_call(
            weights_kernel,
            in_specs=[smem, hbm, hbm, hbm],
            out_specs=[vmem] * 10,
            out_shape=[sds(hid, width)] * 2 + [sds(hid, quarter)] * 8,
            scratch_shapes=[pltpu.SemaphoreType.DMA((10,))],
            compiler_params=PARAMS,
        )(place, w_gate, w_up, w_down)
        wd = [parts[2]]
        for (by, other), v in zip(MOVES[1:], parts[3:]):
            pairs = [
                (i * n_core + c, (i + by) % n_y * n_core + (1 - c if other else c))
                for i in range(n_y)
                for c in range(n_core)
            ]
            wd.append(lax.ppermute(v, ("y", "core"), pairs))
        wg2 = lax.ppermute(parts[0], "core", swap)
        wu2 = lax.ppermute(parts[1], "core", swap)
        both = jnp.stack([gate_scale, up_scale])
        own = lax.dynamic_index_in_dim(both, core, 1, keepdims=False)
        other = lax.ppermute(lax.dynamic_index_in_dim(both, 1 - core, 1, keepdims=False), "core", swap)
        scales = jnp.concatenate([own, other], axis=1)

    def after(v, *others):
        return lax.optimization_barrier((v, *others))[0]

    with jax.named_scope("unpack"):
        x_p, x_q, kv_q = pl.pallas_call(
            unpack_kernel,
            out_shape=[sds(rows, quarter), sds(rows + rows // 2, quarter), sds(rows, kv_cols)],
            compiler_params=PARAMS,
        )(after(arrived, *wd, wg2, wu2, scales), page_slots.reshape(1, -1))

    def shift(v, by):
        return lax.ppermute(v, "y", [(i, (i + by) % n_y) for i in range(n_y)])

    with jax.named_scope("rows"):
        p_left, p_right = shift(x_p, 1), shift(x_p, -1)
        x_q = after(x_q, p_left, p_right)
        p_far = shift(p_left, 1)
        q_left, q_right = shift(x_q, 1), shift(x_q, -1)
        q_far = shift(q_right, -1)

    def piece(k, p):
        return (p[0] + jnp.where(k == 0, 0, jnp.where(k == 1, 3, jnp.where(k == 2, 1, 2)))) % 4

    units = n_core * hid

    def up(pieces):
        r = pieces[0].shape[0]
        return pl.pallas_call(
            up_kernel,
            grid_spec=pltpu.PrefetchScalarGridSpec(
                num_scalar_prefetch=1,
                grid=(4,),
                in_specs=[whole(r, quarter)] * 4
                + [
                    pl.BlockSpec((1, hid, quarter), lambda k, p: (p[1], 0, piece(k, p))),
                    pl.BlockSpec((hid, quarter), lambda k, p: (0, piece(k, p))),
                ]
                * 2
                + [whole(2, units)],
                out_specs=whole(r, units),
                scratch_shapes=[pltpu.VMEM((r, units), F32)] * 2,
            ),
            out_shape=sds(r, units),
            compiler_params=PARAMS,
        )(place, *pieces, w_gate, wg2, w_up, wu2, scales)

    def down(pieces, kv=None):
        r = pieces[0].shape[0]
        shape = (r, quarter) if kv is None else (rows, quarter + half + kv_cols)
        return pl.pallas_call(
            down_kernel if kv is None else down_pack_kernel,
            grid_spec=pltpu.PrefetchScalarGridSpec(
                num_scalar_prefetch=1,
                grid=(1,),
                in_specs=[whole(r, units)] * 4
                + [whole(hid, quarter)] * 8
                + [pl.BlockSpec((1, 1, quarter), lambda k, p: (p[1], 0, p[0]))]
                + ([] if kv is None else [whole(rows, kv_cols)]),
                out_specs=whole(*shape),
            ),
            out_shape=sds(*shape),
            compiler_params=PARAMS,
        )(place, *pieces, *wd, down_scale.reshape(experts, 1, width), *([] if kv is None else [kv]))

    def hidden_pieces(h):
        return h, shift(h, 1), shift(h, -1), shift(h, 2)

    out = []
    for pieces, kv in (((x_p, p_left, p_right, p_far), None), ((x_q, q_left, q_right, q_far), kv_q)):
        with jax.named_scope("up"):
            h = up(pieces)
        with jax.named_scope("down"):
            v = down(hidden_pieces(h), kv)
        with jax.named_scope("back"):
            out.append(exchange(v))

    with jax.named_scope("combine"):
        keep, send, kv_cache = pl.pallas_call(
            functools.partial(combine_kernel, n_dp),
            in_specs=[pl.BlockSpec(memory_space=pltpu.SMEM)] + [pl.BlockSpec(memory_space=pltpu.VMEM)] * 4,
            out_shape=[sds(tok, half, dtype=F32), sds(tok, half, dtype=F32), sds(tok, kv_cols)],
            compiler_params=PARAMS,
        )(place, ids_t, gates_t, *out)
        moe_out = (keep + lax.ppermute(send, "core", [(0, 1), (1, 0)])).astype(BF)
    return moe_out, kv_cache.reshape(tok // PAGE, PAGE, kv_cols)


def solution(mesh):
    shape = mesh.devices.shape
    n_z, n_x, n_y = 8, 4, 4
    fine = Mesh(np.asarray(mesh.devices).reshape(n_z, n_x, n_y, shape[1] // n_y), ("z", "x", "y", "core"))
    group = ("y", "core")
    placed = (
        P(DP, None),
        P(DP, None),
        P(DP, None),
        P(DP, group, None),
        P(DP, group, None),
        P(DP, group, None),
        P(DP, group),
        P(DP, group),
        P(DP, None),
        P(DP, group),
        P(),
    )
    return jax.shard_map(
        on_device,
        mesh=fine,
        in_specs=placed,
        out_specs=(P(DP, group), P(DP, None, group)),
        check_vma=False,
    )
```

time: 481 us -> 213 us (0.44)
  blocking collectives: 240 us -> 31.6 us
  local copies, waits for them, and re-layouts: 55.3 us -> 4.03 us
  Pallas kernels: 0 us -> 42.6 us
  other arithmetic: 39.3 us -> 2.94 us
  starting transfers between devices: 16.2 us -> 48 us
  matrix products: 27.2 us -> 0 us
  between operations: 14.2 us -> 0.76 us
    all_to_all x1, blocking collectives: 240 us -> 31.6 us  [exchange(): lax.all_to_all(v.reshape(n_dp, ROWS, v.shape[-1]), DP, 0, 0, tiled=True)]
    ppermute x0 -> x23, waiting for transfers between devices: none -> 82.6 us  [the longest x12 51 us: shift(): return lax.ppermute(v, 'y', [(i, (i + by) % n_y) for i in range(n_y)])]
    reduce_scatter x1 -> x0, waiting for transfers between devices: 55.4 us -> none  [on_device(): lax.psum_scatter(partial_value, 'expert', scatter_dimension=3, tiled=True)]
    pallas_call x0 -> x8, Pallas kernels: none -> 42.6 us  [the longest x2 15.7 us: up(): pl.pallas_call(up_kernel, grid_spec=pltpu.PrefetchScalarGridSpec(num_scal...]
    another operation x2, other arithmetic: 30.9 us -> 0.63 us  [the longest x1 0.61 us: on_device(): place = jnp.stack([y, core]).astype(jnp.int32)]
    all_to_all x2, waiting for transfers between devices: 28.2 us -> 0.01 us  [exchange(): lax.all_to_all(v.reshape(n_dp, ROWS, v.shape[-1]), DP, 0, 0, tiled=True)]
    dot_general x3 -> x0, matrix products: 27.2 us -> none  [the longest x1 16.8 us: on_device(): jnp.einsum('sech,ehd->secd', hidden, w_down, preferred_element_type=jnp.f...]
    gather x2 -> x0, local copies, waits for them, and re-layouts: 27.2 us -> none  [the longest x1 20.2 us: on_device(): padded[slot_token]]
  transfers between devices with their start and end apart: 3 -> 25, of which waited for: 2 -> 16; matrix products, arithmetic and copies ran while one was open for 1% -> 1% of each run, Pallas kernels for 0% -> 15%
where the time goes in v1:
time: 213 us
  waiting for transfers between devices  82.6 us (39%)
  starting transfers between devices  48 us (23%)
  Pallas kernels  42.6 us (20%)
  blocking collectives  31.6 us (15%)
  local copies, waits for them, and re-layouts  4.03 us (2%)
  other arithmetic  2.94 us (1%)
    ppermute x12, waiting for transfers between devices, shift(): return lax.ppermute(v, 'y', [(i, (i + by) % n_y) for i in range(n_y)])  51 us
    all_to_all x1, blocking collectives, exchange(): lax.all_to_all(v.reshape(n_dp, ROWS, v.shape[-1]), DP, 0, 0, tiled=True)  31.6 us
    ppermute x7, waiting for transfers between devices, on_device(): wd.append(lax.ppermute(v, ('y', 'core'), pairs))  27.9 us
    all_to_all x2, starting transfers between devices, exchange(): lax.all_to_all(v.reshape(n_dp, ROWS, v.shape[-1]), DP, 0, 0, tiled=True)  21.4 us
    pallas_call x2, Pallas kernels, up(): pl.pallas_call(up_kernel, grid_spec=pltpu.PrefetchScalarGridSpec(num_scal...  15.7 us
    ppermute x7, starting transfers between devices, on_device(): wd.append(lax.ppermute(v, ('y', 'core'), pairs))  11.9 us
    pallas_call x2, Pallas kernels, down(): pl.pallas_call(down_kernel if kv is None else down_pack_kernel, grid_spec...  10.7 us
    ppermute x12, starting transfers between devices, shift(): return lax.ppermute(v, 'y', [(i, (i + by) % n_y) for i in range(n_y)])  10.3 us
  transfers between devices with their start and end apart: 25, of which 16 were waited for; matrix products, arithmetic and copies ran while one was open for 1% of the time, Pallas kernels for 15%

profile of v1, /device:TPU:1, one launch (start us, length us, event | category | flops | bytes accessed | tf_op | source)
XLA Modules:
  0.0 212.5 jit_solution(8687416215260501015)
XLA Ops:
  1.2 3.4 %route.1 = bf16[256,2688]{1,0:T(8,128)(2,1)} custom-call(s32[2]{0:T(128)} %pad_add_fusion.place_ref, s32[8,128]{1,0:T(8,128)} %bitcast.25, bf16[128,4096]{1,0:T(8,128)(2,1)} %tok_hbm.1, bf16[128,128]{1,0:T(8,128)(2,1)} %kv_ref.1), custom_call_target="tpu_custom_call" | custom-call | tf_op jit(solution)/shard_map/route/pallas_call | solution.py:248
  4.6 12.0 %all-to-all-start = ((bf16[32,8,2688]{2,1,0:T(8,128)(2,1)}), bf16[32,8,2688]{2,1,0:T(8,128)(2,1)}, u32[]{:S(2)}, u32[]{:S(2)}) async-start(bf16[32,8,2688]{2,1,0:T(8,128)(2,1)} %bitcast.20), calls=%async_computation | async-start | bytes 2752512 | tf_op jit(solution)/shard_map/dispatch/all_to_all | solution.py:258
  16.7 6.3 %weights.1 = (bf16[192,4096]{1,0:T(8,128)(2,1)}, bf16[192,4096]{1,0:T(8,128)(2,1)}, bf16[192,1024]{1,0:T(8,128)(2,1)}, bf16[192,1024]{1,0:T(8,128)(2,1)}, bf16[1...) custom-call(s32[2]{0:T(128)} %pad_add_fusion.place_ref, ...), custom_call_target="tpu_custom_call" | custom-call | tf_op jit(solution)/shard_map/weights/pallas_call | solution.py:265
  23.0 1.0 collective-permute-start.7
  24.8 1.3 collective-permute-start.1
  26.1 2.3 %collective-permute-done.9 = f32[2,192]{1,0:T(2,128)S(1)} collective-permute-done((f32[2,192]{1,0:T(2,128)S(1)}, f32[2,192]{1,0:T(2,128)S(1)}, u32[]{:S(2)}, u32[]{:S(2)}) %collective-permute-start.9) | collective-permute-done | bytes 1568 | tf_op jit(solution)/shard_map/weights/ppermute | solution.py:285
  28.3 1.5 collective-permute-start.2
  29.9 2.5 %collective-permute-start.3 = (bf16[192,1024]{1,0:T(8,128)(2,1)}, bf16[192,1024]{1,0:T(8,128)(2,1)}, u32[]{:S(2)}, u32[]{:S(2)}) collective-permute-start(bf16[192,1024]{1,0:T(8,128)(2,1)} %get-tuple-element.24), channel_id=1, source_target_pairs={{0,6},{1,7},{2,0},{3,1},{4,2},{5,3},{6,4},{7,5},{8,14},{9,15},{10,... | collective-permute-start | bytes 1179656 | tf_op jit(solution)/shard_map/weights/ppermute | solution.py:280
  32.4 4.3 %collective-permute-done.1.refs_6_ = bf16[192,1024]{1,0:T(8,128)(2,1)} collective-permute-done((bf16[192,1024]{1,0:T(8,128)(2,1)}, bf16[192,1024]{1,0:T(8,128)(2,1)}, u32[]{:S(2)}, u32[]{:S(2)}) %collective-permute-start.1) | collective-permute-done | bytes 393248 | tf_op jit(solution)/shard_map/weights/ppermute | solution.py:280
  36.7 3.4 %collective-permute-start.4 = (bf16[192,1024]{1,0:T(8,128)(2,1)}, bf16[192,1024]{1,0:T(8,128)(2,1)S(1)}, u32[]{:S(2)}, u32[]{:S(2)}) collective-permute-start(bf16[192,1024]{1,0:T(8,128)(2,1)} %get-tuple-element.25), channel_id=1, source_target_pairs={{0,7},{1,6},{2,1},{3,0},{4,3},{5,2},{6,5},{7,4},{8,15},{9,14},{10,... | collective-permute-start | bytes 1179656 | tf_op jit(solution)/shard_map/weights/ppermute | solution.py:280
  40.1 5.8 %collective-permute-done.2.refs_7_ = bf16[192,1024]{1,0:T(8,128)(2,1)} collective-permute-done((bf16[192,1024]{1,0:T(8,128)(2,1)}, bf16[192,1024]{1,0:T(8,128)(2,1)}, u32[]{:S(2)}, u32[]{:S(2)}) %collective-permute-start.2) | collective-permute-done | bytes 393248 | tf_op jit(solution)/shard_map/weights/ppermute | solution.py:280
  45.9 1.6 collective-permute-start.5
  47.6 1.1 collective-permute-start.6
  48.7 0.7 pad_maximum_fusion.s_ref
  49.3 16.8 %collective-permute-done.4.refs_9_ = bf16[192,1024]{1,0:T(8,128)(2,1)S(1)} collective-permute-done((bf16[192,1024]{1,0:T(8,128)(2,1)}, bf16[192,1024]{1,0:T(8,128)(2,1)S(1)}, u32[]{:S(2)}, u32[]{:S(2)}) %collective-permute-start.4) | collective-permute-done | bytes 393248 | tf_op jit(solution)/shard_map/weights/ppermute | solution.py:280
  66.1 1.0 collective-permute-done.6.refs_11_
  67.1 0.7 copy-done.5
  67.9 3.4 %unpack.1 = (bf16[256,1024]{1,0:T(8,128)(2,1)}, bf16[384,1024]{1,0:T(8,128)(2,1)}, bf16[256,128]{1,0:T(8,128)(2,1)}) custom-call(bf16[256,2688]{1,0:T(8,128)(2,1)} %bitcast.5.in_ref, s32[1,128]{1,0:T(1,128)} %bitcast.32), custom_call_target="tpu_custom_call" | custom-call | tf_op jit(solution)/shard_map/unpack/pallas_call | solution.py:292
  71.3 3.1 %collective-permute-start.11 = (bf16[256,1024]{1,0:T(8,128)(2,1)}, bf16[256,1024]{1,0:T(8,128)(2,1)}, u32[]{:S(2)}, u32[]{:S(2)}) collective-permute-start(bf16[256,1024]{1,0:T(8,128)(2,1)} %get-tuple-element.31.own_ref), channel_id=1, source_target_pairs={{0,6},{2,0},{4,2},{6,4},{1,7},{3,1},{5,3},{7,5},{8,14},{10,8},{12,... | collective-permute-start | bytes 1572872 | tf_op jit(solution)/shard_map/rows/ppermute | solution.py:299
  74.3 11.7 %collective-permute-done.11.right_ref = bf16[256,1024]{1,0:T(8,128)(2,1)} collective-permute-done((bf16[256,1024]{1,0:T(8,128)(2,1)}, bf16[256,1024]{1,0:T(8,128)(2,1)}, u32[]{:S(2)}, u32[]{:S(2)}) %collective-permute-start.11) | collective-permute-done | bytes 524320 | tf_op jit(solution)/shard_map/rows/ppermute | solution.py:299
  86.0 3.0 %collective-permute-done.10.left_ref = bf16[256,1024]{1,0:T(8,128)(2,1)S(1)} collective-permute-done((bf16[256,1024]{1,0:T(8,128)(2,1)}, bf16[256,1024]{1,0:T(8,128)(2,1)S(1)}, u32[]{:S(2)}, u32[]{:S(2)}) %collective-permute-start.10) | collective-permute-done | bytes 524320 | tf_op jit(solution)/shard_map/rows/ppermute | solution.py:299
  89.8 0.6 collective-permute-start.12
  90.5 13.0 %collective-permute-done.12.far_ref = bf16[256,1024]{1,0:T(8,128)(2,1)} collective-permute-done((bf16[256,1024]{1,0:T(8,128)(2,1)S(1)}, bf16[256,1024]{1,0:T(8,128)(2,1)}, u32[]{:S(2)}, u32[]{:S(2)}) %collective-permute-start.12) | collective-permute-done | bytes 524320 | tf_op jit(solution)/shard_map/rows/ppermute | solution.py:299
  103.4 7.3 %up.2.refs_0_ = bf16[256,384]{1,0:T(8,128)(2,1)} custom-call(s32[2]{0:T(128)} %pad_add_fusion.place_ref, bf16[256,1024]{1,0:T(8,128)(2,1)} %get-tuple-element.31.own_ref, bf16[256,1024]{1,0:T(8,128)(2,1)} %copy-done.7, bf16[256,1024]{1,0:T(8,128)(2,1)} %collective-permute-done.11.right_ref, bf16[256,1024]{1,0:T(8,128)(2,1)} %collective-permute-done.12.far_ref, ...), custom_call_target="tpu_custom_call" | custom-call | tf_op jit(solution)/shard_map/up/pallas_call | solution.py:315
  110.7 1.5 collective-permute-start.14
  112.3 1.1 collective-permute-start.16
  113.4 1.6 collective-permute-start.18
  115.0 0.6 reshape.35.refs_12_
  115.6 1.4 collective-permute-done.15.refs_3_
  117.1 1.5 collective-permute-done.14.refs_2_
  118.5 3.5 %collective-permute-done.13.refs_1_ = bf16[256,384]{1,0:T(8,128)(2,1)S(1)} collective-permute-done((bf16[256,384]{1,0:T(8,128)(2,1)}, bf16[256,384]{1,0:T(8,128)(2,1)S(1)}, u32[]{:S(2)}, u32[]{:S(2)}) %collective-permute-start.13) | collective-permute-done | bytes 196640 | tf_op jit(solution)/shard_map/down/ppermute | solution.py:299
  122.1 0.7 copy-done.13
  122.7 4.8 %down.2 = bf16[256,1024]{1,0:T(8,128)(2,1)} custom-call(s32[2]{0:T(128)} %pad_add_fusion.place_ref, bf16[256,384]{1,0:T(8,128)(2,1)} %up.2.refs_0_, bf16[256,384]{1,0:T(8,128)(2,1)} %copy-done.13, bf16[256,384]{1,0:T(8,128)(2,1)} %copy-done.12, bf16[256,384]{1,0:T(8,128)(2,1)} %copy-done.11, bf16[192,1024]{1,0:T(8,128)(2,1)} %get-tuple-element.20.refs_4_, ...), custom_call_target="tpu_custom_call" | custom-call | tf_op jit(solution)/shard_map/down/pallas_call | solution.py:337
  127.6 9.4 %all-to-all-start.1 = ((bf16[32,8,1024]{2,1,0:T(8,128)(2,1)}), bf16[32,8,1024]{2,1,0:T(8,128)(2,1)S(1)}, u32[]{:S(2)}, u32[]{:S(2)}) async-start(bf16[32,8,1024]{2,1,0:T(8,128)(2,1)} %bitcast.24), calls=%async_computation.1 | async-start | bytes 1048576 | tf_op jit(solution)/shard_map/back/all_to_all | solution.py:258
  137.0 1.9 collective-permute-done.16.left_ref
  138.9 0.9 copy-done.6
  139.8 8.4 %up.3.refs_0_ = bf16[384,384]{1,0:T(8,128)(2,1)} custom-call(s32[2]{0:T(128)} %pad_add_fusion.place_ref, bf16[384,1024]{1,0:T(8,128)(2,1)} %get-tuple-element.33.own_ref, bf16[384,1024]{1,0:T(8,128)(2,1)} %copy-done.6, bf16[384,1024]{1,0:T(8,128)(2,1)} %collective-permute-done.17.right_ref, bf16[384,1024]{1,0:T(8,128)(2,1)} %collective-permute-done.18.far_ref, ...), custom_call_target="tpu_custom_call" | custom-call | tf_op jit(solution)/shard_map/up/pallas_call | solution.py:315
  148.6 1.0 collective-permute-start.20
  150.1 6.5 %collective-permute-done.21.refs_3_ = bf16[384,384]{1,0:T(8,128)(2,1)S(1)} collective-permute-done((bf16[384,384]{1,0:T(8,128)(2,1)}, bf16[384,384]{1,0:T(8,128)(2,1)S(1)}, u32[]{:S(2)}, u32[]{:S(2)}) %collective-permute-start.21) | collective-permute-done | bytes 294944 | tf_op jit(solution)/shard_map/down/ppermute | solution.py:299
  156.6 3.5 %collective-permute-done.20.refs_2_ = bf16[384,384]{1,0:T(8,128)(2,1)S(1)} collective-permute-done((bf16[384,384]{1,0:T(8,128)(2,1)}, bf16[384,384]{1,0:T(8,128)(2,1)S(1)}, u32[]{:S(2)}, u32[]{:S(2)}) %collective-permute-start.20) | collective-permute-done | bytes 294944 | tf_op jit(solution)/shard_map/down/ppermute | solution.py:299
  160.0 5.1 %collective-permute-done.19.refs_1_ = bf16[384,384]{1,0:T(8,128)(2,1)S(1)} collective-permute-done((bf16[384,384]{1,0:T(8,128)(2,1)}, bf16[384,384]{1,0:T(8,128)(2,1)S(1)}, u32[]{:S(2)}, u32[]{:S(2)}) %collective-permute-start.19) | collective-permute-done | bytes 294944 | tf_op jit(solution)/shard_map/down/ppermute | solution.py:299
  165.1 0.7 copy-done.10
  165.8 5.8 %down.3 = bf16[256,1664]{1,0:T(8,128)(2,1)} custom-call(s32[2]{0:T(128)} %pad_add_fusion.place_ref, bf16[384,384]{1,0:T(8,128)(2,1)} %up.3.refs_0_, bf16[384,384]{1,0:T(8,128)(2,1)} %copy-done.10, bf16[384,384]{1,0:T(8,128)(2,1)} %copy-done.9, bf16[384,384]{1,0:T(8,128)(2,1)} %copy-done.8, bf16[192,1024]{1,0:T(8,128)(2,1)} %get-tuple-element.20.refs_4_, ...), custom_call_target="tpu_custom_call" | custom-call | tf_op jit(solution)/shard_map/down/pallas_call | solution.py:337
  171.6 31.6 %all_to_all.15 = bf16[32,8,1664]{2,1,0:T(8,128)(2,1)} all-to-all(bf16[32,8,1664]{2,1,0:T(8,128)(2,1)} %bitcast.22), channel_id=1, replica_groups=mesh['z'=8,'x'=4,'y'=4,'core'=2] {'z','x'}, dimensions={0} | all-to-all | bytes 1703936 | tf_op jit(solution)/shard_map/back/all_to_all | solution.py:258
  203.3 3.1 %combine.1 = (f32[128,512]{1,0:T(8,128)}, f32[128,512]{1,0:T(8,128)}, bf16[128,128]{1,0:T(8,128)(2,1)}) custom-call(s32[2]{0:T(128)} %pad_add_fusion.place_ref, s32[8,128]{1,0:T(8,128)} %bitcast.26, f32[8,128]{1,0:T(8,128)} %bitcast.28, bf16[256,1024]{1,0:T(8,128)(2,1)} %bitcast.23, bf16[256,1664]{1,0:T(8,128)(2,1)} %bitcast.21), custom_call_target="tpu_custom_call" | custom-call | tf_op jit(solution)/shard_map/combine/pallas_call | solution.py:365
  206.4 3.1 %collective-permute-start.22 = (f32[128,512]{1,0:T(8,128)}, f32[128,512]{1,0:T(8,128)S(1)}, u32[]{:S(2)}, u32[]{:S(2)}) collective-permute-start(f32[128,512]{1,0:T(8,128)} %get-tuple-element.36), channel_id=1, source_target_pairs={{0,1},{1,0},{2,3},{3,2},{4,5},{5,4},{6,7},{7,6},{8,9},{9,8},{10,11... | collective-permute-start | bytes 786440 | tf_op jit(solution)/shard_map/combine/ppermute | solution.py:371
  209.5 1.4 collective-permute-done.22
  210.9 1.6 add_convert_fusion
  (52 shorter events, 3.2 us)
Async XLA Ops:
  4.6 63.3 %all-to-all-start = ((bf16[32,8,2688]{2,1,0:T(8,128)(2,1)}), bf16[32,8,2688]{2,1,0:T(8,128)(2,1)}, u32[]{:S(2)}, u32[]{:S(2)}) async-start(bf16[32,8,2688]{2,1,0:T(8,128)(2,1)} %bitcast.20), calls=%async_computation | async-start | bytes 2752512 | tf_op jit(solution)/shard_map/dispatch/all_to_all | solution.py:258
  16.6 7.9 %copy-start.15 = (f32[2,192]{1,0:T(2,128)S(1)}, f32[2,192]{1,0:T(2,128)}, u32[]{:S(2)}) copy-start(f32[2,192]{1,0:T(2,128)} %param.17) | copy-start | bytes 4612
  16.6 7.9 %copy-start.16 = (f32[2,192]{1,0:T(2,128)S(1)}, f32[2,192]{1,0:T(2,128)}, u32[]{:S(2)}) copy-start(f32[2,192]{1,0:T(2,128)} %param.18) | copy-start | bytes 4612
  23.0 44.1 %collective-permute-start.7 = (bf16[192,4096]{1,0:T(8,128)(2,1)}, bf16[192,4096]{1,0:T(8,128)(2,1)S(1)}, u32[]{:S(2)}, u32[]{:S(2)}) collective-permute-start(bf16[192,4096]{1,0:T(8,128)(2,1)} %get-tuple-element.28), channel_id=1, source_target_pairs={{0,1},{1,0},{2,3},{3,2},{4,5},{5,4},{6,7},{7,6},{8,9},{9,8},{10,11... | collective-permute-start | bytes 4718600 | tf_op jit(solution)/shard_map/weights/ppermute | solution.py:281
  24.0 43.8 %collective-permute-start.8 = (bf16[192,4096]{1,0:T(8,128)(2,1)}, bf16[192,4096]{1,0:T(8,128)(2,1)}, u32[]{:S(2)}, u32[]{:S(2)}) collective-permute-start(bf16[192,4096]{1,0:T(8,128)(2,1)} %get-tuple-element.29), channel_id=1, source_target_pairs={{0,1},{1,0},{2,3},{3,2},{4,5},{5,4},{6,7},{7,6},{8,9},{9,8},{10,11... | collective-permute-start | bytes 4718600 | tf_op jit(solution)/shard_map/weights/ppermute | solution.py:282
  24.1 5.7 %collective-permute-start = (bf16[192,1024]{1,0:T(8,128)(2,1)}, bf16[192,1024]{1,0:T(8,128)(2,1)S(1)}, u32[]{:S(2)}, u32[]{:S(2)}) collective-permute-start(bf16[192,1024]{1,0:T(8,128)(2,1)} %get-tuple-element.21), channel_id=1, source_target_pairs={{0,1},{1,0},{2,3},{3,2},{4,5},{5,4},{6,7},{7,6},{8,9},{9,8},{10,11... | collective-permute-start | bytes 1179656 | tf_op jit(solution)/shard_map/weights/ppermute | solution.py:280
  24.6 3.8 %collective-permute-start.9 = (f32[2,192]{1,0:T(2,128)S(1)}, f32[2,192]{1,0:T(2,128)S(1)}, u32[]{:S(2)}, u32[]{:S(2)}) collective-permute-start(f32[2,192]{1,0:T(2,128)S(1)} %bitcast.29), channel_id=1, source_target_pairs={{0,1},{1,0},{2,3},{3,2},{4,5},{5,4},{6,7},{7,6},{8,9},{9,8},{10,11... | collective-permute-start | bytes 4616 | tf_op jit(solution)/shard_map/weights/ppermute | solution.py:285
  24.8 11.9 %collective-permute-start.1 = (bf16[192,1024]{1,0:T(8,128)(2,1)}, bf16[192,1024]{1,0:T(8,128)(2,1)}, u32[]{:S(2)}, u32[]{:S(2)}) collective-permute-start(bf16[192,1024]{1,0:T(8,128)(2,1)} %get-tuple-element.22), channel_id=1, source_target_pairs={{0,2},{1,3},{2,4},{3,5},{4,6},{5,7},{6,0},{7,1},{8,10},{9,11},{10,... | collective-permute-start | bytes 1179656 | tf_op jit(solution)/shard_map/weights/ppermute | solution.py:280
  28.3 17.6 %collective-permute-start.2 = (bf16[192,1024]{1,0:T(8,128)(2,1)}, bf16[192,1024]{1,0:T(8,128)(2,1)}, u32[]{:S(2)}, u32[]{:S(2)}) collective-permute-start(bf16[192,1024]{1,0:T(8,128)(2,1)} %get-tuple-element.23), channel_id=1, source_target_pairs={{0,3},{1,2},{2,5},{3,4},{4,7},{5,6},{6,1},{7,0},{8,11},{9,10},{10,... | collective-permute-start | bytes 1179656 | tf_op jit(solution)/shard_map/weights/ppermute | solution.py:280
  29.9 80.8 %copy-start.2 = (bf16[192,1024]{1,0:T(8,128)(2,1)}, bf16[192,1024]{1,0:T(8,128)(2,1)S(1)}, u32[]{:S(2)}) copy-start(bf16[192,1024]{1,0:T(8,128)(2,1)S(1)} %collective-permute-done.refs_5_) | copy-start | bytes 1179652
  29.9 17.7 %collective-permute-start.3 = (bf16[192,1024]{1,0:T(8,128)(2,1)}, bf16[192,1024]{1,0:T(8,128)(2,1)}, u32[]{:S(2)}, u32[]{:S(2)}) collective-permute-start(bf16[192,1024]{1,0:T(8,128)(2,1)} %get-tuple-element.24), channel_id=1, source_target_pairs={{0,6},{1,7},{2,0},{3,1},{4,2},{5,3},{6,4},{7,5},{8,14},{9,15},{10,... | collective-permute-start | bytes 1179656 | tf_op jit(solution)/shard_map/weights/ppermute | solution.py:280
  36.7 29.4 %collective-permute-start.4 = (bf16[192,1024]{1,0:T(8,128)(2,1)}, bf16[192,1024]{1,0:T(8,128)(2,1)S(1)}, u32[]{:S(2)}, u32[]{:S(2)}) collective-permute-start(bf16[192,1024]{1,0:T(8,128)(2,1)} %get-tuple-element.25), channel_id=1, source_target_pairs={{0,7},{1,6},{2,1},{3,0},{4,3},{5,2},{6,5},{7,4},{8,15},{9,14},{10,... | collective-permute-start | bytes 1179656 | tf_op jit(solution)/shard_map/weights/ppermute | solution.py:280
  45.9 20.2 %collective-permute-start.5 = (bf16[192,1024]{1,0:T(8,128)(2,1)}, bf16[192,1024]{1,0:T(8,128)(2,1)S(1)}, u32[]{:S(2)}, u32[]{:S(2)}) collective-permute-start(bf16[192,1024]{1,0:T(8,128)(2,1)} %get-tuple-element.26), channel_id=1, source_target_pairs={{0,4},{1,5},{2,6},{3,7},{4,0},{5,1},{6,2},{7,3},{8,12},{9,13},{10,... | collective-permute-start | bytes 1179656 | tf_op jit(solution)/shard_map/weights/ppermute | solution.py:280
  47.6 19.6 %collective-permute-start.6 = (bf16[192,1024]{1,0:T(8,128)(2,1)}, bf16[192,1024]{1,0:T(8,128)(2,1)S(1)}, u32[]{:S(2)}, u32[]{:S(2)}) collective-permute-start(bf16[192,1024]{1,0:T(8,128)(2,1)} %get-tuple-element.27), channel_id=1, source_target_pairs={{0,5},{1,4},{2,7},{3,6},{4,1},{5,0},{6,3},{7,2},{8,13},{9,12},{10,... | collective-permute-start | bytes 1179656 | tf_op jit(solution)/shard_map/weights/ppermute | solution.py:280
  66.1 1.0 copy-start.3
  66.1 1.0 copy-start.4
  67.1 0.8 copy-start.5
  67.9 35.6 %copy-start = (bf16[192,4096]{1,0:T(8,128)(2,1)}, bf16[192,4096]{1,0:T(8,128)(2,1)S(1)}, u32[]{:S(2)}) copy-start(bf16[192,4096]{1,0:T(8,128)(2,1)S(1)} %collective-permute-done.7.wg2_ref) | copy-start | bytes 4718596
  71.3 14.7 %collective-permute-start.11 = (bf16[256,1024]{1,0:T(8,128)(2,1)}, bf16[256,1024]{1,0:T(8,128)(2,1)}, u32[]{:S(2)}, u32[]{:S(2)}) collective-permute-start(bf16[256,1024]{1,0:T(8,128)(2,1)} %get-tuple-element.31.own_ref), channel_id=1, source_target_pairs={{0,6},{2,0},{4,2},{6,4},{1,7},{3,1},{5,3},{7,5},{8,14},{10,8},{12,... | collective-permute-start | bytes 1572872 | tf_op jit(solution)/shard_map/rows/ppermute | solution.py:299
  74.3 14.7 %collective-permute-start.10 = (bf16[256,1024]{1,0:T(8,128)(2,1)}, bf16[256,1024]{1,0:T(8,128)(2,1)S(1)}, u32[]{:S(2)}, u32[]{:S(2)}) collective-permute-start(bf16[256,1024]{1,0:T(8,128)(2,1)} %get-tuple-element.31.own_ref), channel_id=1, source_target_pairs={{0,2},{2,4},{4,6},{6,0},{1,3},{3,5},{5,7},{7,1},{8,10},{10,12},{12... | collective-permute-start | bytes 1572872 | tf_op jit(solution)/shard_map/rows/ppermute | solution.py:299
  89.0 0.8 copy-start.7
  89.0 26.0 %copy-start.14 = (f32[2,4096]{1,0:T(2,128)S(1)}, f32[2,4096]{1,0:T(2,128)}, u32[]{:S(2)}) copy-start(f32[2,4096]{1,0:T(2,128)} %param.19) | copy-start | bytes 98308
  89.0 24.4 %collective-permute-start.17 = (bf16[384,1024]{1,0:T(8,128)(2,1)}, bf16[384,1024]{1,0:T(8,128)(2,1)}, u32[]{:S(2)}, u32[]{:S(2)}) collective-permute-start(bf16[384,1024]{1,0:T(8,128)(2,1)} %get-tuple-element.33.own_ref), channel_id=1, source_target_pairs={{0,6},{2,0},{4,2},{6,4},{1,7},{3,1},{5,3},{7,5},{8,14},{10,8},{12,... | collective-permute-start | bytes 2359304 | tf_op jit(solution)/shard_map/rows/ppermute | solution.py:299
  89.8 13.6 %collective-permute-start.12 = (bf16[256,1024]{1,0:T(8,128)(2,1)S(1)}, bf16[256,1024]{1,0:T(8,128)(2,1)}, u32[]{:S(2)}, u32[]{:S(2)}) collective-permute-start(bf16[256,1024]{1,0:T(8,128)(2,1)S(1)} %collective-permute-done.10.left_ref), channel_id=1, source_target_pairs={{0,2},{2,4},{4,6},{6,0},{1,3},{3,5},{5,7},{7,1},{8,10},{10,12},{12... | collective-permute-start | bytes 1572872 | tf_op jit(solution)/shard_map/rows/ppermute | solution.py:299
  110.7 6.3 %collective-permute-start.15 = (bf16[256,384]{1,0:T(8,128)(2,1)}, bf16[256,384]{1,0:T(8,128)(2,1)S(1)}, u32[]{:S(2)}, u32[]{:S(2)}) collective-permute-start(bf16[256,384]{1,0:T(8,128)(2,1)} %up.2.refs_0_), channel_id=1, source_target_pairs={{0,4},{2,6},{4,0},{6,2},{1,5},{3,7},{5,1},{7,3},{8,12},{10,14},{12... | collective-permute-start | bytes 589832 | tf_op jit(solution)/shard_map/down/ppermute | solution.py:299
  110.7 7.8 %collective-permute-start.14 = (bf16[256,384]{1,0:T(8,128)(2,1)}, bf16[256,384]{1,0:T(8,128)(2,1)S(1)}, u32[]{:S(2)}, u32[]{:S(2)}) collective-permute-start(bf16[256,384]{1,0:T(8,128)(2,1)} %up.2.refs_0_), channel_id=1, source_target_pairs={{0,6},{2,0},{4,2},{6,4},{1,7},{3,1},{5,3},{7,5},{8,14},{10,8},{12,... | collective-permute-start | bytes 589832 | tf_op jit(solution)/shard_map/down/ppermute | solution.py:299
  112.3 9.8 %collective-permute-start.13 = (bf16[256,384]{1,0:T(8,128)(2,1)}, bf16[256,384]{1,0:T(8,128)(2,1)S(1)}, u32[]{:S(2)}, u32[]{:S(2)}) collective-permute-start(bf16[256,384]{1,0:T(8,128)(2,1)} %up.2.refs_0_), channel_id=1, source_target_pairs={{0,2},{2,4},{4,6},{6,0},{1,3},{3,5},{5,7},{7,1},{8,10},{10,12},{12... | collective-permute-start | bytes 589832 | tf_op jit(solution)/shard_map/down/ppermute | solution.py:299
  112.3 26.6 %collective-permute-start.16 = (bf16[384,1024]{1,0:T(8,128)(2,1)}, bf16[384,1024]{1,0:T(8,128)(2,1)S(1)}, u32[]{:S(2)}, u32[]{:S(2)}) collective-permute-start(bf16[384,1024]{1,0:T(8,128)(2,1)} %get-tuple-element.33.own_ref), channel_id=1, source_target_pairs={{0,2},{2,4},{4,6},{6,0},{1,3},{3,5},{5,7},{7,1},{8,10},{10,12},{12... | collective-permute-start | bytes 2359304 | tf_op jit(solution)/shard_map/rows/ppermute | solution.py:299
  113.4 25.5 %collective-permute-start.18 = (bf16[384,1024]{1,0:T(8,128)(2,1)}, bf16[384,1024]{1,0:T(8,128)(2,1)}, u32[]{:S(2)}, u32[]{:S(2)}) collective-permute-start(bf16[384,1024]{1,0:T(8,128)(2,1)} %collective-permute-done.17.right_ref), channel_id=1, source_target_pairs={{0,6},{2,0},{4,2},{6,4},{1,7},{3,1},{5,3},{7,5},{8,14},{10,8},{12,... | collective-permute-start | bytes 2359304 | tf_op jit(solution)/shard_map/rows/ppermute | solution.py:299
  117.1 5.0 %copy-start.11 = (bf16[256,384]{1,0:T(8,128)(2,1)}, bf16[256,384]{1,0:T(8,128)(2,1)S(1)}, u32[]{:S(2)}) copy-start(bf16[256,384]{1,0:T(8,128)(2,1)S(1)} %collective-permute-done.15.refs_3_) | copy-start | bytes 589828
  118.5 3.5 %copy-start.12 = (bf16[256,384]{1,0:T(8,128)(2,1)}, bf16[256,384]{1,0:T(8,128)(2,1)S(1)}, u32[]{:S(2)}) copy-start(bf16[256,384]{1,0:T(8,128)(2,1)S(1)} %collective-permute-done.14.refs_2_) | copy-start | bytes 589828
  122.1 0.7 copy-start.13
  127.6 44.0 %all-to-all-start.1 = ((bf16[32,8,1024]{2,1,0:T(8,128)(2,1)}), bf16[32,8,1024]{2,1,0:T(8,128)(2,1)S(1)}, u32[]{:S(2)}, u32[]{:S(2)}) async-start(bf16[32,8,1024]{2,1,0:T(8,128)(2,1)} %bitcast.24), calls=%async_computation.1 | async-start | bytes 1048576 | tf_op jit(solution)/shard_map/back/all_to_all | solution.py:258
  138.9 0.9 copy-start.6
  148.2 8.3 %collective-permute-start.21 = (bf16[384,384]{1,0:T(8,128)(2,1)}, bf16[384,384]{1,0:T(8,128)(2,1)S(1)}, u32[]{:S(2)}, u32[]{:S(2)}) collective-permute-start(bf16[384,384]{1,0:T(8,128)(2,1)} %up.3.refs_0_), channel_id=1, source_target_pairs={{0,4},{2,6},{4,0},{6,2},{1,5},{3,7},{5,1},{7,3},{8,12},{10,14},{12... | collective-permute-start | bytes 884744 | tf_op jit(solution)/shard_map/down/ppermute | solution.py:299
  148.6 11.4 %collective-permute-start.20 = (bf16[384,384]{1,0:T(8,128)(2,1)}, bf16[384,384]{1,0:T(8,128)(2,1)S(1)}, u32[]{:S(2)}, u32[]{:S(2)}) collective-permute-start(bf16[384,384]{1,0:T(8,128)(2,1)} %up.3.refs_0_), channel_id=1, source_target_pairs={{0,6},{2,0},{4,2},{6,4},{1,7},{3,1},{5,3},{7,5},{8,14},{10,8},{12,... | collective-permute-start | bytes 884744 | tf_op jit(solution)/shard_map/down/ppermute | solution.py:299
  149.6 15.5 %collective-permute-start.19 = (bf16[384,384]{1,0:T(8,128)(2,1)}, bf16[384,384]{1,0:T(8,128)(2,1)S(1)}, u32[]{:S(2)}, u32[]{:S(2)}) collective-permute-start(bf16[384,384]{1,0:T(8,128)(2,1)} %up.3.refs_0_), channel_id=1, source_target_pairs={{0,2},{2,4},{4,6},{6,0},{1,3},{3,5},{5,7},{7,1},{8,10},{10,12},{12... | collective-permute-start | bytes 884744 | tf_op jit(solution)/shard_map/down/ppermute | solution.py:299
  156.6 8.5 %copy-start.8 = (bf16[384,384]{1,0:T(8,128)(2,1)}, bf16[384,384]{1,0:T(8,128)(2,1)S(1)}, u32[]{:S(2)}) copy-start(bf16[384,384]{1,0:T(8,128)(2,1)S(1)} %collective-permute-done.21.refs_3_) | copy-start | bytes 884740
  160.0 5.1 %copy-start.9 = (bf16[384,384]{1,0:T(8,128)(2,1)}, bf16[384,384]{1,0:T(8,128)(2,1)S(1)}, u32[]{:S(2)}) copy-start(bf16[384,384]{1,0:T(8,128)(2,1)S(1)} %collective-permute-done.20.refs_2_) | copy-start | bytes 884740
  165.1 0.7 copy-start.10
  171.6 31.7 %copy-start.1 = (bf16[32,8,1024]{2,1,0:T(8,128)(2,1)}, bf16[32,8,1024]{2,1,0:T(8,128)(2,1)S(1)}, u32[]{:S(2)}) copy-start(bf16[32,8,1024]{2,1,0:T(8,128)(2,1)S(1)} %all-to-all-done.1) | copy-start | bytes 1572868
  206.4 4.5 %collective-permute-start.22 = (f32[128,512]{1,0:T(8,128)}, f32[128,512]{1,0:T(8,128)S(1)}, u32[]{:S(2)}, u32[]{:S(2)}) collective-permute-start(f32[128,512]{1,0:T(8,128)} %get-tuple-element.36), channel_id=1, source_target_pairs={{0,1},{1,0},{2,3},{3,2},{4,5},{5,4},{6,7},{7,6},{8,9},{9,8},{10,11... | collective-permute-start | bytes 786440 | tf_op jit(solution)/shard_map/combine/ppermute | solution.py:371

commit v2 on v1

v2 whole, which is shorter than its diff:
```python
import functools

import jax
import jax.numpy as jnp
import numpy as np
from jax import lax
from jax.experimental import pallas as pl
from jax.experimental.pallas import tpu as pltpu
from jax.sharding import Mesh
from jax.sharding import PartitionSpec as P

BF = jnp.bfloat16
F32 = jnp.float32
PAGE = 32
ROWS = 8
DP = ("z", "x")
MOVES = ((0, False), (0, True), (1, False), (1, True), (3, False), (3, True), (2, False), (2, True))


def dot(a, b):
    return lax.dot_general(a, b, (((1,), (0,)), ((), ())), preferred_element_type=F32)


def dot_nt(a, b):
    return lax.dot_general(a, b, (((1,), (1,)), ((), ())), preferred_element_type=F32)


def dot_tn(a, b):
    return lax.dot_general(a, b, (((0,), (0,)), ((), ())), preferred_element_type=F32)


def iota(shape, dim):
    return lax.broadcasted_iota(jnp.int32, shape, dim)


def ones(cond, dtype=BF):
    return jnp.where(cond, 1.0, 0.0).astype(dtype)


def slot_codes(ids_t, parity, n_dst, none):
    picks, tok = ids_t.shape
    expert = 2 * iota((n_dst, tok), 0) + parity
    named = jnp.zeros((n_dst, tok), F32)
    for k in range(picks):
        named = named + ones(ids_t[k : k + 1, :] == expert, F32)
    earlier = ones(iota((tok, tok), 0) < iota((tok, tok), 1))
    place = dot(named.astype(BF), earlier)
    code = jnp.where(named > 0, place, none)
    spread = ones((iota((n_dst * ROWS, n_dst), 0) // ROWS) == iota((n_dst * ROWS, n_dst), 1))
    return dot(spread, code.astype(BF)), spread


def selections(code):
    row = iota(code.shape, 0) % ROWS
    slot = row.astype(F32)
    low = row < 4
    return (
        code == slot,
        code == slot + 8.0,
        (code == slot + 16.0) & low,
        (code == slot + 12.0) & jnp.logical_not(low),
    )


def route_kernel(n_dst, place_ref, ids_ref, tok_hbm, kv_ref, wg_hbm, wu_hbm, wd_hbm, out_ref, g_ref, u_ref, *refs):
    cuts, (tok_ref, sems) = refs[:-2], refs[-2:]
    quarter = tok_ref.shape[1]
    half = quarter // 2
    y, core = place_ref[0], place_ref[1]
    cols = pl.ds(pl.multiple_of(y * quarter, quarter), quarter)
    copies = [(tok_hbm.at[:, cols], tok_ref)]
    for (by, other), cut in zip(MOVES, cuts):
        cols = pl.ds(pl.multiple_of(lax.rem(y + by, 4) * quarter, quarter), quarter)
        copies.append((wd_hbm.at[1 - core if other else core, :, cols], cut))
    sibling = pl.ds(1 - core, 1)
    copies += [(wg_hbm.at[sibling], g_ref), (wu_hbm.at[sibling], u_ref)]
    copies = [pltpu.make_async_copy(a, b, sems.at[i]) for i, (a, b) in enumerate(copies)]
    for c in copies:
        c.start()
    code, _ = slot_codes(ids_ref[...], place_ref[1], n_dst, 200.0)
    first, second, low, high = selections(code)
    n, t = code.shape
    row, col = iota((n, t), 0), iota((n, t), 1)
    piece = (col == (row % ROWS) * PAGE + row // ROWS) & (row % ROWS < t // PAGE)
    out_ref[:, 2 * quarter + half :] = dot(ones(piece), kv_ref[...]).astype(BF)
    copies[0].wait()
    tok = tok_ref[...]
    out_ref[:, :quarter] = dot(ones(first), tok).astype(BF)
    out_ref[:, quarter : 2 * quarter] = dot(ones(second), tok).astype(BF)
    out_ref[:, 2 * quarter : 2 * quarter + half] = (
        dot(ones(low), tok[:, :half]) + dot(ones(high), tok[:, half:])
    ).astype(BF)
    for c in copies[1:]:
        c.wait()


def unpack_kernel(in_ref, slots_ref, p_ref, q_ref, kv_ref):
    n = in_ref.shape[0]
    quarter = q_ref.shape[1]
    half = quarter // 2
    p_ref[...] = in_ref[:, :quarter]
    q_ref[:n] = in_ref[:, quarter : 2 * quarter]
    m = n // 2
    row, col = iota((m, n), 0), iota((m, n), 1)
    at = (row // 4) * ROWS + row % 4
    mixed = in_ref[:, 2 * quarter : 2 * quarter + half]
    q_ref[n:, :half] = dot(ones(col == at), mixed).astype(BF)
    q_ref[n:, half:] = dot(ones(col == at + 4), mixed).astype(BF)
    pages = slots_ref.shape[1]
    row, col = iota((pages, n), 0), iota((pages, n), 1)
    held = col % ROWS < 4
    spread = ones(held & (row == (col // ROWS) * 4 + col % ROWS))
    slots = jnp.broadcast_to(slots_ref[...].astype(F32), (8, pages)).astype(BF)
    slots = jnp.where(held[0:1], dot(slots, spread)[0:1], -2.0)
    row = iota((n, n), 0)
    wanted = jnp.where(row % ROWS < 4, (row // ROWS) * 4 + row % ROWS, -1).astype(F32)
    kv_ref[...] = dot(ones(slots == wanted), in_ref[:, 2 * quarter + half :]).astype(BF)


def gated(both, s_ref):
    n = s_ref.shape[1]
    g, u = both[:, :n] * s_ref[0:1, :], both[:, n:] * s_ref[1:2, :]
    return (g / (1.0 + jnp.exp(-g)) * u).astype(BF)


def up_step(acc_ref, x_ref, w_refs, first):
    w = jnp.concatenate([ref[0] for ref in w_refs], axis=0)
    both = dot_nt(x_ref[...], w)
    if first:
        acc_ref[...] = both
    else:
        acc_ref[...] += both


def up_kernel(place_ref, *refs):
    w_refs, s_ref, out_ref, acc_ref = refs[4:8], refs[8], refs[9], refs[10]
    k = pl.program_id(0)
    for i in range(4):
        pl.when(k == i)(functools.partial(up_step, acc_ref, refs[i], w_refs, i == 0))

    @pl.when(k == 3)
    def _():
        out_ref[...] = gated(acc_ref[...], s_ref)


def up_first_kernel(place_ref, *refs):
    k = pl.program_id(0)
    for i in range(2):
        pl.when(k == i)(functools.partial(up_step, refs[6], refs[i], refs[2:6], i == 0))


def up_last_kernel(place_ref, *refs):
    w_refs, part_ref, s_ref, out_ref, acc_ref = refs[2:6], refs[6], refs[7], refs[8], refs[9]
    k = pl.program_id(0)
    for i in range(2):
        pl.when(k == i)(functools.partial(up_step, acc_ref, refs[i], w_refs, i == 0))

    @pl.when(k == 1)
    def _():
        out_ref[...] = gated(acc_ref[...] + part_ref[...], s_ref)


def down_sum(h_refs, w_refs):
    acc = None
    for i, h_ref in enumerate(h_refs):
        w = jnp.concatenate([w_refs[2 * i][...], w_refs[2 * i + 1][...]], axis=0)
        part = dot(h_ref[...], w)
        acc = part if acc is None else acc + part
    return acc


def down_kernel(place_ref, *refs):
    refs[13][...] = (down_sum(refs[:4], refs[4:12]) * refs[12][0]).astype(BF)


def down_first_kernel(h_ref, same_ref, cross_ref, out_ref):
    out_ref[...] = down_sum((h_ref,), (same_ref, cross_ref))


def down_last_kernel(place_ref, *refs):
    acc_ref, s_ref, kv_ref, out_ref = refs[9:]
    y = ((acc_ref[...] + down_sum(refs[:3], refs[3:9])) * s_ref[0]).astype(BF)
    n, quarter = kv_ref.shape[0], y.shape[1]
    half = quarter // 2
    out_ref[:, :quarter] = y[:n]
    rest = y[n:]
    m = n // 2
    row, col = iota((n, m), 0), iota((n, m), 1)
    hit = col == (row // ROWS) * 4 + row % 4
    low = row % ROWS < 4
    out_ref[:, quarter : quarter + half] = (
        dot(ones(hit & low), rest[:, :half]) + dot(ones(hit & jnp.logical_not(low)), rest[:, half:])
    ).astype(BF)
    out_ref[:, quarter + half :] = kv_ref[...]


def combine_kernel(n_dst, place_ref, ids_ref, gates_ref, p_ref, q_ref, keep_ref, send_ref, kv_ref):
    parity = place_ref[1]
    ids, gates = ids_ref[...], gates_ref[...]
    code, spread = slot_codes(ids, parity, n_dst, 200.0)
    picks, tok = ids.shape
    expert = 2 * iota((n_dst, tok), 0) + parity
    gate = jnp.zeros((n_dst, tok), F32)
    for k in range(picks):
        gate = gate + jnp.where(ids[k : k + 1, :] == expert, gates[k : k + 1, :], 0.0)
    top = gate.astype(BF)
    rest = (gate - top.astype(F32)).astype(BF)
    top, rest = dot(spread, top), dot(spread, rest)
    first, second, low, high = selections(code)

    def mix(where, rows):
        return dot_tn(jnp.where(where, top, 0.0).astype(BF), rows) + dot_tn(
            jnp.where(where, rest, 0.0).astype(BF), rows
        )

    quarter = p_ref.shape[1]
    half = quarter // 2
    mixed = q_ref[:, quarter : quarter + half]
    sums = []
    for where, lo in ((low, 0), (high, half)):
        cols = slice(lo, lo + half)
        sums.append(mix(first, p_ref[:, cols]) + mix(second, q_ref[:, cols]) + mix(where, mixed))
    even = parity == 0
    keep_ref[...] = jnp.where(even, sums[0], sums[1])
    send_ref[...] = jnp.where(even, sums[1], sums[0])
    n = q_ref.shape[0]
    row, col = iota((tok, n), 0), iota((tok, n), 1)
    kv_ref[...] = dot(ones(col == (row % PAGE) * ROWS + row // PAGE), q_ref[:, quarter + half :]).astype(BF)


def sds(*shape, dtype=BF):
    return jax.ShapeDtypeStruct(shape, dtype)


def whole(*shape):
    return pl.BlockSpec(shape, lambda *a: (0,) * len(shape))


CHEAP = pl.CostEstimate(flops=1000, bytes_accessed=1000, transcendentals=0)
PARAMS = pltpu.CompilerParams(vmem_limit_bytes=62 * 1024 * 1024)


def on_device(
    tokens, expert_ids, gates, w_gate, w_up, w_down, gate_scale, up_scale, down_scale, kv_rows, page_slots
):
    y, core = lax.axis_index("y"), lax.axis_index("core")
    n_dp = lax.axis_size("z") * lax.axis_size("x")
    n_y, n_core = lax.axis_size("y"), lax.axis_size("core")
    tok, width = tokens.shape
    quarter = width // n_y
    half = quarter // 2
    experts, hid = w_gate.shape[:2]
    kv_cols = kv_rows.shape[1]
    rows = n_dp * ROWS
    place = jnp.stack([y, core]).astype(jnp.int32)
    ids_t, gates_t = expert_ids.T, gates.T
    picks = ids_t.shape[0]

    payload = quarter + half + kv_cols
    hbm = pl.BlockSpec(memory_space=pltpu.HBM)
    vmem = pl.BlockSpec(memory_space=pltpu.VMEM)
    smem = pl.BlockSpec(memory_space=pltpu.SMEM)
    swap = [(0, 1), (1, 0)]

    def after(v, *others):
        return lax.optimization_barrier((v, *others))[0]

    with jax.named_scope("route"):
        outgoing, other_g, other_u, *cuts = pl.pallas_call(
            functools.partial(route_kernel, n_dp),
            in_specs=[smem, vmem, hbm, vmem, hbm, hbm, hbm],
            out_specs=[vmem] * 11,
            out_shape=[sds(rows, quarter + payload)] + [sds(1, hid, width)] * 2 + [sds(hid, quarter)] * 8,
            scratch_shapes=[pltpu.VMEM((tok, quarter), BF), pltpu.SemaphoreType.DMA((11,))],
            compiler_params=PARAMS,
            cost_estimate=CHEAP,
        )(place, ids_t, tokens, kv_rows, w_gate, w_up, w_down)
        wd = [cuts[0]]
        for (by, other), v in zip(MOVES[1:], cuts[1:]):
            pairs = [
                (i * n_core + c, (i + by) % n_y * n_core + (1 - c if other else c))
                for i in range(n_y)
                for c in range(n_core)
            ]
            wd.append(lax.ppermute(v, ("y", "core"), pairs))

    def exchange(v):
        return lax.all_to_all(v.reshape(n_dp, ROWS, v.shape[-1]), DP, 0, 0, tiled=True).reshape(v.shape)

    with jax.named_scope("dispatch"):
        arrived = exchange(outgoing)

    with jax.named_scope("scales"):
        both = jnp.stack([gate_scale, up_scale])
        own = lax.dynamic_index_in_dim(both, core, 1, keepdims=False)
        other = lax.ppermute(lax.dynamic_index_in_dim(both, 1 - core, 1, keepdims=False), "core", swap)
        scales = jnp.concatenate([own, other], axis=1)

    with jax.named_scope("unpack"):
        x_p, x_q, kv_q = pl.pallas_call(
            unpack_kernel,
            out_shape=[sds(rows, quarter), sds(rows + rows // 2, quarter), sds(rows, kv_cols)],
            compiler_params=PARAMS,
            cost_estimate=CHEAP,
        )(after(arrived, *wd, scales), page_slots.reshape(1, -1))

    def shift(v, by):
        return lax.ppermute(v, "y", [(i, (i + by) % n_y) for i in range(n_y)])

    with jax.named_scope("rows"):
        p_left, p_right = shift(x_p, 1), shift(x_p, -1)
        p_far = shift(p_left, 1)
        q_right = shift(after(x_q, p_right), -1)
        q_left = shift(after(x_q, p_far), 1)
        q_far = shift(q_right, -1)

    with jax.named_scope("swap"):
        w2 = [lax.ppermute(w, "core", swap) for w in (other_g, other_u)]

    units = n_core * hid

    def columns(k, p, steps):
        by = steps[0]
        for i, s in enumerate(steps[1:], 1):
            by = jnp.where(k == i, s, by)
        return lax.rem(p[0] + by, n_y)

    def weight_specs(*steps):
        def own():
            return pl.BlockSpec((1, hid, quarter), lambda k, p: (p[1], 0, columns(k, p, steps)))

        def other():
            return pl.BlockSpec((1, hid, quarter), lambda k, p: (0, 0, columns(k, p, steps)))

        return [own(), other(), own(), other()]

    def call(kernel, steps, in_specs, out_specs, out_shape, scratch=()):
        return pl.pallas_call(
            kernel,
            grid_spec=pltpu.PrefetchScalarGridSpec(
                num_scalar_prefetch=1,
                grid=(steps,),
                in_specs=in_specs,
                out_specs=out_specs,
                scratch_shapes=list(scratch),
            ),
            out_shape=out_shape,
            compiler_params=PARAMS,
            cost_estimate=CHEAP,
        )

    weights = (w_gate, w2[0], w_up, w2[1])
    channel = pl.BlockSpec((1, 1, quarter), lambda k, p: (p[1], 0, p[0]))
    down_scale = down_scale.reshape(experts, 1, width)

    def acc(r):
        return [pltpu.VMEM((r, 2 * units), F32)]

    with jax.named_scope("up"):
        r = rows
        h_p = call(
            up_kernel,
            4,
            [whole(r, quarter)] * 4 + weight_specs(0, 3, 1, 2) + [whole(2, units)],
            whole(r, units),
            sds(r, units),
            acc(r),
        )(place, x_p, p_left, p_right, p_far, *weights, scales)

    with jax.named_scope("up"):
        r = rows + rows // 2
        both_q = call(
            up_first_kernel,
            2,
            [whole(r, quarter)] * 2 + weight_specs(0, 1),
            whole(r, 2 * units),
            sds(r, 2 * units, dtype=F32),
        )(place, x_q, q_right, *weights)
    with jax.named_scope("down"):
        near = [shift(h_p, 1), shift(h_p, -1), shift(h_p, 2)]
        near[2] = after(near[2], both_q)
        r = rows
        v_p = call(
            down_kernel,
            1,
            [whole(r, units)] * 4 + [whole(hid, quarter)] * 8 + [channel],
            whole(r, quarter),
            sds(r, quarter),
        )(place, h_p, *near, *wd, down_scale)
        back_p = exchange(v_p)

    with jax.named_scope("up"):
        r = rows + rows // 2
        h_q = call(
            up_last_kernel,
            2,
            [whole(r, quarter)] * 2 + weight_specs(3, 2) + [whole(r, 2 * units), whole(2, units)],
            whole(r, units),
            sds(r, units),
            acc(r),
        )(place, q_left, q_far, *weights, both_q, scales)

    with jax.named_scope("down"):
        near = [shift(h_q, 1), shift(h_q, -1), shift(h_q, 2)]
        part = pl.pallas_call(
            down_first_kernel,
            out_shape=sds(r, quarter, dtype=F32),
            compiler_params=PARAMS,
            cost_estimate=CHEAP,
        )(h_q, *wd[:2])
        v_q = call(
            down_last_kernel,
            1,
            [whole(r, units)] * 3
            + [whole(hid, quarter)] * 6
            + [whole(r, quarter), channel, whole(rows, kv_cols)],
            whole(rows, payload),
            sds(rows, payload),
        )(place, *near, *wd[2:], part, down_scale, kv_q)
        back_q = exchange(v_q)

    with jax.named_scope("combine"):
        keep, send, kv_cache = pl.pallas_call(
            functools.partial(combine_kernel, n_dp),
            in_specs=[pl.BlockSpec(memory_space=pltpu.SMEM)] + [pl.BlockSpec(memory_space=pltpu.VMEM)] * 4,
            out_shape=[sds(tok, half, dtype=F32), sds(tok, half, dtype=F32), sds(tok, kv_cols)],
            compiler_params=PARAMS,
            cost_estimate=CHEAP,
        )(place, ids_t, gates_t, back_p, back_q)
        moe_out = (keep + lax.ppermute(send, "core", [(0, 1), (1, 0)])).astype(BF)
    return moe_out, kv_cache.reshape(tok // PAGE, PAGE, kv_cols)


def solution(mesh):
    shape = mesh.devices.shape
    n_z, n_x, n_y = 8, 4, 4
    fine = Mesh(np.asarray(mesh.devices).reshape(n_z, n_x, n_y, shape[1] // n_y), ("z", "x", "y", "core"))
    group = ("y", "core")
    placed = (
        P(DP, None),
        P(DP, None),
        P(DP, None),
        P(DP, group, None),
        P(DP, group, None),
        P(DP, group, None),
        P(DP, group),
        P(DP, group),
        P(DP, None),
        P(DP, group),
        P(),
    )
    return jax.shard_map(
        on_device,
        mesh=fine,
        in_specs=placed,
        out_specs=(P(DP, group), P(DP, None, group)),
        check_vma=False,
    )
```

time: 213 us -> 199 us (0.934)
  waiting for transfers between devices: 82.6 us -> 62.8 us
  starting transfers between devices: 48 us -> 53.8 us
  blocking collectives: 31.6 us -> 28.5 us
    ppermute x12, waiting for transfers between devices: 51 us -> 34.3 us  [shift(): return lax.ppermute(v, 'y', [(i, (i + by) % n_y) for i in range(n_y)])]
    ppermute x12, starting transfers between devices: 10.3 us -> 14.6 us  [shift(): return lax.ppermute(v, 'y', [(i, (i + by) % n_y) for i in range(n_y)])]
    pallas_call x1, Pallas kernels: 3.38 us -> 7.11 us  [on_device(): pl.pallas_call(functools.partial(route_kernel, n_dp), in_specs=[smem, vme...]
    ppermute x1, starting transfers between devices: 3.09 us -> 6.41 us  [on_device(): moe_out = (keep + lax.ppermute(send, 'core', [(0, 1), (1, 0)])).astype(BF)]
    all_to_all x1, blocking collectives: 31.6 us -> 28.5 us  [exchange(): lax.all_to_all(v.reshape(n_dp, ROWS, v.shape[-1]), DP, 0, 0, tiled=True)]
    pallas_call x5 -> x6, Pallas kernels: 32.7 us -> 31.3 us  [the longest x1 6.98 us: on_device(): call(up_kernel, 4, [whole(r, quarter)] * 4 + weight_specs(0, 3, 1, 2) + [...]
    unnamed x36 -> x44, local copies, waits for them, and re-layouts: 3.39 us -> 4.51 us
  transfers between devices with their start and end apart: 25 -> 25, of which waited for: 16 -> 13; matrix products, arithmetic and copies ran while one was open for 1% -> 1% of each run, Pallas kernels for 15% -> 17%
where the time goes in v2:
time: 199 us; the launch traced here: 198 us
  waiting for transfers between devices  62.8 us (32%)
  starting transfers between devices  53.8 us (27%)
  Pallas kernels  44.4 us (22%)
  blocking collectives  28.5 us (14%)
  local copies, waits for them, and re-layouts  5.15 us (3%)
  other arithmetic  2.93 us (1%)
    ppermute x12, waiting for transfers between devices, shift(): return lax.ppermute(v, 'y', [(i, (i + by) % n_y) for i in range(n_y)])  34.3 us
    all_to_all x1, blocking collectives, exchange(): lax.all_to_all(v.reshape(n_dp, ROWS, v.shape[-1]), DP, 0, 0, tiled=True)  28.5 us
    ppermute x7, waiting for transfers between devices, on_device(): wd.append(lax.ppermute(v, ('y', 'core'), pairs))  26.3 us
    all_to_all x2, starting transfers between devices, exchange(): lax.all_to_all(v.reshape(n_dp, ROWS, v.shape[-1]), DP, 0, 0, tiled=True)  21.6 us
    ppermute x12, starting transfers between devices, shift(): return lax.ppermute(v, 'y', [(i, (i + by) % n_y) for i in range(n_y)])  14.6 us
    ppermute x7, starting transfers between devices, on_device(): wd.append(lax.ppermute(v, ('y', 'core'), pairs))  10.1 us
    pallas_call x1, Pallas kernels, on_device(): pl.pallas_call(functools.partial(route_kernel, n_dp), in_specs=[smem, vme...  7.11 us
    pallas_call x1, Pallas kernels, on_device(): call(up_kernel, 4, [whole(r, quarter)] * 4 + weight_specs(0, 3, 1, 2) + [...  6.98 us
  transfers between devices with their start and end apart: 25, of which 13 were waited for; matrix products, arithmetic and copies ran while one was open for 1% of the time, Pallas kernels for 17%

profile of v2, /device:TPU:1, one launch (start us, length us, event | category | flops | bytes accessed | tf_op | source)
XLA Modules:
  0.0 198.4 jit_solution(2667259961458046766)
XLA Ops:
  0.6 0.6 pad_add_fusion.place_ref
  1.2 7.1 %route.1 = (bf16[256,2688]{1,0:T(8,128)(2,1)}, bf16[1,192,4096]{2,1,0:T(8,128)(2,1)}, bf16[1,192,4096]{2,1,0:T(8,128)(2,1)}, bf16[192,1024]{1,0:T(8,128)(2,1)}, ...) custom-call(s32[2]{0:T(128)} %pad_add_fusion.place_ref, ...), custom_call_target="tpu_custom_call" | custom-call | flops 1000 | bytes 1000 | tf_op jit(solution)/shard_map/route/pallas_call | solution.py:269
  8.4 12.1 %all-to-all-start = ((bf16[32,8,2688]{2,1,0:T(8,128)(2,1)}), bf16[32,8,2688]{2,1,0:T(8,128)(2,1)}, u32[]{:S(2)}, u32[]{:S(2)}) async-start(bf16[32,8,2688]{2,1,0:T(8,128)(2,1)} %bitcast.24), calls=%async_computation | async-start | bytes 2752512 | tf_op jit(solution)/shard_map/dispatch/all_to_all | solution.py:288
  20.6 1.0 collective-permute-start
  21.6 1.3 collective-permute-start.1
  22.9 1.5 collective-permute-start.2
  24.5 1.4 collective-permute-start.3
  25.9 0.5 collective-permute-start.7
  26.4 0.8 collective-permute-done.7
  27.7 1.6 collective-permute-start.5
  29.3 4.4 %collective-permute-done.1.refs_6_.refs_3_ = bf16[192,1024]{1,0:T(8,128)(2,1)S(1)} collective-permute-done((bf16[192,1024]{1,0:T(8,128)(2,1)S(1)}, bf16[192,1024]{1,0:T(8,128)(2,1)S(1)}, u32[]{:S(2)}, u32[]{:S(2)}) %collective-permute-start.1) | collective-permute-done | bytes 393248 | tf_op jit(solution)/shard_map/route/ppermute | solution.py:285
  33.7 2.7 %collective-permute-start.6 = (bf16[192,1024]{1,0:T(8,128)(2,1)S(1)}, bf16[192,1024]{1,0:T(8,128)(2,1)}, u32[]{:S(2)}, u32[]{:S(2)}) collective-permute-start(bf16[192,1024]{1,0:T(8,128)(2,1)S(1)} %copy-done.17), channel_id=1, source_target_pairs={{0,5},{1,4},{2,7},{3,6},{4,1},{5,0},{6,3},{7,2},{8,13},{9,12},{10,... | collective-permute-start | bytes 1179656 | tf_op jit(solution)/shard_map/route/ppermute | solution.py:285
  36.4 6.1 %collective-permute-done.2.refs_7_.refs_4_ = bf16[192,1024]{1,0:T(8,128)(2,1)S(1)} collective-permute-done((bf16[192,1024]{1,0:T(8,128)(2,1)S(1)}, bf16[192,1024]{1,0:T(8,128)(2,1)S(1)}, u32[]{:S(2)}, u32[]{:S(2)}) %collective-permute-start.2) | collective-permute-done | bytes 393248 | tf_op jit(solution)/shard_map/route/ppermute | solution.py:285
  42.6 0.8 copy-done.3
  43.3 0.5 collective-permute-start.12
  43.8 0.7 pad_maximum_fusion.refs_8_.refs_7_
  44.9 6.8 %collective-permute-done.5.refs_10_.refs_7_ = bf16[192,1024]{1,0:T(8,128)(2,1)} collective-permute-done((bf16[192,1024]{1,0:T(8,128)(2,1)}, bf16[192,1024]{1,0:T(8,128)(2,1)}, u32[]{:S(2)}, u32[]{:S(2)}) %collective-permute-start.5) | collective-permute-done | bytes 393248 | tf_op jit(solution)/shard_map/route/ppermute | solution.py:285
  51.7 8.6 %collective-permute-done.6.refs_11_.refs_8_ = bf16[192,1024]{1,0:T(8,128)(2,1)} collective-permute-done((bf16[192,1024]{1,0:T(8,128)(2,1)S(1)}, bf16[192,1024]{1,0:T(8,128)(2,1)}, u32[]{:S(2)}, u32[]{:S(2)}) %collective-permute-start.6) | collective-permute-done | bytes 393248 | tf_op jit(solution)/shard_map/route/ppermute | solution.py:285
  60.3 2.9 %unpack.1 = (bf16[256,1024]{1,0:T(8,128)(2,1)}, bf16[384,1024]{1,0:T(8,128)(2,1)}, bf16[256,128]{1,0:T(8,128)(2,1)}) custom-call(bf16[256,2688]{1,0:T(8,128)(2,1)} %bitcast.5.in_ref, s32[1,128]{1,0:T(1,128)} %bitcast.32), custom_call_target="tpu_custom_call" | custom-call | flops 1000 | bytes 1000 | tf_op jit(solution)/shard_map/unpack/pallas_call | solution.py:300
  63.2 3.2 %collective-permute-start.9 = (bf16[256,1024]{1,0:T(8,128)(2,1)}, bf16[256,1024]{1,0:T(8,128)(2,1)S(1)}, u32[]{:S(2)}, u32[]{:S(2)}) collective-permute-start(bf16[256,1024]{1,0:T(8,128)(2,1)} %get-tuple-element.33.refs_0_), channel_id=1, source_target_pairs={{0,6},{2,0},{4,2},{6,4},{1,7},{3,1},{5,3},{7,5},{8,14},{10,8},{12,... | collective-permute-start | bytes 1572872 | tf_op jit(solution)/shard_map/rows/ppermute | solution.py:308
  66.4 11.7 %collective-permute-done.9.refs_2_ = bf16[256,1024]{1,0:T(8,128)(2,1)S(1)} collective-permute-done((bf16[256,1024]{1,0:T(8,128)(2,1)}, bf16[256,1024]{1,0:T(8,128)(2,1)S(1)}, u32[]{:S(2)}, u32[]{:S(2)}) %collective-permute-start.9) | collective-permute-done | bytes 524320 | tf_op jit(solution)/shard_map/rows/ppermute | solution.py:308
  78.0 3.3 %collective-permute-start.16 = (bf16[384,1024]{1,0:T(8,128)(2,1)}, bf16[384,1024]{1,0:T(8,128)(2,1)}, u32[]{:S(2)}, u32[]{:S(2)}) collective-permute-start(bf16[384,1024]{1,0:T(8,128)(2,1)} %get-tuple-element.39.refs_0_), channel_id=1, source_target_pairs={{0,6},{2,0},{4,2},{6,4},{1,7},{3,1},{5,3},{7,5},{8,14},{10,8},{12,... | collective-permute-start | bytes 2359304 | tf_op jit(solution)/shard_map/rows/ppermute | solution.py:308
  81.4 0.7 copy-done.7
  82.1 12.9 %collective-permute-done.10.refs_3_ = bf16[256,1024]{1,0:T(8,128)(2,1)} collective-permute-done((bf16[256,1024]{1,0:T(8,128)(2,1)S(1)}, bf16[256,1024]{1,0:T(8,128)(2,1)}, u32[]{:S(2)}, u32[]{:S(2)}) %collective-permute-start.10) | collective-permute-done | bytes 524320 | tf_op jit(solution)/shard_map/rows/ppermute | solution.py:308
  95.0 7.0 %up.3.refs_0_ = bf16[256,384]{1,0:T(8,128)(2,1)} custom-call(s32[2]{0:T(128)} %pad_add_fusion.place_ref, bf16[256,1024]{1,0:T(8,128)(2,1)} %get-tuple-element.33.refs_0_, bf16[256,1024]{1,0:T(8,128)(2,1)} %copy-done.7, bf16[256,1024]{1,0:T(8,128)(2,1)} %copy-done.6, bf16[256,1024]{1,0:T(8,128)(2,1)} %collective-permute-done.10.refs_3_, ...), custom_call_target="tpu_custom_call" | custom-call | flops 1000 | bytes 1000 | tf_op jit(solution)/shard_map/up/pallas_call | solution.py:361
  102.1 2.7 %collective-permute-start.14 = (bf16[256,384]{1,0:T(8,128)(2,1)}, bf16[256,384]{1,0:T(8,128)(2,1)S(1)}, u32[]{:S(2)}, u32[]{:S(2)}) collective-permute-start(bf16[256,384]{1,0:T(8,128)(2,1)} %up.3.refs_0_), channel_id=1, source_target_pairs={{0,6},{2,0},{4,2},{6,4},{1,7},{3,1},{5,3},{7,5},{8,14},{10,8},{12,... | collective-permute-start | bytes 589832 | tf_op jit(solution)/shard_map/down/ppermute | solution.py:308
  104.8 2.7 %collective-permute-start.18 = (bf16[384,1024]{1,0:T(8,128)(2,1)}, bf16[384,1024]{1,0:T(8,128)(2,1)}, u32[]{:S(2)}, u32[]{:S(2)}) collective-permute-start(bf16[384,1024]{1,0:T(8,128)(2,1)} %collective-permute-done.16.refs_1_), channel_id=1, source_target_pairs={{0,6},{2,0},{4,2},{6,4},{1,7},{3,1},{5,3},{7,5},{8,14},{10,8},{12,... | collective-permute-start | bytes 2359304 | tf_op jit(solution)/shard_map/rows/ppermute | solution.py:308
  107.5 0.6 reshape.34.refs_12_.refs_10_
  108.1 5.4 %up.4.refs_6_ = f32[384,768]{1,0:T(8,128)} custom-call(s32[2]{0:T(128)} %pad_add_fusion.place_ref, bf16[384,1024]{1,0:T(8,128)(2,1)} %get-tuple-element.39.refs_0_, bf16[384,1024]{1,0:T(8,128)(2,1)} %collective-permute-done.16.refs_1_, bf16[2,192,4096]{2,1,0:T(8,128)(2,1)} %refs_2_.3, bf16[1,192,4096]{2,1,0:T(8,128)(2,1)} %copy-done, ...), custom_call_target="tpu_custom_call" | custom-call | flops 1000 | bytes 1000 | tf_op jit(solution)/shard_map/up/pallas_call | solution.py:372
  113.5 0.7 collective-permute-done.13.refs_1_
  114.2 0.7 copy-done.12
  114.9 0.7 copy-done.13
  115.6 4.9 %down.3 = bf16[256,1024]{1,0:T(8,128)(2,1)} custom-call(s32[2]{0:T(128)} %pad_add_fusion.place_ref, bf16[256,384]{1,0:T(8,128)(2,1)} %up.3.refs_0_, bf16[256,384]{1,0:T(8,128)(2,1)} %copy-done.12, bf16[256,384]{1,0:T(8,128)(2,1)} %copy-done.13, bf16[256,384]{1,0:T(8,128)(2,1)} %copy-done.11, bf16[192,1024]{1,0:T(8,128)(2,1)} %get-tuple-element.24.refs_4_.same_ref, ...), custom_call_target="tpu_custom_call" | custom-call | flops 1000 | bytes 1000 | tf_op jit(solution)/shard_map/down/pallas_call | solution.py:383
  120.4 9.5 %all-to-all-start.1 = ((bf16[32,8,1024]{2,1,0:T(8,128)(2,1)}), bf16[32,8,1024]{2,1,0:T(8,128)(2,1)S(1)}, u32[]{:S(2)}, u32[]{:S(2)}) async-start(bf16[32,8,1024]{2,1,0:T(8,128)(2,1)} %bitcast.23), calls=%async_computation.1 | async-start | bytes 1048576 | tf_op jit(solution)/shard_map/down/all_to_all | solution.py:288
  130.0 1.1 collective-permute-done.17.refs_0_
  131.1 0.9 copy-done.5
  132.0 5.6 %up.5.h_ref = bf16[384,384]{1,0:T(8,128)(2,1)} custom-call(s32[2]{0:T(128)} %pad_add_fusion.place_ref, bf16[384,1024]{1,0:T(8,128)(2,1)} %copy-done.5, bf16[384,1024]{1,0:T(8,128)(2,1)} %collective-permute-done.18.refs_1_, bf16[2,192,4096]{2,1,0:T(8,128)(2,1)} %refs_2_.3, bf16[1,192,4096]{2,1,0:T(8,128)(2,1)} %copy-done, bf16[2,192,4096]{2,1,0:T(8,128)(2,1)} %refs_4_.5, ...), custom_call_target="tpu_custom_call" | custom-call | flops 1000 | bytes 1000 | tf_op jit(solution)/shard_map/up/pallas_call | solution.py:394
  137.5 2.7 %collective-permute-start.20 = (bf16[384,384]{1,0:T(8,128)(2,1)}, bf16[384,384]{1,0:T(8,128)(2,1)S(1)}, u32[]{:S(2)}, u32[]{:S(2)}) collective-permute-start(bf16[384,384]{1,0:T(8,128)(2,1)} %up.5.h_ref), channel_id=1, source_target_pairs={{0,6},{2,0},{4,2},{6,4},{1,7},{3,1},{5,3},{7,5},{8,14},{10,8},{12,... | collective-permute-start | bytes 884744 | tf_op jit(solution)/shard_map/down/ppermute | solution.py:308
  140.2 2.9 %down.4.refs_9_ = f32[384,1024]{1,0:T(8,128)} custom-call(bf16[384,384]{1,0:T(8,128)(2,1)} %up.5.h_ref, bf16[192,1024]{1,0:T(8,128)(2,1)} %get-tuple-element.24.refs_4_.same_ref, bf16[192,1024]{1,0:T(8,128)(2,1)} %copy-done.4), custom_call_target="tpu_custom_call" | custom-call | flops 1000 | bytes 1000 | tf_op jit(solution)/shard_map/down/pallas_call | solution.py:405
  143.1 4.1 %collective-permute-done.19.refs_0_ = bf16[384,384]{1,0:T(8,128)(2,1)S(1)} collective-permute-done((bf16[384,384]{1,0:T(8,128)(2,1)}, bf16[384,384]{1,0:T(8,128)(2,1)S(1)}, u32[]{:S(2)}, u32[]{:S(2)}) %collective-permute-start.19) | collective-permute-done | bytes 294944 | tf_op jit(solution)/shard_map/down/ppermute | solution.py:308
  147.2 3.8 %collective-permute-done.21.refs_2_ = bf16[384,384]{1,0:T(8,128)(2,1)S(1)} collective-permute-done((bf16[384,384]{1,0:T(8,128)(2,1)}, bf16[384,384]{1,0:T(8,128)(2,1)S(1)}, u32[]{:S(2)}, u32[]{:S(2)}) %collective-permute-start.21) | collective-permute-done | bytes 294944 | tf_op jit(solution)/shard_map/down/ppermute | solution.py:308
  151.0 0.7 copy-done.10
  151.7 5.6 %down.5 = bf16[256,1664]{1,0:T(8,128)(2,1)} custom-call(s32[2]{0:T(128)} %pad_add_fusion.place_ref, bf16[384,384]{1,0:T(8,128)(2,1)} %copy-done.8, bf16[384,384]{1,0:T(8,128)(2,1)} %copy-done.9, bf16[384,384]{1,0:T(8,128)(2,1)} %copy-done.10, bf16[192,1024]{1,0:T(8,128)(2,1)} %copy-done.2, bf16[192,1024]{1,0:T(8,128)(2,1)} %copy-done.3, ...), custom_call_target="tpu_custom_call" | custom-call | flops 1000 | bytes 1000 | tf_op jit(solution)/shard_map/down/pallas_call | solution.py:411
  157.3 28.5 %all_to_all.15 = bf16[32,8,1664]{2,1,0:T(8,128)(2,1)} all-to-all(bf16[32,8,1664]{2,1,0:T(8,128)(2,1)} %bitcast.21), channel_id=1, replica_groups=mesh['z'=8,'x'=4,'y'=4,'core'=2] {'z','x'}, dimensions={0} | all-to-all | bytes 1703936 | tf_op jit(solution)/shard_map/down/all_to_all | solution.py:288
  185.8 3.2 %combine.1 = (f32[128,512]{1,0:T(8,128)}, f32[128,512]{1,0:T(8,128)}, bf16[128,128]{1,0:T(8,128)(2,1)}) custom-call(s32[2]{0:T(128)} %pad_add_fusion.place_ref, s32[8,128]{1,0:T(8,128)} %bitcast.26, f32[8,128]{1,0:T(8,128)} %bitcast.28, bf16[256,1024]{1,0:T(8,128)(2,1)} %bitcast.22, bf16[256,1664]{1,0:T(8,128)(2,1)} %bitcast.20), custom_call_target="tpu_custom_call" | custom-call | flops 1000 | bytes 1000 | tf_op jit(solution)/shard_map/combine/pallas_call | solution.py:423
  188.9 6.4 %collective-permute-start.22 = (f32[128,512]{1,0:T(8,128)}, f32[128,512]{1,0:T(8,128)S(1)}, u32[]{:S(2)}, u32[]{:S(2)}) collective-permute-start(f32[128,512]{1,0:T(8,128)} %get-tuple-element.42), channel_id=1, source_target_pairs={{0,1},{1,0},{2,3},{3,2},{4,5},{5,4},{6,7},{7,6},{8,9},{9,8},{10,11... | collective-permute-start | bytes 786440 | tf_op jit(solution)/shard_map/combine/ppermute | solution.py:430
  195.3 1.4 collective-permute-done.22
  196.7 1.6 add_convert_fusion
  (61 shorter events, 1.1 us)
Async XLA Ops:
  8.4 12.2 %copy-start.20 = (bf16[192,1024]{1,0:T(8,128)(2,1)S(1)}, bf16[192,1024]{1,0:T(8,128)(2,1)}, u32[]{:S(2)}) copy-start(bf16[192,1024]{1,0:T(8,128)(2,1)} %get-tuple-element.25) | copy-start | bytes 1179652
  8.4 13.2 %copy-start.19 = (bf16[192,1024]{1,0:T(8,128)(2,1)S(1)}, bf16[192,1024]{1,0:T(8,128)(2,1)}, u32[]{:S(2)}) copy-start(bf16[192,1024]{1,0:T(8,128)(2,1)} %get-tuple-element.26) | copy-start | bytes 1179652
  8.4 14.5 %copy-start.18 = (bf16[192,1024]{1,0:T(8,128)(2,1)S(1)}, bf16[192,1024]{1,0:T(8,128)(2,1)}, u32[]{:S(2)}) copy-start(bf16[192,1024]{1,0:T(8,128)(2,1)} %get-tuple-element.27) | copy-start | bytes 1179652
  8.4 17.5 %copy-start.15 = (f32[2,192]{1,0:T(2,128)S(1)}, f32[2,192]{1,0:T(2,128)}, u32[]{:S(2)}) copy-start(f32[2,192]{1,0:T(2,128)} %param.17) | copy-start | bytes 4612
  8.4 17.5 %copy-start.16 = (f32[2,192]{1,0:T(2,128)S(1)}, f32[2,192]{1,0:T(2,128)}, u32[]{:S(2)}) copy-start(f32[2,192]{1,0:T(2,128)} %param.18) | copy-start | bytes 4612
  8.4 25.3 %copy-start.17 = (bf16[192,1024]{1,0:T(8,128)(2,1)S(1)}, bf16[192,1024]{1,0:T(8,128)(2,1)}, u32[]{:S(2)}) copy-start(bf16[192,1024]{1,0:T(8,128)(2,1)} %get-tuple-element.31) | copy-start | bytes 1179652
  8.4 51.9 %all-to-all-start = ((bf16[32,8,2688]{2,1,0:T(8,128)(2,1)}), bf16[32,8,2688]{2,1,0:T(8,128)(2,1)}, u32[]{:S(2)}, u32[]{:S(2)}) async-start(bf16[32,8,2688]{2,1,0:T(8,128)(2,1)} %bitcast.24), calls=%async_computation | async-start | bytes 2752512 | tf_op jit(solution)/shard_map/dispatch/all_to_all | solution.py:288
  20.6 7.2 %collective-permute-start = (bf16[192,1024]{1,0:T(8,128)(2,1)S(1)}, bf16[192,1024]{1,0:T(8,128)(2,1)S(1)}, u32[]{:S(2)}, u32[]{:S(2)}) collective-permute-start(bf16[192,1024]{1,0:T(8,128)(2,1)S(1)} %copy-done.20), channel_id=1, source_target_pairs={{0,1},{1,0},{2,3},{3,2},{4,5},{5,4},{6,7},{7,6},{8,9},{9,8},{10,11... | collective-permute-start | bytes 1179656 | tf_op jit(solution)/shard_map/route/ppermute | solution.py:285
  21.6 12.1 %collective-permute-start.1 = (bf16[192,1024]{1,0:T(8,128)(2,1)S(1)}, bf16[192,1024]{1,0:T(8,128)(2,1)S(1)}, u32[]{:S(2)}, u32[]{:S(2)}) collective-permute-start(bf16[192,1024]{1,0:T(8,128)(2,1)S(1)} %copy-done.19), channel_id=1, source_target_pairs={{0,2},{1,3},{2,4},{3,5},{4,6},{5,7},{6,0},{7,1},{8,10},{9,11},{10,... | collective-permute-start | bytes 1179656 | tf_op jit(solution)/shard_map/route/ppermute | solution.py:285
  22.9 19.6 %collective-permute-start.2 = (bf16[192,1024]{1,0:T(8,128)(2,1)S(1)}, bf16[192,1024]{1,0:T(8,128)(2,1)S(1)}, u32[]{:S(2)}, u32[]{:S(2)}) collective-permute-start(bf16[192,1024]{1,0:T(8,128)(2,1)S(1)} %copy-done.18), channel_id=1, source_target_pairs={{0,3},{1,2},{2,5},{3,4},{4,7},{5,6},{6,1},{7,0},{8,11},{9,10},{10,... | collective-permute-start | bytes 1179656 | tf_op jit(solution)/shard_map/route/ppermute | solution.py:285
  24.5 18.9 %collective-permute-start.3 = (bf16[192,1024]{1,0:T(8,128)(2,1)}, bf16[192,1024]{1,0:T(8,128)(2,1)}, u32[]{:S(2)}, u32[]{:S(2)}) collective-permute-start(bf16[192,1024]{1,0:T(8,128)(2,1)} %get-tuple-element.28), channel_id=1, source_target_pairs={{0,6},{1,7},{2,0},{3,1},{4,2},{5,3},{6,4},{7,5},{8,14},{9,15},{10,... | collective-permute-start | bytes 1179656 | tf_op jit(solution)/shard_map/route/ppermute | solution.py:285
  25.9 1.4 collective-permute-start.7
  27.2 17.7 %collective-permute-start.4 = (bf16[192,1024]{1,0:T(8,128)(2,1)}, bf16[192,1024]{1,0:T(8,128)(2,1)}, u32[]{:S(2)}, u32[]{:S(2)}) collective-permute-start(bf16[192,1024]{1,0:T(8,128)(2,1)} %get-tuple-element.29), channel_id=1, source_target_pairs={{0,7},{1,6},{2,1},{3,0},{4,3},{5,2},{6,5},{7,4},{8,15},{9,14},{10,... | collective-permute-start | bytes 1179656 | tf_op jit(solution)/shard_map/route/ppermute | solution.py:285
  27.7 15.6 %copy-start.4 = (bf16[192,1024]{1,0:T(8,128)(2,1)}, bf16[192,1024]{1,0:T(8,128)(2,1)S(1)}, u32[]{:S(2)}) copy-start(bf16[192,1024]{1,0:T(8,128)(2,1)S(1)} %collective-permute-done.refs_5_.cross_ref) | copy-start | bytes 1179652
  27.7 24.0 %collective-permute-start.5 = (bf16[192,1024]{1,0:T(8,128)(2,1)}, bf16[192,1024]{1,0:T(8,128)(2,1)}, u32[]{:S(2)}, u32[]{:S(2)}) collective-permute-start(bf16[192,1024]{1,0:T(8,128)(2,1)} %get-tuple-element.30), channel_id=1, source_target_pairs={{0,4},{1,5},{2,6},{3,7},{4,0},{5,1},{6,2},{7,3},{8,12},{9,13},{10,... | collective-permute-start | bytes 1179656 | tf_op jit(solution)/shard_map/route/ppermute | solution.py:285
  33.7 68.3 %copy-start.2 = (bf16[192,1024]{1,0:T(8,128)(2,1)}, bf16[192,1024]{1,0:T(8,128)(2,1)S(1)}, u32[]{:S(2)}) copy-start(bf16[192,1024]{1,0:T(8,128)(2,1)S(1)} %collective-permute-done.1.refs_6_.refs_3_) | copy-start | bytes 1179652
  33.7 26.6 %collective-permute-start.6 = (bf16[192,1024]{1,0:T(8,128)(2,1)S(1)}, bf16[192,1024]{1,0:T(8,128)(2,1)}, u32[]{:S(2)}, u32[]{:S(2)}) collective-permute-start(bf16[192,1024]{1,0:T(8,128)(2,1)S(1)} %copy-done.17), channel_id=1, source_target_pairs={{0,5},{1,4},{2,7},{3,6},{4,1},{5,0},{6,3},{7,2},{8,13},{9,12},{10,... | collective-permute-start | bytes 1179656 | tf_op jit(solution)/shard_map/route/ppermute | solution.py:285
  42.6 0.8 copy-start.3
  43.3 38.0 %collective-permute-start.11 = (bf16[1,192,4096]{2,1,0:T(8,128)(2,1)}, bf16[1,192,4096]{2,1,0:T(8,128)(2,1)S(1)}, u32[]{:S(2)}, u32[]{:S(2)}) collective-permute-start(bf16[1,192,4096]{2,1,0:T(8,128)(2,1)} %get-tuple-element.34), channel_id=1, source_target_pairs={{0,1},{1,0},{2,3},{3,2},{4,5},{5,4},{6,7},{7,6},{8,9},{9,8},{10,11... | collective-permute-start | bytes 4718600 | tf_op jit(solution)/shard_map/swap/ppermute | solution.py:318
  43.3 38.1 %collective-permute-start.12 = (bf16[1,192,4096]{2,1,0:T(8,128)(2,1)}, bf16[1,192,4096]{2,1,0:T(8,128)(2,1)}, u32[]{:S(2)}, u32[]{:S(2)}) collective-permute-start(bf16[1,192,4096]{2,1,0:T(8,128)(2,1)} %get-tuple-element.35), channel_id=1, source_target_pairs={{0,1},{1,0},{2,3},{3,2},{4,5},{5,4},{6,7},{7,6},{8,9},{9,8},{10,11... | collective-permute-start | bytes 4718600 | tf_op jit(solution)/shard_map/swap/ppermute | solution.py:318
  63.2 14.9 %collective-permute-start.9 = (bf16[256,1024]{1,0:T(8,128)(2,1)}, bf16[256,1024]{1,0:T(8,128)(2,1)S(1)}, u32[]{:S(2)}, u32[]{:S(2)}) collective-permute-start(bf16[256,1024]{1,0:T(8,128)(2,1)} %get-tuple-element.33.refs_0_), channel_id=1, source_target_pairs={{0,6},{2,0},{4,2},{6,4},{1,7},{3,1},{5,3},{7,5},{8,14},{10,8},{12,... | collective-permute-start | bytes 1572872 | tf_op jit(solution)/shard_map/rows/ppermute | solution.py:308
  66.4 15.0 %collective-permute-start.8 = (bf16[256,1024]{1,0:T(8,128)(2,1)}, bf16[256,1024]{1,0:T(8,128)(2,1)S(1)}, u32[]{:S(2)}, u32[]{:S(2)}) collective-permute-start(bf16[256,1024]{1,0:T(8,128)(2,1)} %get-tuple-element.33.refs_0_), channel_id=1, source_target_pairs={{0,2},{2,4},{4,6},{6,0},{1,3},{3,5},{5,7},{7,1},{8,10},{10,12},{12... | collective-permute-start | bytes 1572872 | tf_op jit(solution)/shard_map/rows/ppermute | solution.py:308
  78.0 3.3 %copy-start.6 = (bf16[256,1024]{1,0:T(8,128)(2,1)}, bf16[256,1024]{1,0:T(8,128)(2,1)S(1)}, u32[]{:S(2)}) copy-start(bf16[256,1024]{1,0:T(8,128)(2,1)S(1)} %collective-permute-done.9.refs_2_) | copy-start | bytes 1572868
  78.0 29.4 %copy-start.14 = (f32[2,4096]{1,0:T(2,128)S(1)}, f32[2,4096]{1,0:T(2,128)}, u32[]{:S(2)}) copy-start(f32[2,4096]{1,0:T(2,128)} %param.19) | copy-start | bytes 98308
  78.0 26.7 %collective-permute-start.16 = (bf16[384,1024]{1,0:T(8,128)(2,1)}, bf16[384,1024]{1,0:T(8,128)(2,1)}, u32[]{:S(2)}, u32[]{:S(2)}) collective-permute-start(bf16[384,1024]{1,0:T(8,128)(2,1)} %get-tuple-element.39.refs_0_), channel_id=1, source_target_pairs={{0,6},{2,0},{4,2},{6,4},{1,7},{3,1},{5,3},{7,5},{8,14},{10,8},{12,... | collective-permute-start | bytes 2359304 | tf_op jit(solution)/shard_map/rows/ppermute | solution.py:308
  81.4 0.8 copy-start.7
  81.4 13.7 %collective-permute-start.10 = (bf16[256,1024]{1,0:T(8,128)(2,1)S(1)}, bf16[256,1024]{1,0:T(8,128)(2,1)}, u32[]{:S(2)}, u32[]{:S(2)}) collective-permute-start(bf16[256,1024]{1,0:T(8,128)(2,1)S(1)} %collective-permute-done.8.refs_1_), channel_id=1, source_target_pairs={{0,2},{2,4},{4,6},{6,0},{1,3},{3,5},{5,7},{7,1},{8,10},{10,12},{12... | collective-permute-start | bytes 1572872 | tf_op jit(solution)/shard_map/rows/ppermute | solution.py:308
  81.4 13.6 %copy-start = (bf16[1,192,4096]{2,1,0:T(8,128)(2,1)}, bf16[1,192,4096]{2,1,0:T(8,128)(2,1)S(1)}, u32[]{:S(2)}) copy-start(bf16[1,192,4096]{2,1,0:T(8,128)(2,1)S(1)} %collective-permute-done.11.refs_5_.refs_3_) | copy-start | bytes 4718596
  102.0 11.5 %collective-permute-start.15 = (bf16[256,384]{1,0:T(8,128)(2,1)}, bf16[256,384]{1,0:T(8,128)(2,1)S(1)}, u32[]{:S(2)}, u32[]{:S(2)}) collective-permute-start(bf16[256,384]{1,0:T(8,128)(2,1)} %up.3.refs_0_), channel_id=1, source_target_pairs={{0,4},{2,6},{4,0},{6,2},{1,5},{3,7},{5,1},{7,3},{8,12},{10,14},{12... | collective-permute-start | bytes 589832 | tf_op jit(solution)/shard_map/down/ppermute | solution.py:308
  102.0 12.2 %collective-permute-start.13 = (bf16[256,384]{1,0:T(8,128)(2,1)}, bf16[256,384]{1,0:T(8,128)(2,1)S(1)}, u32[]{:S(2)}, u32[]{:S(2)}) collective-permute-start(bf16[256,384]{1,0:T(8,128)(2,1)} %up.3.refs_0_), channel_id=1, source_target_pairs={{0,2},{2,4},{4,6},{6,0},{1,3},{3,5},{5,7},{7,1},{8,10},{10,12},{12... | collective-permute-start | bytes 589832 | tf_op jit(solution)/shard_map/down/ppermute | solution.py:308
  102.1 12.1 %collective-permute-start.14 = (bf16[256,384]{1,0:T(8,128)(2,1)}, bf16[256,384]{1,0:T(8,128)(2,1)S(1)}, u32[]{:S(2)}, u32[]{:S(2)}) collective-permute-start(bf16[256,384]{1,0:T(8,128)(2,1)} %up.3.refs_0_), channel_id=1, source_target_pairs={{0,6},{2,0},{4,2},{6,4},{1,7},{3,1},{5,3},{7,5},{8,14},{10,8},{12,... | collective-permute-start | bytes 589832 | tf_op jit(solution)/shard_map/down/ppermute | solution.py:308
  104.8 26.3 %collective-permute-start.17 = (bf16[384,1024]{1,0:T(8,128)(2,1)}, bf16[384,1024]{1,0:T(8,128)(2,1)S(1)}, u32[]{:S(2)}, u32[]{:S(2)}) collective-permute-start(bf16[384,1024]{1,0:T(8,128)(2,1)} %get-tuple-element.39.refs_0_), channel_id=1, source_target_pairs={{0,2},{2,4},{4,6},{6,0},{1,3},{3,5},{5,7},{7,1},{8,10},{10,12},{12... | collective-permute-start | bytes 2359304 | tf_op jit(solution)/shard_map/rows/ppermute | solution.py:308
  104.8 26.3 %collective-permute-start.18 = (bf16[384,1024]{1,0:T(8,128)(2,1)}, bf16[384,1024]{1,0:T(8,128)(2,1)}, u32[]{:S(2)}, u32[]{:S(2)}) collective-permute-start(bf16[384,1024]{1,0:T(8,128)(2,1)} %collective-permute-done.16.refs_1_), channel_id=1, source_target_pairs={{0,6},{2,0},{4,2},{6,4},{1,7},{3,1},{5,3},{7,5},{8,14},{10,8},{12,... | collective-permute-start | bytes 2359304 | tf_op jit(solution)/shard_map/rows/ppermute | solution.py:308
  113.5 0.7 copy-start.11
  114.2 0.7 copy-start.12
  114.9 0.7 copy-start.13
  120.4 36.9 %all-to-all-start.1 = ((bf16[32,8,1024]{2,1,0:T(8,128)(2,1)}), bf16[32,8,1024]{2,1,0:T(8,128)(2,1)S(1)}, u32[]{:S(2)}, u32[]{:S(2)}) async-start(bf16[32,8,1024]{2,1,0:T(8,128)(2,1)} %bitcast.23), calls=%async_computation.1 | async-start | bytes 1048576 | tf_op jit(solution)/shard_map/down/all_to_all | solution.py:288
  131.1 0.9 copy-start.5
  137.5 9.7 %collective-permute-start.19 = (bf16[384,384]{1,0:T(8,128)(2,1)}, bf16[384,384]{1,0:T(8,128)(2,1)S(1)}, u32[]{:S(2)}, u32[]{:S(2)}) collective-permute-start(bf16[384,384]{1,0:T(8,128)(2,1)} %up.5.h_ref), channel_id=1, source_target_pairs={{0,2},{2,4},{4,6},{6,0},{1,3},{3,5},{5,7},{7,1},{8,10},{10,12},{12... | collective-permute-start | bytes 884744 | tf_op jit(solution)/shard_map/down/ppermute | solution.py:308
  137.5 9.7 %collective-permute-start.20 = (bf16[384,384]{1,0:T(8,128)(2,1)}, bf16[384,384]{1,0:T(8,128)(2,1)S(1)}, u32[]{:S(2)}, u32[]{:S(2)}) collective-permute-start(bf16[384,384]{1,0:T(8,128)(2,1)} %up.5.h_ref), channel_id=1, source_target_pairs={{0,6},{2,0},{4,2},{6,4},{1,7},{3,1},{5,3},{7,5},{8,14},{10,8},{12,... | collective-permute-start | bytes 884744 | tf_op jit(solution)/shard_map/down/ppermute | solution.py:308
  140.2 10.8 %collective-permute-start.21 = (bf16[384,384]{1,0:T(8,128)(2,1)}, bf16[384,384]{1,0:T(8,128)(2,1)S(1)}, u32[]{:S(2)}, u32[]{:S(2)}) collective-permute-start(bf16[384,384]{1,0:T(8,128)(2,1)} %up.5.h_ref), channel_id=1, source_target_pairs={{0,4},{2,6},{4,0},{6,2},{1,5},{3,7},{5,1},{7,3},{8,12},{10,14},{12... | collective-permute-start | bytes 884744 | tf_op jit(solution)/shard_map/down/ppermute | solution.py:308
  147.2 3.8 %copy-start.8 = (bf16[384,384]{1,0:T(8,128)(2,1)}, bf16[384,384]{1,0:T(8,128)(2,1)S(1)}, u32[]{:S(2)}) copy-start(bf16[384,384]{1,0:T(8,128)(2,1)S(1)} %collective-permute-done.19.refs_0_) | copy-start | bytes 884740
  147.2 3.8 %copy-start.9 = (bf16[384,384]{1,0:T(8,128)(2,1)}, bf16[384,384]{1,0:T(8,128)(2,1)S(1)}, u32[]{:S(2)}) copy-start(bf16[384,384]{1,0:T(8,128)(2,1)S(1)} %collective-permute-done.20.refs_1_) | copy-start | bytes 884740
  151.0 0.7 copy-start.10
  157.3 28.5 %copy-start.1 = (bf16[32,8,1024]{2,1,0:T(8,128)(2,1)}, bf16[32,8,1024]{2,1,0:T(8,128)(2,1)S(1)}, u32[]{:S(2)}) copy-start(bf16[32,8,1024]{2,1,0:T(8,128)(2,1)S(1)} %all-to-all-done.1) | copy-start | bytes 1572868
  188.9 7.8 %collective-permute-start.22 = (f32[128,512]{1,0:T(8,128)}, f32[128,512]{1,0:T(8,128)S(1)}, u32[]{:S(2)}, u32[]{:S(2)}) collective-permute-start(f32[128,512]{1,0:T(8,128)} %get-tuple-element.42), channel_id=1, source_target_pairs={{0,1},{1,0},{2,3},{3,2},{4,5},{5,4},{6,7},{7,6},{8,9},{9,8},{10,11... | collective-permute-start | bytes 786440 | tf_op jit(solution)/shard_map/combine/ppermute | solution.py:430

commit v3 on v2

--- a/solution.py
+++ b/solution.py
@@ -62,7 +62,7 @@
     )
 
 
-def route_kernel(n_dst, place_ref, ids_ref, tok_hbm, kv_ref, wg_hbm, wu_hbm, wd_hbm, out_ref, g_ref, u_ref, *refs):
+def route_kernel(n_dst, place_ref, ids_ref, tok_hbm, kv_ref, wd_hbm, out_ref, *refs):
     cuts, (tok_ref, sems) = refs[:-2], refs[-2:]
     quarter = tok_ref.shape[1]
     half = quarter // 2
@@ -72,8 +72,6 @@
     for (by, other), cut in zip(MOVES, cuts):
         cols = pl.ds(pl.multiple_of(lax.rem(y + by, 4) * quarter, quarter), quarter)
         copies.append((wd_hbm.at[1 - core if other else core, :, cols], cut))
-    sibling = pl.ds(1 - core, 1)
-    copies += [(wg_hbm.at[sibling], g_ref), (wu_hbm.at[sibling], u_ref)]
     copies = [pltpu.make_async_copy(a, b, sems.at[i]) for i, (a, b) in enumerate(copies)]
     for c in copies:
         c.start()
@@ -91,6 +89,16 @@
         dot(ones(low), tok[:, :half]) + dot(ones(high), tok[:, half:])
     ).astype(BF)
     for c in copies[1:]:
+        c.wait()
+
+
+def other_kernel(place_ref, wg_ref, wu_ref, g_ref, u_ref, sems):
+    sibling = pl.ds(1 - place_ref[1], 1)
+    copies = [(wg_ref.at[sibling], g_ref), (wu_ref.at[sibling], u_ref)]
+    copies = [pltpu.make_async_copy(a, b, sems.at[i]) for i, (a, b) in enumerate(copies)]
+    for c in copies:
+        c.start()
+    for c in copies:
         c.wait()
 
 
@@ -132,30 +140,20 @@
         acc_ref[...] += both
 
 
-def up_kernel(place_ref, *refs):
-    w_refs, s_ref, out_ref, acc_ref = refs[4:8], refs[8], refs[9], refs[10]
+def up_first_kernel(place_ref, *refs):
+    *x_refs, w0, w1, w2, w3, acc_ref = refs
     k = pl.program_id(0)
-    for i in range(4):
-        pl.when(k == i)(functools.partial(up_step, acc_ref, refs[i], w_refs, i == 0))
-
-    @pl.when(k == 3)
-    def _():
-        out_ref[...] = gated(acc_ref[...], s_ref)
-
-
-def up_first_kernel(place_ref, *refs):
+    for i, x_ref in enumerate(x_refs):
+        pl.when(k == i)(functools.partial(up_step, acc_ref, x_ref, (w0, w1, w2, w3), i == 0))
+
+
+def up_last_kernel(place_ref, *refs):
+    *x_refs, w0, w1, w2, w3, part_ref, s_ref, out_ref, acc_ref = refs
     k = pl.program_id(0)
-    for i in range(2):
-        pl.when(k == i)(functools.partial(up_step, refs[6], refs[i], refs[2:6], i == 0))
-
-
-def up_last_kernel(place_ref, *refs):
-    w_refs, part_ref, s_ref, out_ref, acc_ref = refs[2:6], refs[6], refs[7], refs[8], refs[9]
-    k = pl.program_id(0)
-    for i in range(2):
-        pl.when(k == i)(functools.partial(up_step, acc_ref, refs[i], w_refs, i == 0))
-
-    @pl.when(k == 1)
+    for i, x_ref in enumerate(x_refs):
+        pl.when(k == i)(functools.partial(up_step, acc_ref, x_ref, (w0, w1, w2, w3), i == 0))
+
+    @pl.when(k == len(x_refs) - 1)
     def _():
         out_ref[...] = gated(acc_ref[...] + part_ref[...], s_ref)
 
@@ -194,7 +192,7 @@
     out_ref[:, quarter + half :] = kv_ref[...]
 
 
-def combine_kernel(n_dst, place_ref, ids_ref, gates_ref, p_ref, q_ref, keep_ref, send_ref, kv_ref):
+def combine_first_kernel(n_dst, place_ref, ids_ref, gates_ref, in_ref, acc_ref, gates_out_ref):
     parity = place_ref[1]
     ids, gates = ids_ref[...], gates_ref[...]
     code, spread = slot_codes(ids, parity, n_dst, 200.0)
@@ -206,26 +204,29 @@
     top = gate.astype(BF)
     rest = (gate - top.astype(F32)).astype(BF)
     top, rest = dot(spread, top), dot(spread, rest)
-    first, second, low, high = selections(code)
-
-    def mix(where, rows):
-        return dot_tn(jnp.where(where, top, 0.0).astype(BF), rows) + dot_tn(
-            jnp.where(where, rest, 0.0).astype(BF), rows
-        )
-
-    quarter = p_ref.shape[1]
-    half = quarter // 2
-    mixed = q_ref[:, quarter : quarter + half]
-    sums = []
-    for where, lo in ((low, 0), (high, half)):
-        cols = slice(lo, lo + half)
-        sums.append(mix(first, p_ref[:, cols]) + mix(second, q_ref[:, cols]) + mix(where, mixed))
-    even = parity == 0
-    keep_ref[...] = jnp.where(even, sums[0], sums[1])
-    send_ref[...] = jnp.where(even, sums[1], sums[0])
-    n = q_ref.shape[0]
+    first, *others = selections(code)
+    for i, where in enumerate(others):
+        gates_out_ref[2 * i] = jnp.where(where, top, 0.0).astype(BF)
+        gates_out_ref[2 * i + 1] = jnp.where(where, rest, 0.0).astype(BF)
+    acc_ref[...] = dot_tn(jnp.where(first, top, 0.0).astype(BF), in_ref[...]) + dot_tn(
+        jnp.where(first, rest, 0.0).astype(BF), in_ref[...]
+    )
+
+
+def combine_last_kernel(place_ref, g_ref, acc_ref, in_ref, keep_ref, send_ref, kv_ref):
+    half = keep_ref.shape[1]
+    quarter = 2 * half
+    rows = in_ref[:, :quarter]
+    mixed = in_ref[:, quarter : quarter + half]
+    sums = acc_ref[...] + dot_tn(g_ref[0], rows) + dot_tn(g_ref[1], rows)
+    low = sums[:, :half] + dot_tn(g_ref[2], mixed) + dot_tn(g_ref[3], mixed)
+    high = sums[:, half:] + dot_tn(g_ref[4], mixed) + dot_tn(g_ref[5], mixed)
+    even = place_ref[1] == 0
+    keep_ref[...] = jnp.where(even, low, high)
+    send_ref[...] = jnp.where(even, high, low)
+    n, tok = in_ref.shape[0], keep_ref.shape[0]
     row, col = iota((tok, n), 0), iota((tok, n), 1)
-    kv_ref[...] = dot(ones(col == (row % PAGE) * ROWS + row // PAGE), q_ref[:, quarter + half :]).astype(BF)
+    kv_ref[...] = dot(ones(col == (row % PAGE) * ROWS + row // PAGE), in_ref[:, quarter + half :]).astype(BF)
 
 
 def sds(*shape, dtype=BF):
@@ -238,6 +239,7 @@
 
 CHEAP = pl.CostEstimate(flops=1000, bytes_accessed=1000, transcendentals=0)
 PARAMS = pltpu.CompilerParams(vmem_limit_bytes=62 * 1024 * 1024)
+SMALL = pltpu.CompilerParams(vmem_limit_bytes=24 * 1024 * 1024)
 
 
 def on_device(
@@ -266,15 +268,24 @@
         return lax.optimization_barrier((v, *others))[0]
 
     with jax.named_scope("route"):
-        outgoing, other_g, other_u, *cuts = pl.pallas_call(
+        outgoing, *cuts = pl.pallas_call(
             functools.partial(route_kernel, n_dp),
-            in_specs=[smem, vmem, hbm, vmem, hbm, hbm, hbm],
-            out_specs=[vmem] * 11,
-            out_shape=[sds(rows, quarter + payload)] + [sds(1, hid, width)] * 2 + [sds(hid, quarter)] * 8,
-            scratch_shapes=[pltpu.VMEM((tok, quarter), BF), pltpu.SemaphoreType.DMA((11,))],
+            in_specs=[smem, vmem, hbm, vmem, hbm],
+            out_specs=[vmem] * 9,
+            out_shape=[sds(rows, quarter + payload)] + [sds(hid, quarter)] * 8,
+            scratch_shapes=[pltpu.VMEM((tok, quarter), BF), pltpu.SemaphoreType.DMA((9,))],
             compiler_params=PARAMS,
             cost_estimate=CHEAP,
-        )(place, ids_t, tokens, kv_rows, w_gate, w_up, w_down)
+        )(place, ids_t, tokens, kv_rows, w_down)
+        other_g, other_u = pl.pallas_call(
+            other_kernel,
+            in_specs=[smem, hbm, hbm],
+            out_specs=[vmem] * 2,
+            out_shape=[sds(1, hid, width)] * 2,
+            scratch_shapes=[pltpu.SemaphoreType.DMA((2,))],
+            compiler_params=PARAMS,
+            cost_estimate=CHEAP,
+        )(place, after(w_gate, outgoing), w_up)
         wd = [cuts[0]]
         for (by, other), v in zip(MOVES[1:], cuts[1:]):
             pairs = [
@@ -282,6 +293,8 @@
                 for i in range(n_y)
                 for c in range(n_core)
             ]
+            if len(wd) == 7:
+                v = after(v, other_g)
             wd.append(lax.ppermute(v, ("y", "core"), pairs))
 
     def exchange(v):
@@ -310,7 +323,7 @@
     with jax.named_scope("rows"):
         p_left, p_right = shift(x_p, 1), shift(x_p, -1)
         p_far = shift(p_left, 1)
-        q_right = shift(after(x_q, p_right), -1)
+        q_right = shift(after(x_q, p_right, p_left), -1)
         q_left = shift(after(x_q, p_far), 1)
         q_far = shift(q_right, -1)
 
@@ -334,7 +347,7 @@
 
         return [own(), other(), own(), other()]
 
-    def call(kernel, steps, in_specs, out_specs, out_shape, scratch=()):
+    def call(kernel, steps, in_specs, out_specs, out_shape, scratch=(), params=PARAMS):
         return pl.pallas_call(
             kernel,
             grid_spec=pltpu.PrefetchScalarGridSpec(
@@ -345,7 +358,7 @@
                 scratch_shapes=list(scratch),
             ),
             out_shape=out_shape,
-            compiler_params=PARAMS,
+            compiler_params=params,
             cost_estimate=CHEAP,
         )
 
@@ -358,14 +371,21 @@
 
     with jax.named_scope("up"):
         r = rows
+        both_p = call(
+            up_first_kernel,
+            3,
+            [whole(r, quarter)] * 3 + weight_specs(0, 3, 1),
+            whole(r, 2 * units),
+            sds(r, 2 * units, dtype=F32),
+        )(place, x_p, p_left, p_right, *weights)
         h_p = call(
-            up_kernel,
-            4,
-            [whole(r, quarter)] * 4 + weight_specs(0, 3, 1, 2) + [whole(2, units)],
+            up_last_kernel,
+            1,
+            [whole(r, quarter)] + weight_specs(2) + [whole(r, 2 * units), whole(2, units)],
             whole(r, units),
             sds(r, units),
             acc(r),
-        )(place, x_p, p_left, p_right, p_far, *weights, scales)
+        )(place, p_far, *weights, both_p, scales)
 
     with jax.named_scope("up"):
         r = rows + rows // 2
@@ -386,6 +406,7 @@
             [whole(r, units)] * 4 + [whole(hid, quarter)] * 8 + [channel],
             whole(r, quarter),
             sds(r, quarter),
+            params=SMALL,
         )(place, h_p, *near, *wd, down_scale)
         back_p = exchange(v_p)
 
@@ -405,7 +426,7 @@
         part = pl.pallas_call(
             down_first_kernel,
             out_shape=sds(r, quarter, dtype=F32),
-            compiler_params=PARAMS,
+            compiler_params=SMALL,
             cost_estimate=CHEAP,
         )(h_q, *wd[:2])
         v_q = call(
@@ -416,17 +437,25 @@
             + [whole(r, quarter), channel, whole(rows, kv_cols)],
             whole(rows, payload),
             sds(rows, payload),
+            params=SMALL,
         )(place, *near, *wd[2:], part, down_scale, kv_q)
         back_q = exchange(v_q)
 
     with jax.named_scope("combine"):
+        total, picked = pl.pallas_call(
+            functools.partial(combine_first_kernel, n_dp),
+            in_specs=[smem] + [vmem] * 3,
+            out_shape=[sds(tok, quarter, dtype=F32), sds(6, rows, tok)],
+            compiler_params=SMALL,
+            cost_estimate=CHEAP,
+        )(place, ids_t, gates_t, back_p)
         keep, send, kv_cache = pl.pallas_call(
-            functools.partial(combine_kernel, n_dp),
-            in_specs=[pl.BlockSpec(memory_space=pltpu.SMEM)] + [pl.BlockSpec(memory_space=pltpu.VMEM)] * 4,
+            combine_last_kernel,
+            in_specs=[smem] + [vmem] * 3,
             out_shape=[sds(tok, half, dtype=F32), sds(tok, half, dtype=F32), sds(tok, kv_cols)],
-            compiler_params=PARAMS,
-            cost_estimate=CHEAP,
-        )(place, ids_t, gates_t, back_p, back_q)
+            compiler_params=SMALL,
+            cost_estimate=CHEAP,
+        )(place, picked, total, back_q)
         moe_out = (keep + lax.ppermute(send, "core", [(0, 1), (1, 0)])).astype(BF)
     return moe_out, kv_cache.reshape(tok // PAGE, PAGE, kv_cols)
 

time: 199 us -> 189 us (0.950)
  blocking collectives: 28.5 us -> 0 us
  starting transfers between devices: 53.8 us -> 63.2 us
  waiting for transfers between devices: 62.8 us -> 71.3 us
    all_to_all x1 -> x0, blocking collectives: 28.5 us -> none  [exchange(): lax.all_to_all(v.reshape(n_dp, ROWS, v.shape[-1]), DP, 0, 0, tiled=True)]
    all_to_all x2 -> x3, waiting for transfers between devices: 0.01 us -> 17.6 us  [exchange(): lax.all_to_all(v.reshape(n_dp, ROWS, v.shape[-1]), DP, 0, 0, tiled=True)]
    all_to_all x2 -> x3, starting transfers between devices: 21.6 us -> 31 us  [exchange(): lax.all_to_all(v.reshape(n_dp, ROWS, v.shape[-1]), DP, 0, 0, tiled=True)]
    pallas_call x2 -> x5, Pallas kernels: 10.1 us -> 17.1 us  [the longest x1 6.17 us: on_device(): call(up_first_kernel, 3, [whole(r, quarter)] * 3 + weight_specs(0, 3, 1),...]
    ppermute x12, waiting for transfers between devices: 34.3 us -> 29.4 us  [shift(): return lax.ppermute(v, 'y', [(i, (i + by) % n_y) for i in range(n_y)])]
    ppermute x7, waiting for transfers between devices: 26.3 us -> 23.2 us  [on_device(): wd.append(lax.ppermute(v, ('y', 'core'), pairs))]
    pallas_call x1, Pallas kernels: 5.57 us -> 3.14 us  [on_device(): call(down_last_kernel, 1, [whole(r, units)] * 3 + [whole(hid, quarter)] *...]
    pallas_call x1, Pallas kernels: 7.11 us -> 4.93 us  [on_device(): pl.pallas_call(functools.partial(route_kernel, n_dp), in_specs=[smem, vme...]
  transfers between devices with their start and end apart: 25 -> 26, of which waited for: 13 -> 14; matrix products, arithmetic and copies ran while one was open for 1% -> 0% of each run, Pallas kernels for 17% -> 20%
where the time goes in v3:
time: 189 us
  waiting for transfers between devices  71.3 us (38%)
  starting transfers between devices  63.2 us (33%)
  Pallas kernels  44.6 us (24%)
  local copies, waits for them, and re-layouts  6.52 us (3%)
  other arithmetic  2.02 us (1%)
    all_to_all x3, starting transfers between devices, exchange(): lax.all_to_all(v.reshape(n_dp, ROWS, v.shape[-1]), DP, 0, 0, tiled=True)  31 us
    ppermute x12, waiting for transfers between devices, shift(): return lax.ppermute(v, 'y', [(i, (i + by) % n_y) for i in range(n_y)])  29.4 us
    ppermute x7, waiting for transfers between devices, on_device(): wd.append(lax.ppermute(v, ('y', 'core'), pairs))  23.2 us
    all_to_all x3, waiting for transfers between devices, exchange(): lax.all_to_all(v.reshape(n_dp, ROWS, v.shape[-1]), DP, 0, 0, tiled=True)  17.6 us
    ppermute x12, starting transfers between devices, shift(): return lax.ppermute(v, 'y', [(i, (i + by) % n_y) for i in range(n_y)])  14.9 us
    ppermute x7, starting transfers between devices, on_device(): wd.append(lax.ppermute(v, ('y', 'core'), pairs))  9.89 us
    unnamed x44, local copies, waits for them, and re-layouts  6.5 us
    ppermute x1, starting transfers between devices, on_device(): moe_out = (keep + lax.ppermute(send, 'core', [(0, 1), (1, 0)])).astype(BF)  6.37 us
  transfers between devices with their start and end apart: 26, of which 14 were waited for; matrix products, arithmetic and copies ran while one was open for 0% of the time, Pallas kernels for 20%

profile of v3, /device:TPU:1, one launch (start us, length us, event | category | flops | bytes accessed | tf_op | source)
XLA Modules:
  0.0 188.5 jit_solution(10994476507246848366)
XLA Ops:
  1.3 4.9 %route.2 = (bf16[256,2688]{1,0:T(8,128)(2,1)}, bf16[192,1024]{1,0:T(8,128)(2,1)}, bf16[192,1024]{1,0:T(8,128)(2,1)}, bf16[192,1024]{1,0:T(8,128)(2,1)}, bf16[192...) custom-call(s32[2]{0:T(128)} %pad_add_fusion.place_ref, ...), custom_call_target="tpu_custom_call" | custom-call | flops 1000 | bytes 1000 | tf_op jit(solution)/shard_map/route/pallas_call | solution.py:271
  6.3 12.0 %all-to-all-start = ((bf16[32,8,2688]{2,1,0:T(8,128)(2,1)}), bf16[32,8,2688]{2,1,0:T(8,128)(2,1)}, u32[]{:S(2)}, u32[]{:S(2)}) async-start(bf16[32,8,2688]{2,1,0:T(8,128)(2,1)} %bitcast.25), calls=%async_computation | async-start | bytes 2752512 | tf_op jit(solution)/shard_map/dispatch/all_to_all | solution.py:301
  18.3 1.0 collective-permute-start
  19.3 1.3 collective-permute-start.1
  20.6 1.5 collective-permute-start.2
  22.1 1.4 collective-permute-start.3
  24.1 4.2 %route.3 = (bf16[1,192,4096]{2,1,0:T(8,128)(2,1)}, bf16[1,192,4096]{2,1,0:T(8,128)(2,1)}) custom-call(s32[2]{0:T(128)} %pad_add_fusion.place_ref, bf16[2,192,4096]{2,1,0:T(8,128)(2,1)} %refs_2_.3, bf16[2,192,4096]{2,1,0:T(8,128)(2,1)} %refs_4_.3), custom_call_target="tpu_custom_call" | custom-call | flops 1000 | bytes 1000 | tf_op jit(solution)/shard_map/route/pallas_call | solution.py:280
  28.7 1.5 collective-permute-start.5
  30.3 1.3 collective-permute-done.1.refs_6_.refs_3_
  31.6 2.7 %collective-permute-start.6 = (bf16[192,1024]{1,0:T(8,128)(2,1)S(1)}, bf16[192,1024]{1,0:T(8,128)(2,1)S(1)}, u32[]{:S(2)}, u32[]{:S(2)}) collective-permute-start(bf16[192,1024]{1,0:T(8,128)(2,1)S(1)} %copy-done.20), channel_id=1, source_target_pairs={{0,5},{1,4},{2,7},{3,6},{4,1},{5,0},{6,3},{7,2},{8,13},{9,12},{10,... | collective-permute-start | bytes 1179656 | tf_op jit(solution)/shard_map/route/ppermute | solution.py:298
  34.3 6.1 %collective-permute-done.2.refs_7_.refs_4_ = bf16[192,1024]{1,0:T(8,128)(2,1)S(1)} collective-permute-done((bf16[192,1024]{1,0:T(8,128)(2,1)}, bf16[192,1024]{1,0:T(8,128)(2,1)S(1)}, u32[]{:S(2)}, u32[]{:S(2)}) %collective-permute-start.2) | collective-permute-done | bytes 393248 | tf_op jit(solution)/shard_map/route/ppermute | solution.py:298
  41.6 1.0 collective-permute-done.4.refs_9_.refs_6_
  42.6 7.0 %collective-permute-done.5.refs_10_.refs_7_ = bf16[192,1024]{1,0:T(8,128)(2,1)S(1)} collective-permute-done((bf16[192,1024]{1,0:T(8,128)(2,1)}, bf16[192,1024]{1,0:T(8,128)(2,1)S(1)}, u32[]{:S(2)}, u32[]{:S(2)}) %collective-permute-start.5) | collective-permute-done | bytes 393248 | tf_op jit(solution)/shard_map/route/ppermute | solution.py:298
  49.6 0.7 copy-done.2
  50.3 7.8 %collective-permute-done.6.refs_11_.refs_8_ = bf16[192,1024]{1,0:T(8,128)(2,1)S(1)} collective-permute-done((bf16[192,1024]{1,0:T(8,128)(2,1)S(1)}, bf16[192,1024]{1,0:T(8,128)(2,1)S(1)}, u32[]{:S(2)}, u32[]{:S(2)}) %collective-permute-start.6) | collective-permute-done | bytes 393248 | tf_op jit(solution)/shard_map/route/ppermute | solution.py:298
  58.1 0.8 copy-done.5
  58.9 2.9 %unpack.1 = (bf16[256,1024]{1,0:T(8,128)(2,1)}, bf16[384,1024]{1,0:T(8,128)(2,1)}, bf16[256,128]{1,0:T(8,128)(2,1)}) custom-call(bf16[256,2688]{1,0:T(8,128)(2,1)} %bitcast.5.in_ref, s32[1,128]{1,0:T(1,128)} %bitcast.30), custom_call_target="tpu_custom_call" | custom-call | flops 1000 | bytes 1000 | tf_op jit(solution)/shard_map/unpack/pallas_call | solution.py:313
  61.8 2.2 %collective-permute-start.8 = (bf16[256,1024]{1,0:T(8,128)(2,1)}, bf16[256,1024]{1,0:T(8,128)(2,1)}, u32[]{:S(2)}, u32[]{:S(2)}) collective-permute-start(bf16[256,1024]{1,0:T(8,128)(2,1)} %get-tuple-element.40.refs_0_), channel_id=1, source_target_pairs={{0,2},{2,4},{4,6},{6,0},{1,3},{3,5},{5,7},{7,1},{8,10},{10,12},{12... | collective-permute-start | bytes 1572872 | tf_op jit(solution)/shard_map/rows/ppermute | solution.py:321
  63.9 1.6 collective-permute-start.12
  65.5 12.1 %collective-permute-done.8.refs_1_ = bf16[256,1024]{1,0:T(8,128)(2,1)} collective-permute-done((bf16[256,1024]{1,0:T(8,128)(2,1)}, bf16[256,1024]{1,0:T(8,128)(2,1)}, u32[]{:S(2)}, u32[]{:S(2)}) %collective-permute-start.8) | collective-permute-done | bytes 524320 | tf_op jit(solution)/shard_map/rows/ppermute | solution.py:321
  77.7 3.0 %collective-permute-start.16 = (bf16[384,1024]{1,0:T(8,128)(2,1)}, bf16[384,1024]{1,0:T(8,128)(2,1)}, u32[]{:S(2)}, u32[]{:S(2)}) collective-permute-start(bf16[384,1024]{1,0:T(8,128)(2,1)} %get-tuple-element.47.refs_0_), channel_id=1, source_target_pairs={{0,6},{2,0},{4,2},{6,4},{1,7},{3,1},{5,3},{7,5},{8,14},{10,8},{12,... | collective-permute-start | bytes 2359304 | tf_op jit(solution)/shard_map/rows/ppermute | solution.py:321
  80.8 6.2 %up.4.refs_5_ = f32[256,768]{1,0:T(8,128)} custom-call(s32[2]{0:T(128)} %pad_add_fusion.place_ref, bf16[256,1024]{1,0:T(8,128)(2,1)} %get-tuple-element.40.refs_0_, bf16[256,1024]{1,0:T(8,128)(2,1)} %collective-permute-done.8.refs_1_, bf16[256,1024]{1,0:T(8,128)(2,1)} %collective-permute-done.12.refs_2_, bf16[2,192,4096]{2,1,0:T(8,128)(2,1)} %refs_2_.3, ...), custom_call_target="tpu_custom_call" | custom-call | flops 1000 | bytes 1000 | tf_op jit(solution)/shard_map/up/pallas_call | solution.py:374
  86.9 8.1 %collective-permute-done.9.refs_0_ = bf16[256,1024]{1,0:T(8,128)(2,1)} collective-permute-done((bf16[256,1024]{1,0:T(8,128)(2,1)}, bf16[256,1024]{1,0:T(8,128)(2,1)}, u32[]{:S(2)}, u32[]{:S(2)}) %collective-permute-start.9) | collective-permute-done | bytes 524320 | tf_op jit(solution)/shard_map/rows/ppermute | solution.py:321
  95.1 3.7 %up.5.refs_0_ = bf16[256,384]{1,0:T(8,128)(2,1)} custom-call(s32[2]{0:T(128)} %pad_add_fusion.place_ref, bf16[256,1024]{1,0:T(8,128)(2,1)} %collective-permute-done.9.refs_0_, bf16[2,192,4096]{2,1,0:T(8,128)(2,1)} %refs_2_.3, bf16[1,192,4096]{2,1,0:T(8,128)(2,1)} %collective-permute-done.10.refs_4_.refs_2_.refs_3_, bf16[2,192,4096]{2,1,0:T(8,128)(2,1)} %refs_4_.3, ...), custom_call_target="tpu_custom_call" | custom-call | flops 1000 | bytes 1000 | tf_op jit(solution)/shard_map/up/pallas_call | solution.py:381
  98.8 2.7 %collective-permute-start.14 = (bf16[256,384]{1,0:T(8,128)(2,1)}, bf16[256,384]{1,0:T(8,128)(2,1)}, u32[]{:S(2)}, u32[]{:S(2)}) collective-permute-start(bf16[256,384]{1,0:T(8,128)(2,1)} %up.5.refs_0_), channel_id=1, source_target_pairs={{0,6},{2,0},{4,2},{6,4},{1,7},{3,1},{5,3},{7,5},{8,14},{10,8},{12,... | collective-permute-start | bytes 589832 | tf_op jit(solution)/shard_map/down/ppermute | solution.py:321
  101.5 2.7 %collective-permute-start.18 = (bf16[384,1024]{1,0:T(8,128)(2,1)}, bf16[384,1024]{1,0:T(8,128)(2,1)}, u32[]{:S(2)}, u32[]{:S(2)}) collective-permute-start(bf16[384,1024]{1,0:T(8,128)(2,1)} %collective-permute-done.16.refs_1_), channel_id=1, source_target_pairs={{0,6},{2,0},{4,2},{6,4},{1,7},{3,1},{5,3},{7,5},{8,14},{10,8},{12,... | collective-permute-start | bytes 2359304 | tf_op jit(solution)/shard_map/rows/ppermute | solution.py:321
  104.2 5.5 %up.6.refs_6_ = f32[384,768]{1,0:T(8,128)} custom-call(s32[2]{0:T(128)} %pad_add_fusion.place_ref, bf16[384,1024]{1,0:T(8,128)(2,1)} %get-tuple-element.47.refs_0_, bf16[384,1024]{1,0:T(8,128)(2,1)} %collective-permute-done.16.refs_1_, bf16[2,192,4096]{2,1,0:T(8,128)(2,1)} %refs_2_.3, bf16[1,192,4096]{2,1,0:T(8,128)(2,1)} %collective-permute-done.10.refs_4_.refs_2_.refs_3_, ...), custom_call_target="tpu_custom_call" | custom-call | flops 1000 | bytes 1000 | tf_op jit(solution)/shard_map/up/pallas_call | solution.py:392
  109.8 1.2 collective-permute-done.13.refs_1_
  111.0 1.0 copy-done.3
  112.0 1.0 copy-done.6
  113.0 1.0 copy-done.8
  114.0 3.8 %down.3 = bf16[256,1024]{1,0:T(8,128)(2,1)} custom-call(s32[2]{0:T(128)S(1)} %copy-done.13, bf16[256,384]{1,0:T(8,128)(2,1)S(1)} %copy-done.11, bf16[256,384]{1,0:T(8,128)(2,1)} %collective-permute-done.13.refs_1_, bf16[256,384]{1,0:T(8,128)(2,1)} %collective-permute-done.14.refs_2_, bf16[256,384]{1,0:T(8,128)(2,1)S(1)} %collective-permute-done.15.refs_3_, ...), custom_call_target="tpu_custom_call" | custom-call | flops 1000 | bytes 1000 | tf_op jit(solution)/shard_map/down/pallas_call | solution.py:403
  117.8 9.4 %all-to-all-start.1 = ((bf16[32,8,1024]{2,1,0:T(8,128)(2,1)}), bf16[32,8,1024]{2,1,0:T(8,128)(2,1)S(1)}, u32[]{:S(2)}, u32[]{:S(2)}) async-start(bf16[32,8,1024]{2,1,0:T(8,128)(2,1)} %bitcast.9), calls=%async_computation.1 | async-start | bytes 1048576 | tf_op jit(solution)/shard_map/down/all_to_all | solution.py:301
  127.9 5.7 %up.7.h_ref = bf16[384,384]{1,0:T(8,128)(2,1)} custom-call(s32[2]{0:T(128)} %pad_add_fusion.place_ref, bf16[384,1024]{1,0:T(8,128)(2,1)} %collective-permute-done.17.refs_0_, bf16[384,1024]{1,0:T(8,128)(2,1)} %collective-permute-done.18.refs_1_, bf16[2,192,4096]{2,1,0:T(8,128)(2,1)} %refs_2_.3, ...), custom_call_target="tpu_custom_call" | custom-call | flops 1000 | bytes 1000 | tf_op jit(solution)/shard_map/up/pallas_call | solution.py:415
  133.7 2.7 %collective-permute-start.20 = (bf16[384,384]{1,0:T(8,128)(2,1)}, bf16[384,384]{1,0:T(8,128)(2,1)S(1)}, u32[]{:S(2)}, u32[]{:S(2)}) collective-permute-start(bf16[384,384]{1,0:T(8,128)(2,1)} %up.7.h_ref), channel_id=1, source_target_pairs={{0,6},{2,0},{4,2},{6,4},{1,7},{3,1},{5,3},{7,5},{8,14},{10,8},{12,... | collective-permute-start | bytes 884744 | tf_op jit(solution)/shard_map/down/ppermute | solution.py:321
  136.4 1.0 copy-done.9
  137.4 1.0 copy-done.10
  138.3 1.6 down.4.refs_9_
  139.9 4.2 %collective-permute-done.19.refs_0_ = bf16[384,384]{1,0:T(8,128)(2,1)S(1)} collective-permute-done((bf16[384,384]{1,0:T(8,128)(2,1)}, bf16[384,384]{1,0:T(8,128)(2,1)S(1)}, u32[]{:S(2)}, u32[]{:S(2)}) %collective-permute-start.19) | collective-permute-done | bytes 294944 | tf_op jit(solution)/shard_map/down/ppermute | solution.py:321
  144.1 3.0 %collective-permute-done.21.refs_2_ = bf16[384,384]{1,0:T(8,128)(2,1)S(1)} collective-permute-done((bf16[384,384]{1,0:T(8,128)(2,1)}, bf16[384,384]{1,0:T(8,128)(2,1)S(1)}, u32[]{:S(2)}, u32[]{:S(2)}) %collective-permute-start.21) | collective-permute-done | bytes 294944 | tf_op jit(solution)/shard_map/down/ppermute | solution.py:321
  147.1 3.1 %down.5 = bf16[256,1664]{1,0:T(8,128)(2,1)} custom-call(s32[2]{0:T(128)S(1)} %copy-done.14, bf16[384,384]{1,0:T(8,128)(2,1)S(1)} %collective-permute-done.19.refs_0_, bf16[384,384]{1,0:T(8,128)(2,1)S(1)} %collective-permute-done.20.refs_1_, bf16[384,384]{1,0:T(8,128)(2,1)S(1)} %collective-permute-done.21.refs_2_, ...), custom_call_target="tpu_custom_call" | custom-call | flops 1000 | bytes 1000 | tf_op jit(solution)/shard_map/down/pallas_call | solution.py:432
  150.2 9.6 %all-to-all-start.2 = ((bf16[32,8,1664]{2,1,0:T(8,128)(2,1)}), bf16[32,8,1664]{2,1,0:T(8,128)(2,1)S(1)}, u32[]{:S(2)}, u32[]{:S(2)}) async-start(bf16[32,8,1664]{2,1,0:T(8,128)(2,1)} %bitcast.11), calls=%async_computation.2 | async-start | bytes 1703936 | tf_op jit(solution)/shard_map/down/all_to_all | solution.py:301
  159.8 1.3 combine.2
  161.1 17.6 %all-to-all-done.2 = bf16[32,8,1664]{2,1,0:T(8,128)(2,1)S(1)} async-done(((bf16[32,8,1664]{2,1,0:T(8,128)(2,1)}), bf16[32,8,1664]{2,1,0:T(8,128)(2,1)S(1)}, u32[]{:S(2)}, u32[]{:S(2)}) %all-to-all-start.2) | async-done | bytes 852000 | tf_op jit(solution)/shard_map/down/all_to_all | solution.py:301
  178.7 1.6 combine.3
  180.3 6.4 %collective-permute-start.22 = (f32[128,512]{1,0:T(8,128)S(1)}, f32[128,512]{1,0:T(8,128)S(1)}, u32[]{:S(2)}, u32[]{:S(2)}) collective-permute-start(f32[128,512]{1,0:T(8,128)S(1)} %get-tuple-element.50), channel_id=1, source_target_pairs={{0,1},{1,0},{2,3},{3,2},{4,5},{5,4},{6,7},{7,6},{8,9},{9,8},{10,11... | collective-permute-start | bytes 786440 | tf_op jit(solution)/shard_map/combine/ppermute | solution.py:459
  186.7 1.2 collective-permute-done.22
  187.9 0.7 add_convert_fusion
  (65 shorter events, 3.7 us)
Async XLA Ops:
  6.2 17.3 %copy-start.18 = (f32[2,192]{1,0:T(2,128)S(1)}, f32[2,192]{1,0:T(2,128)}, u32[]{:S(2)}) copy-start(f32[2,192]{1,0:T(2,128)} %param.17) | copy-start | bytes 4612
  6.2 17.3 %copy-start.19 = (f32[2,192]{1,0:T(2,128)S(1)}, f32[2,192]{1,0:T(2,128)}, u32[]{:S(2)}) copy-start(f32[2,192]{1,0:T(2,128)} %param.18) | copy-start | bytes 4612
  6.3 52.6 %all-to-all-start = ((bf16[32,8,2688]{2,1,0:T(8,128)(2,1)}), bf16[32,8,2688]{2,1,0:T(8,128)(2,1)}, u32[]{:S(2)}, u32[]{:S(2)}) async-start(bf16[32,8,2688]{2,1,0:T(8,128)(2,1)} %bitcast.25), calls=%async_computation | async-start | bytes 2752512 | tf_op jit(solution)/shard_map/dispatch/all_to_all | solution.py:301
  18.3 10.5 %collective-permute-start = (bf16[192,1024]{1,0:T(8,128)(2,1)}, bf16[192,1024]{1,0:T(8,128)(2,1)}, u32[]{:S(2)}, u32[]{:S(2)}) collective-permute-start(bf16[192,1024]{1,0:T(8,128)(2,1)} %get-tuple-element.29), channel_id=1, source_target_pairs={{0,1},{1,0},{2,3},{3,2},{4,5},{5,4},{6,7},{7,6},{8,9},{9,8},{10,11... | collective-permute-start | bytes 1179656 | tf_op jit(solution)/shard_map/route/ppermute | solution.py:298
  19.3 12.3 %collective-permute-start.1 = (bf16[192,1024]{1,0:T(8,128)(2,1)}, bf16[192,1024]{1,0:T(8,128)(2,1)S(1)}, u32[]{:S(2)}, u32[]{:S(2)}) collective-permute-start(bf16[192,1024]{1,0:T(8,128)(2,1)} %get-tuple-element.30), channel_id=1, source_target_pairs={{0,2},{1,3},{2,4},{3,5},{4,6},{5,7},{6,0},{7,1},{8,10},{9,11},{10,... | collective-permute-start | bytes 1179656 | tf_op jit(solution)/shard_map/route/ppermute | solution.py:298
  20.6 19.8 %collective-permute-start.2 = (bf16[192,1024]{1,0:T(8,128)(2,1)}, bf16[192,1024]{1,0:T(8,128)(2,1)S(1)}, u32[]{:S(2)}, u32[]{:S(2)}) collective-permute-start(bf16[192,1024]{1,0:T(8,128)(2,1)} %get-tuple-element.31), channel_id=1, source_target_pairs={{0,3},{1,2},{2,5},{3,4},{4,7},{5,6},{6,1},{7,0},{8,11},{9,10},{10,... | collective-permute-start | bytes 1179656 | tf_op jit(solution)/shard_map/route/ppermute | solution.py:298
  22.1 18.3 %collective-permute-start.3 = (bf16[192,1024]{1,0:T(8,128)(2,1)}, bf16[192,1024]{1,0:T(8,128)(2,1)S(1)}, u32[]{:S(2)}, u32[]{:S(2)}) collective-permute-start(bf16[192,1024]{1,0:T(8,128)(2,1)} %get-tuple-element.32), channel_id=1, source_target_pairs={{0,6},{1,7},{2,0},{3,1},{4,2},{5,3},{6,4},{7,5},{8,14},{9,15},{10,... | collective-permute-start | bytes 1179656 | tf_op jit(solution)/shard_map/route/ppermute | solution.py:298
  23.6 8.0 %copy-start.20 = (bf16[192,1024]{1,0:T(8,128)(2,1)S(1)}, bf16[192,1024]{1,0:T(8,128)(2,1)}, u32[]{:S(2)}) copy-start(bf16[192,1024]{1,0:T(8,128)(2,1)} %get-tuple-element.38) | copy-start | bytes 1179652
  23.6 4.8 %collective-permute-start.7 = (f32[2,192]{1,0:T(2,128)S(1)}, f32[2,192]{1,0:T(2,128)S(1)}, u32[]{:S(2)}, u32[]{:S(2)}) collective-permute-start(f32[2,192]{1,0:T(2,128)S(1)} %bitcast.27), channel_id=1, source_target_pairs={{0,1},{1,0},{2,3},{3,2},{4,5},{5,4},{6,7},{7,6},{8,9},{9,8},{10,11... | collective-permute-start | bytes 4616 | tf_op jit(solution)/shard_map/scales/ppermute | solution.py:309
  28.4 14.2 %collective-permute-start.4 = (bf16[192,1024]{1,0:T(8,128)(2,1)}, bf16[192,1024]{1,0:T(8,128)(2,1)S(1)}, u32[]{:S(2)}, u32[]{:S(2)}) collective-permute-start(bf16[192,1024]{1,0:T(8,128)(2,1)} %get-tuple-element.33), channel_id=1, source_target_pairs={{0,7},{1,6},{2,1},{3,0},{4,3},{5,2},{6,5},{7,4},{8,15},{9,14},{10,... | collective-permute-start | bytes 1179656 | tf_op jit(solution)/shard_map/route/ppermute | solution.py:298
  28.7 20.9 %collective-permute-start.5 = (bf16[192,1024]{1,0:T(8,128)(2,1)}, bf16[192,1024]{1,0:T(8,128)(2,1)S(1)}, u32[]{:S(2)}, u32[]{:S(2)}) collective-permute-start(bf16[192,1024]{1,0:T(8,128)(2,1)} %get-tuple-element.34), channel_id=1, source_target_pairs={{0,4},{1,5},{2,6},{3,7},{4,0},{5,1},{6,2},{7,3},{8,12},{9,13},{10,... | collective-permute-start | bytes 1179656 | tf_op jit(solution)/shard_map/route/ppermute | solution.py:298
  31.6 26.5 %collective-permute-start.6 = (bf16[192,1024]{1,0:T(8,128)(2,1)S(1)}, bf16[192,1024]{1,0:T(8,128)(2,1)S(1)}, u32[]{:S(2)}, u32[]{:S(2)}) collective-permute-start(bf16[192,1024]{1,0:T(8,128)(2,1)S(1)} %copy-done.20), channel_id=1, source_target_pairs={{0,5},{1,4},{2,7},{3,6},{4,1},{5,0},{6,3},{7,2},{8,13},{9,12},{10,... | collective-permute-start | bytes 1179656 | tf_op jit(solution)/shard_map/route/ppermute | solution.py:298
  40.4 40.3 %collective-permute-start.10 = (bf16[1,192,4096]{2,1,0:T(8,128)(2,1)}, bf16[1,192,4096]{2,1,0:T(8,128)(2,1)}, u32[]{:S(2)}, u32[]{:S(2)}) collective-permute-start(bf16[1,192,4096]{2,1,0:T(8,128)(2,1)} %get-tuple-element.37), channel_id=1, source_target_pairs={{0,1},{1,0},{2,3},{3,2},{4,5},{5,4},{6,7},{7,6},{8,9},{9,8},{10,11... | collective-permute-start | bytes 4718600 | tf_op jit(solution)/shard_map/swap/ppermute | solution.py:331
  40.5 40.3 %collective-permute-start.11 = (bf16[1,192,4096]{2,1,0:T(8,128)(2,1)}, bf16[1,192,4096]{2,1,0:T(8,128)(2,1)}, u32[]{:S(2)}, u32[]{:S(2)}) collective-permute-start(bf16[1,192,4096]{2,1,0:T(8,128)(2,1)} %get-tuple-element.41), channel_id=1, source_target_pairs={{0,1},{1,0},{2,3},{3,2},{4,5},{5,4},{6,7},{7,6},{8,9},{9,8},{10,11... | collective-permute-start | bytes 4718600 | tf_op jit(solution)/shard_map/swap/ppermute | solution.py:331
  42.6 68.4 %copy-start = (bf16[192,1024]{1,0:T(8,128)(2,1)}, bf16[192,1024]{1,0:T(8,128)(2,1)S(1)}, u32[]{:S(2)}) copy-start(bf16[192,1024]{1,0:T(8,128)(2,1)S(1)} %collective-permute-done.4.refs_9_.refs_6_) | copy-start | bytes 1179652
  49.6 0.7 copy-start.2
  58.1 0.8 copy-start.5
  61.8 15.9 %collective-permute-start.8 = (bf16[256,1024]{1,0:T(8,128)(2,1)}, bf16[256,1024]{1,0:T(8,128)(2,1)}, u32[]{:S(2)}, u32[]{:S(2)}) collective-permute-start(bf16[256,1024]{1,0:T(8,128)(2,1)} %get-tuple-element.40.refs_0_), channel_id=1, source_target_pairs={{0,2},{2,4},{4,6},{6,0},{1,3},{3,5},{5,7},{7,1},{8,10},{10,12},{12... | collective-permute-start | bytes 1572872 | tf_op jit(solution)/shard_map/rows/ppermute | solution.py:321
  63.9 13.8 %collective-permute-start.12 = (bf16[256,1024]{1,0:T(8,128)(2,1)}, bf16[256,1024]{1,0:T(8,128)(2,1)}, u32[]{:S(2)}, u32[]{:S(2)}) collective-permute-start(bf16[256,1024]{1,0:T(8,128)(2,1)} %get-tuple-element.40.refs_0_), channel_id=1, source_target_pairs={{0,6},{2,0},{4,2},{6,4},{1,7},{3,1},{5,3},{7,5},{8,14},{10,8},{12,... | collective-permute-start | bytes 1572872 | tf_op jit(solution)/shard_map/rows/ppermute | solution.py:321
  77.7 23.8 %collective-permute-start.16 = (bf16[384,1024]{1,0:T(8,128)(2,1)}, bf16[384,1024]{1,0:T(8,128)(2,1)}, u32[]{:S(2)}, u32[]{:S(2)}) collective-permute-start(bf16[384,1024]{1,0:T(8,128)(2,1)} %get-tuple-element.47.refs_0_), channel_id=1, source_target_pairs={{0,6},{2,0},{4,2},{6,4},{1,7},{3,1},{5,3},{7,5},{8,14},{10,8},{12,... | collective-permute-start | bytes 2359304 | tf_op jit(solution)/shard_map/rows/ppermute | solution.py:321
  80.7 14.3 %collective-permute-start.9 = (bf16[256,1024]{1,0:T(8,128)(2,1)}, bf16[256,1024]{1,0:T(8,128)(2,1)}, u32[]{:S(2)}, u32[]{:S(2)}) collective-permute-start(bf16[256,1024]{1,0:T(8,128)(2,1)} %collective-permute-done.8.refs_1_), channel_id=1, source_target_pairs={{0,2},{2,4},{4,6},{6,0},{1,3},{3,5},{5,7},{7,1},{8,10},{10,12},{12... | collective-permute-start | bytes 1572872 | tf_op jit(solution)/shard_map/rows/ppermute | solution.py:321
  86.9 17.2 %copy-start.17 = (f32[2,4096]{1,0:T(2,128)S(1)}, f32[2,4096]{1,0:T(2,128)}, u32[]{:S(2)}) copy-start(f32[2,4096]{1,0:T(2,128)} %param.19) | copy-start | bytes 98308
  98.8 11.0 %collective-permute-start.15 = (bf16[256,384]{1,0:T(8,128)(2,1)}, bf16[256,384]{1,0:T(8,128)(2,1)S(1)}, u32[]{:S(2)}, u32[]{:S(2)}) collective-permute-start(bf16[256,384]{1,0:T(8,128)(2,1)} %up.5.refs_0_), channel_id=1, source_target_pairs={{0,4},{2,6},{4,0},{6,2},{1,5},{3,7},{5,1},{7,3},{8,12},{10,14},{12... | collective-permute-start | bytes 589832 | tf_op jit(solution)/shard_map/down/ppermute | solution.py:321
  98.8 12.2 %collective-permute-start.13 = (bf16[256,384]{1,0:T(8,128)(2,1)}, bf16[256,384]{1,0:T(8,128)(2,1)}, u32[]{:S(2)}, u32[]{:S(2)}) collective-permute-start(bf16[256,384]{1,0:T(8,128)(2,1)} %up.5.refs_0_), channel_id=1, source_target_pairs={{0,2},{2,4},{4,6},{6,0},{1,3},{3,5},{5,7},{7,1},{8,10},{10,12},{12... | collective-permute-start | bytes 589832 | tf_op jit(solution)/shard_map/down/ppermute | solution.py:321
  98.8 12.2 %collective-permute-start.14 = (bf16[256,384]{1,0:T(8,128)(2,1)}, bf16[256,384]{1,0:T(8,128)(2,1)}, u32[]{:S(2)}, u32[]{:S(2)}) collective-permute-start(bf16[256,384]{1,0:T(8,128)(2,1)} %up.5.refs_0_), channel_id=1, source_target_pairs={{0,6},{2,0},{4,2},{6,4},{1,7},{3,1},{5,3},{7,5},{8,14},{10,8},{12,... | collective-permute-start | bytes 589832 | tf_op jit(solution)/shard_map/down/ppermute | solution.py:321
  101.5 26.4 %collective-permute-start.17 = (bf16[384,1024]{1,0:T(8,128)(2,1)}, bf16[384,1024]{1,0:T(8,128)(2,1)}, u32[]{:S(2)}, u32[]{:S(2)}) collective-permute-start(bf16[384,1024]{1,0:T(8,128)(2,1)} %get-tuple-element.47.refs_0_), channel_id=1, source_target_pairs={{0,2},{2,4},{4,6},{6,0},{1,3},{3,5},{5,7},{7,1},{8,10},{10,12},{12... | collective-permute-start | bytes 2359304 | tf_op jit(solution)/shard_map/rows/ppermute | solution.py:321
  101.5 26.4 %collective-permute-start.18 = (bf16[384,1024]{1,0:T(8,128)(2,1)}, bf16[384,1024]{1,0:T(8,128)(2,1)}, u32[]{:S(2)}, u32[]{:S(2)}) collective-permute-start(bf16[384,1024]{1,0:T(8,128)(2,1)} %collective-permute-done.16.refs_1_), channel_id=1, source_target_pairs={{0,6},{2,0},{4,2},{6,4},{1,7},{3,1},{5,3},{7,5},{8,14},{10,8},{12,... | collective-permute-start | bytes 2359304 | tf_op jit(solution)/shard_map/rows/ppermute | solution.py:321
  104.2 6.8 %copy-start.11 = (bf16[256,384]{1,0:T(8,128)(2,1)S(1)}, bf16[256,384]{1,0:T(8,128)(2,1)}, u32[]{:S(2)}) copy-start(bf16[256,384]{1,0:T(8,128)(2,1)} %up.5.refs_0_) | copy-start | bytes 589828
  104.2 6.8 %copy-start.13 = (s32[2]{0:T(128)S(1)}, s32[2]{0:T(128)}, u32[]{:S(2)}) copy-start(s32[2]{0:T(128)} %pad_add_fusion.place_ref) | copy-start | bytes 28
  111.0 1.0 copy-start.3
  112.0 1.0 copy-start.6
  113.0 1.0 copy-start.8
  117.8 32.4 %all-to-all-start.1 = ((bf16[32,8,1024]{2,1,0:T(8,128)(2,1)}), bf16[32,8,1024]{2,1,0:T(8,128)(2,1)S(1)}, u32[]{:S(2)}, u32[]{:S(2)}) async-start(bf16[32,8,1024]{2,1,0:T(8,128)(2,1)} %bitcast.9), calls=%async_computation.1 | async-start | bytes 1048576 | tf_op jit(solution)/shard_map/down/all_to_all | solution.py:301
  127.9 19.2 %copy-start.12 = (bf16[256,128]{1,0:T(8,128)(2,1)S(1)}, bf16[256,128]{1,0:T(8,128)(2,1)}, u32[]{:S(2)}) copy-start(bf16[256,128]{1,0:T(8,128)(2,1)} %get-tuple-element.48.refs_11_) | copy-start | bytes 196612
  127.9 19.2 %copy-start.14 = (s32[2]{0:T(128)S(1)}, s32[2]{0:T(128)}, u32[]{:S(2)}) copy-start(s32[2]{0:T(128)} %pad_add_fusion.place_ref) | copy-start | bytes 28
  133.6 13.5 %copy-start.1 = (bf16[192,1024]{1,0:T(8,128)(2,1)S(1)}, bf16[192,1024]{1,0:T(8,128)(2,1)}, u32[]{:S(2)}) copy-start(bf16[192,1024]{1,0:T(8,128)(2,1)} %copy-done) | copy-start | bytes 1179652
  133.6 13.5 %copy-start.4 = (bf16[192,1024]{1,0:T(8,128)(2,1)S(1)}, bf16[192,1024]{1,0:T(8,128)(2,1)}, u32[]{:S(2)}) copy-start(bf16[192,1024]{1,0:T(8,128)(2,1)} %copy-done.2) | copy-start | bytes 1179652
  133.6 13.5 %copy-start.7 = (bf16[192,1024]{1,0:T(8,128)(2,1)S(1)}, bf16[192,1024]{1,0:T(8,128)(2,1)}, u32[]{:S(2)}) copy-start(bf16[192,1024]{1,0:T(8,128)(2,1)} %copy-done.5) | copy-start | bytes 1179652
  133.6 10.5 %collective-permute-start.19 = (bf16[384,384]{1,0:T(8,128)(2,1)}, bf16[384,384]{1,0:T(8,128)(2,1)S(1)}, u32[]{:S(2)}, u32[]{:S(2)}) collective-permute-start(bf16[384,384]{1,0:T(8,128)(2,1)} %up.7.h_ref), channel_id=1, source_target_pairs={{0,2},{2,4},{4,6},{6,0},{1,3},{3,5},{5,7},{7,1},{8,10},{10,12},{12... | collective-permute-start | bytes 884744 | tf_op jit(solution)/shard_map/down/ppermute | solution.py:321
  133.7 10.4 %collective-permute-start.20 = (bf16[384,384]{1,0:T(8,128)(2,1)}, bf16[384,384]{1,0:T(8,128)(2,1)S(1)}, u32[]{:S(2)}, u32[]{:S(2)}) collective-permute-start(bf16[384,384]{1,0:T(8,128)(2,1)} %up.7.h_ref), channel_id=1, source_target_pairs={{0,6},{2,0},{4,2},{6,4},{1,7},{3,1},{5,3},{7,5},{8,14},{10,8},{12,... | collective-permute-start | bytes 884744 | tf_op jit(solution)/shard_map/down/ppermute | solution.py:321
  136.3 10.7 %collective-permute-start.21 = (bf16[384,384]{1,0:T(8,128)(2,1)}, bf16[384,384]{1,0:T(8,128)(2,1)S(1)}, u32[]{:S(2)}, u32[]{:S(2)}) collective-permute-start(bf16[384,384]{1,0:T(8,128)(2,1)} %up.7.h_ref), channel_id=1, source_target_pairs={{0,4},{2,6},{4,0},{6,2},{1,5},{3,7},{5,1},{7,3},{8,12},{10,14},{12... | collective-permute-start | bytes 884744 | tf_op jit(solution)/shard_map/down/ppermute | solution.py:321
  136.4 1.0 copy-start.9
  137.3 1.0 copy-start.10
  150.2 9.6 %copy-start.15 = (s32[128,8]{0,1:T(8,128)S(1)}, s32[128,8]{0,1:T(8,128)}, u32[]{:S(2)}) copy-start(s32[128,8]{0,1:T(8,128)} %param.12) | copy-start | bytes 12292
  150.2 9.6 %copy-start.16 = (f32[128,8]{0,1:T(8,128)S(1)}, f32[128,8]{0,1:T(8,128)}, u32[]{:S(2)}) copy-start(f32[128,8]{0,1:T(8,128)} %param.13) | copy-start | bytes 12292
  150.2 28.4 %all-to-all-start.2 = ((bf16[32,8,1664]{2,1,0:T(8,128)(2,1)}), bf16[32,8,1664]{2,1,0:T(8,128)(2,1)S(1)}, u32[]{:S(2)}, u32[]{:S(2)}) async-start(bf16[32,8,1664]{2,1,0:T(8,128)(2,1)} %bitcast.11), calls=%async_computation.2 | async-start | bytes 1703936 | tf_op jit(solution)/shard_map/down/all_to_all | solution.py:301
  180.3 7.5 %collective-permute-start.22 = (f32[128,512]{1,0:T(8,128)S(1)}, f32[128,512]{1,0:T(8,128)S(1)}, u32[]{:S(2)}, u32[]{:S(2)}) collective-permute-start(f32[128,512]{1,0:T(8,128)S(1)} %get-tuple-element.50), channel_id=1, source_target_pairs={{0,1},{1,0},{2,3},{3,2},{4,5},{5,4},{6,7},{7,6},{8,9},{9,8},{10,11... | collective-permute-start | bytes 786440 | tf_op jit(solution)/shard_map/combine/ppermute | solution.py:459

commit v4 on v3

--- a/solution.py
+++ b/solution.py
@@ -406,7 +406,6 @@
             [whole(r, units)] * 4 + [whole(hid, quarter)] * 8 + [channel],
             whole(r, quarter),
             sds(r, quarter),
-            params=SMALL,
         )(place, h_p, *near, *wd, down_scale)
         back_p = exchange(v_p)
 

time: 189 us -> 188 us (level)
  local copies, waits for them, and re-layouts: 6.52 us -> 3.11 us
  Pallas kernels: 44.6 us -> 46.8 us
    unnamed x44 -> x48, local copies, waits for them, and re-layouts: 6.5 us -> 2.47 us
  transfers between devices with their start and end apart: 26 -> 26, of which waited for: 14 -> 13; matrix products, arithmetic and copies ran while one was open for 0% -> 1% of each run, Pallas kernels for 20% -> 21%
where the time goes in v4:
time: 188 us; the launch traced here: 187 us
  waiting for transfers between devices  72.6 us (39%)
  starting transfers between devices  61.9 us (33%)
  Pallas kernels  46.8 us (25%)
  local copies, waits for them, and re-layouts  3.11 us (2%)
  other arithmetic  1.93 us (1%)
    all_to_all x3, starting transfers between devices, exchange(): lax.all_to_all(v.reshape(n_dp, ROWS, v.shape[-1]), DP, 0, 0, tiled=True)  31 us
    ppermute x12, waiting for transfers between devices, shift(): return lax.ppermute(v, 'y', [(i, (i + by) % n_y) for i in range(n_y)])  29.9 us
    ppermute x7, waiting for transfers between devices, on_device(): wd.append(lax.ppermute(v, ('y', 'core'), pairs))  24 us
    all_to_all x3, waiting for transfers between devices, exchange(): lax.all_to_all(v.reshape(n_dp, ROWS, v.shape[-1]), DP, 0, 0, tiled=True)  17.6 us
    ppermute x12, starting transfers between devices, shift(): return lax.ppermute(v, 'y', [(i, (i + by) % n_y) for i in range(n_y)])  13.6 us
    ppermute x7, starting transfers between devices, on_device(): wd.append(lax.ppermute(v, ('y', 'core'), pairs))  9.89 us
    ppermute x1, starting transfers between devices, on_device(): moe_out = (keep + lax.ppermute(send, 'core', [(0, 1), (1, 0)])).astype(BF)  6.37 us
    pallas_call x1, Pallas kernels, on_device(): call(up_first_kernel, 3, [whole(r, quarter)] * 3 + weight_specs(0, 3, 1),...  6.17 us
  transfers between devices with their start and end apart: 26, of which 13 were waited for; matrix products, arithmetic and copies ran while one was open for 1% of the time, Pallas kernels for 21%

profile of v4, /device:TPU:1, one launch (start us, length us, event | category | flops | bytes accessed | tf_op | source)
XLA Modules:
  0.0 187.4 jit_solution(2739114825550245709)
XLA Ops:
  0.6 0.6 pad_add_fusion.place_ref
  1.2 5.0 %route.2 = (bf16[256,2688]{1,0:T(8,128)(2,1)}, bf16[192,1024]{1,0:T(8,128)(2,1)}, bf16[192,1024]{1,0:T(8,128)(2,1)}, bf16[192,1024]{1,0:T(8,128)(2,1)}, bf16[192...) custom-call(s32[2]{0:T(128)} %pad_add_fusion.place_ref, ...), custom_call_target="tpu_custom_call" | custom-call | flops 1000 | bytes 1000 | tf_op jit(solution)/shard_map/route/pallas_call | solution.py:271
  6.2 12.0 %all-to-all-start = ((bf16[32,8,2688]{2,1,0:T(8,128)(2,1)}), bf16[32,8,2688]{2,1,0:T(8,128)(2,1)}, u32[]{:S(2)}, u32[]{:S(2)}) async-start(bf16[32,8,2688]{2,1,0:T(8,128)(2,1)} %bitcast.26), calls=%async_computation | async-start | bytes 2752512 | tf_op jit(solution)/shard_map/dispatch/all_to_all | solution.py:301
  18.2 1.0 collective-permute-start
  19.3 1.3 collective-permute-start.1
  20.6 1.5 collective-permute-start.2
  22.1 1.4 collective-permute-start.3
  24.1 4.2 %route.3 = (bf16[1,192,4096]{2,1,0:T(8,128)(2,1)}, bf16[1,192,4096]{2,1,0:T(8,128)(2,1)}) custom-call(s32[2]{0:T(128)} %pad_add_fusion.place_ref, bf16[2,192,4096]{2,1,0:T(8,128)(2,1)} %refs_2_.3, bf16[2,192,4096]{2,1,0:T(8,128)(2,1)} %refs_4_.3), custom_call_target="tpu_custom_call" | custom-call | flops 1000 | bytes 1000 | tf_op jit(solution)/shard_map/route/pallas_call | solution.py:280
  28.7 1.5 collective-permute-start.5
  30.2 1.3 collective-permute-done.1.refs_6_.refs_3_
  31.6 2.7 %collective-permute-start.6 = (bf16[192,1024]{1,0:T(8,128)(2,1)S(1)}, bf16[192,1024]{1,0:T(8,128)(2,1)}, u32[]{:S(2)}, u32[]{:S(2)}) collective-permute-start(bf16[192,1024]{1,0:T(8,128)(2,1)S(1)} %copy-done.22), channel_id=1, source_target_pairs={{0,5},{1,4},{2,7},{3,6},{4,1},{5,0},{6,3},{7,2},{8,13},{9,12},{10,... | collective-permute-start | bytes 1179656 | tf_op jit(solution)/shard_map/route/ppermute | solution.py:298
  34.3 6.1 %collective-permute-done.2.refs_7_.refs_4_ = bf16[192,1024]{1,0:T(8,128)(2,1)S(1)} collective-permute-done((bf16[192,1024]{1,0:T(8,128)(2,1)}, bf16[192,1024]{1,0:T(8,128)(2,1)S(1)}, u32[]{:S(2)}, u32[]{:S(2)}) %collective-permute-start.2) | collective-permute-done | bytes 393248 | tf_op jit(solution)/shard_map/route/ppermute | solution.py:298
  40.9 0.7 pad_maximum_fusion.refs_6_.refs_7_
  41.6 1.0 collective-permute-done.4.refs_9_.refs_6_
  42.6 7.0 %collective-permute-done.5.refs_10_.refs_7_ = bf16[192,1024]{1,0:T(8,128)(2,1)} collective-permute-done((bf16[192,1024]{1,0:T(8,128)(2,1)}, bf16[192,1024]{1,0:T(8,128)(2,1)}, u32[]{:S(2)}, u32[]{:S(2)}) %collective-permute-start.5) | collective-permute-done | bytes 393248 | tf_op jit(solution)/shard_map/route/ppermute | solution.py:298
  49.6 8.6 %collective-permute-done.6.refs_11_.refs_8_ = bf16[192,1024]{1,0:T(8,128)(2,1)} collective-permute-done((bf16[192,1024]{1,0:T(8,128)(2,1)S(1)}, bf16[192,1024]{1,0:T(8,128)(2,1)}, u32[]{:S(2)}, u32[]{:S(2)}) %collective-permute-start.6) | collective-permute-done | bytes 393248 | tf_op jit(solution)/shard_map/route/ppermute | solution.py:298
  58.2 2.9 %unpack.1 = (bf16[256,1024]{1,0:T(8,128)(2,1)}, bf16[384,1024]{1,0:T(8,128)(2,1)}, bf16[256,128]{1,0:T(8,128)(2,1)}) custom-call(bf16[256,2688]{1,0:T(8,128)(2,1)} %bitcast.5.in_ref, s32[1,128]{1,0:T(1,128)} %bitcast.31), custom_call_target="tpu_custom_call" | custom-call | flops 1000 | bytes 1000 | tf_op jit(solution)/shard_map/unpack/pallas_call | solution.py:313
  61.0 1.4 collective-permute-start.8
  62.5 1.6 collective-permute-start.12
  64.1 12.5 %collective-permute-done.8.refs_1_ = bf16[256,1024]{1,0:T(8,128)(2,1)} collective-permute-done((bf16[256,1024]{1,0:T(8,128)(2,1)}, bf16[256,1024]{1,0:T(8,128)(2,1)}, u32[]{:S(2)}, u32[]{:S(2)}) %collective-permute-start.8) | collective-permute-done | bytes 524320 | tf_op jit(solution)/shard_map/rows/ppermute | solution.py:321
  76.5 2.4 %collective-permute-start.16 = (bf16[384,1024]{1,0:T(8,128)(2,1)}, bf16[384,1024]{1,0:T(8,128)(2,1)}, u32[]{:S(2)}, u32[]{:S(2)}) collective-permute-start(bf16[384,1024]{1,0:T(8,128)(2,1)} %get-tuple-element.47.refs_0_), channel_id=1, source_target_pairs={{0,6},{2,0},{4,2},{6,4},{1,7},{3,1},{5,3},{7,5},{8,14},{10,8},{12,... | collective-permute-start | bytes 2359304 | tf_op jit(solution)/shard_map/rows/ppermute | solution.py:321
  79.0 6.2 %up.4.refs_5_ = f32[256,768]{1,0:T(8,128)} custom-call(s32[2]{0:T(128)} %pad_add_fusion.place_ref, bf16[256,1024]{1,0:T(8,128)(2,1)} %get-tuple-element.40.refs_0_, bf16[256,1024]{1,0:T(8,128)(2,1)} %collective-permute-done.8.refs_1_, bf16[256,1024]{1,0:T(8,128)(2,1)} %collective-permute-done.12.refs_2_, bf16[2,192,4096]{2,1,0:T(8,128)(2,1)} %refs_2_.3, ...), custom_call_target="tpu_custom_call" | custom-call | flops 1000 | bytes 1000 | tf_op jit(solution)/shard_map/up/pallas_call | solution.py:374
  85.2 7.5 %collective-permute-done.9.refs_0_ = bf16[256,1024]{1,0:T(8,128)(2,1)} collective-permute-done((bf16[256,1024]{1,0:T(8,128)(2,1)}, bf16[256,1024]{1,0:T(8,128)(2,1)}, u32[]{:S(2)}, u32[]{:S(2)}) %collective-permute-start.9) | collective-permute-done | bytes 524320 | tf_op jit(solution)/shard_map/rows/ppermute | solution.py:321
  92.7 3.9 %up.5.refs_0_ = bf16[256,384]{1,0:T(8,128)(2,1)} custom-call(s32[2]{0:T(128)} %pad_add_fusion.place_ref, bf16[256,1024]{1,0:T(8,128)(2,1)} %collective-permute-done.9.refs_0_, bf16[2,192,4096]{2,1,0:T(8,128)(2,1)} %refs_2_.3, bf16[1,192,4096]{2,1,0:T(8,128)(2,1)} %collective-permute-done.10.refs_4_.refs_2_.refs_3_, bf16[2,192,4096]{2,1,0:T(8,128)(2,1)} %refs_4_.3, ...), custom_call_target="tpu_custom_call" | custom-call | flops 1000 | bytes 1000 | tf_op jit(solution)/shard_map/up/pallas_call | solution.py:381
  96.6 2.7 %collective-permute-start.14 = (bf16[256,384]{1,0:T(8,128)(2,1)}, bf16[256,384]{1,0:T(8,128)(2,1)S(1)}, u32[]{:S(2)}, u32[]{:S(2)}) collective-permute-start(bf16[256,384]{1,0:T(8,128)(2,1)} %up.5.refs_0_), channel_id=1, source_target_pairs={{0,6},{2,0},{4,2},{6,4},{1,7},{3,1},{5,3},{7,5},{8,14},{10,8},{12,... | collective-permute-start | bytes 589832 | tf_op jit(solution)/shard_map/down/ppermute | solution.py:321
  99.2 2.7 %collective-permute-start.18 = (bf16[384,1024]{1,0:T(8,128)(2,1)}, bf16[384,1024]{1,0:T(8,128)(2,1)}, u32[]{:S(2)}, u32[]{:S(2)}) collective-permute-start(bf16[384,1024]{1,0:T(8,128)(2,1)} %collective-permute-done.16.refs_1_), channel_id=1, source_target_pairs={{0,6},{2,0},{4,2},{6,4},{1,7},{3,1},{5,3},{7,5},{8,14},{10,8},{12,... | collective-permute-start | bytes 2359304 | tf_op jit(solution)/shard_map/rows/ppermute | solution.py:321
  101.9 0.6 reshape.34.refs_12_.refs_10_
  102.6 5.4 %up.6.refs_6_ = f32[384,768]{1,0:T(8,128)} custom-call(s32[2]{0:T(128)} %pad_add_fusion.place_ref, bf16[384,1024]{1,0:T(8,128)(2,1)} %get-tuple-element.47.refs_0_, bf16[384,1024]{1,0:T(8,128)(2,1)} %collective-permute-done.16.refs_1_, bf16[2,192,4096]{2,1,0:T(8,128)(2,1)} %refs_2_.3, bf16[1,192,4096]{2,1,0:T(8,128)(2,1)} %collective-permute-done.10.refs_4_.refs_2_.refs_3_, ...), custom_call_target="tpu_custom_call" | custom-call | flops 1000 | bytes 1000 | tf_op jit(solution)/shard_map/up/pallas_call | solution.py:392
  108.0 0.6 collective-permute-done.13.refs_1_
  108.6 0.6 copy-done.17
  109.2 0.7 copy-done.18
  109.9 4.9 %down.3 = bf16[256,1024]{1,0:T(8,128)(2,1)} custom-call(s32[2]{0:T(128)} %pad_add_fusion.place_ref, bf16[256,384]{1,0:T(8,128)(2,1)} %up.5.refs_0_, bf16[256,384]{1,0:T(8,128)(2,1)} %copy-done.17, bf16[256,384]{1,0:T(8,128)(2,1)} %copy-done.18, bf16[256,384]{1,0:T(8,128)(2,1)} %copy-done.16, bf16[192,1024]{1,0:T(8,128)(2,1)} %get-tuple-element.28.refs_4_.same_ref, ...), custom_call_target="tpu_custom_call" | custom-call | flops 1000 | bytes 1000 | tf_op jit(solution)/shard_map/down/pallas_call | solution.py:403
  114.8 9.5 %all-to-all-start.1 = ((bf16[32,8,1024]{2,1,0:T(8,128)(2,1)}), bf16[32,8,1024]{2,1,0:T(8,128)(2,1)S(1)}, u32[]{:S(2)}, u32[]{:S(2)}) async-start(bf16[32,8,1024]{2,1,0:T(8,128)(2,1)} %bitcast.25), calls=%async_computation.1 | async-start | bytes 1048576 | tf_op jit(solution)/shard_map/down/all_to_all | solution.py:301
  124.3 1.2 collective-permute-done.17.refs_0_
  125.5 5.7 %up.7.h_ref = bf16[384,384]{1,0:T(8,128)(2,1)} custom-call(s32[2]{0:T(128)} %pad_add_fusion.place_ref, bf16[384,1024]{1,0:T(8,128)(2,1)} %collective-permute-done.17.refs_0_, bf16[384,1024]{1,0:T(8,128)(2,1)} %collective-permute-done.18.refs_1_, bf16[2,192,4096]{2,1,0:T(8,128)(2,1)} %refs_2_.3, ...), custom_call_target="tpu_custom_call" | custom-call | flops 1000 | bytes 1000 | tf_op jit(solution)/shard_map/up/pallas_call | solution.py:414
  131.3 2.7 %collective-permute-start.20 = (bf16[384,384]{1,0:T(8,128)(2,1)}, bf16[384,384]{1,0:T(8,128)(2,1)S(1)}, u32[]{:S(2)}, u32[]{:S(2)}) collective-permute-start(bf16[384,384]{1,0:T(8,128)(2,1)} %up.7.h_ref), channel_id=1, source_target_pairs={{0,6},{2,0},{4,2},{6,4},{1,7},{3,1},{5,3},{7,5},{8,14},{10,8},{12,... | collective-permute-start | bytes 884744 | tf_op jit(solution)/shard_map/down/ppermute | solution.py:321
  134.0 1.0 copy-done.9
  135.0 1.6 down.4.refs_9_
  136.6 3.8 %collective-permute-done.19.refs_0_ = bf16[384,384]{1,0:T(8,128)(2,1)S(1)} collective-permute-done((bf16[384,384]{1,0:T(8,128)(2,1)}, bf16[384,384]{1,0:T(8,128)(2,1)S(1)}, u32[]{:S(2)}, u32[]{:S(2)}) %collective-permute-start.19) | collective-permute-done | bytes 294944 | tf_op jit(solution)/shard_map/down/ppermute | solution.py:321
  140.3 4.3 %collective-permute-done.21.refs_2_ = bf16[384,384]{1,0:T(8,128)(2,1)S(1)} collective-permute-done((bf16[384,384]{1,0:T(8,128)(2,1)}, bf16[384,384]{1,0:T(8,128)(2,1)S(1)}, u32[]{:S(2)}, u32[]{:S(2)}) %collective-permute-start.21) | collective-permute-done | bytes 294944 | tf_op jit(solution)/shard_map/down/ppermute | solution.py:321
  144.7 4.3 %down.5 = bf16[256,1664]{1,0:T(8,128)(2,1)} custom-call(s32[2]{0:T(128)S(1)} %copy-done.12, bf16[384,384]{1,0:T(8,128)(2,1)S(1)} %collective-permute-done.19.refs_0_, bf16[384,384]{1,0:T(8,128)(2,1)S(1)} %collective-permute-done.20.refs_1_, bf16[384,384]{1,0:T(8,128)(2,1)S(1)} %collective-permute-done.21.refs_2_, bf16[192,1024]{1,0:T(8,128)(2,1)S(1)} %copy-done.1, ...), custom_call_target="tpu_custom_call" | custom-call | flops 1000 | bytes 1000 | tf_op jit(solution)/shard_map/down/pallas_call | solution.py:431
  149.0 9.6 %all-to-all-start.2 = ((bf16[32,8,1664]{2,1,0:T(8,128)(2,1)}), bf16[32,8,1664]{2,1,0:T(8,128)(2,1)S(1)}, u32[]{:S(2)}, u32[]{:S(2)}) async-start(bf16[32,8,1664]{2,1,0:T(8,128)(2,1)} %bitcast.11), calls=%async_computation.2 | async-start | bytes 1703936 | tf_op jit(solution)/shard_map/down/all_to_all | solution.py:301
  158.6 1.3 combine.2
  159.9 17.6 %all-to-all-done.2 = bf16[32,8,1664]{2,1,0:T(8,128)(2,1)S(1)} async-done(((bf16[32,8,1664]{2,1,0:T(8,128)(2,1)}), bf16[32,8,1664]{2,1,0:T(8,128)(2,1)S(1)}, u32[]{:S(2)}, u32[]{:S(2)}) %all-to-all-start.2) | async-done | bytes 852000 | tf_op jit(solution)/shard_map/down/all_to_all | solution.py:301
  177.5 1.6 combine.3
  179.1 6.4 %collective-permute-start.22 = (f32[128,512]{1,0:T(8,128)S(1)}, f32[128,512]{1,0:T(8,128)S(1)}, u32[]{:S(2)}, u32[]{:S(2)}) collective-permute-start(f32[128,512]{1,0:T(8,128)S(1)} %get-tuple-element.50), channel_id=1, source_target_pairs={{0,1},{1,0},{2,3},{3,2},{4,5},{5,4},{6,7},{7,6},{8,9},{9,8},{10,11... | collective-permute-start | bytes 786440 | tf_op jit(solution)/shard_map/combine/ppermute | solution.py:458
  185.5 1.2 collective-permute-done.22
  186.7 0.7 add_convert_fusion
  (69 shorter events, 1.7 us)
Async XLA Ops:
  6.2 17.3 %copy-start.20 = (f32[2,192]{1,0:T(2,128)S(1)}, f32[2,192]{1,0:T(2,128)}, u32[]{:S(2)}) copy-start(f32[2,192]{1,0:T(2,128)} %param.17) | copy-start | bytes 4612
  6.2 17.3 %copy-start.21 = (f32[2,192]{1,0:T(2,128)S(1)}, f32[2,192]{1,0:T(2,128)}, u32[]{:S(2)}) copy-start(f32[2,192]{1,0:T(2,128)} %param.18) | copy-start | bytes 4612
  6.2 51.9 %all-to-all-start = ((bf16[32,8,2688]{2,1,0:T(8,128)(2,1)}), bf16[32,8,2688]{2,1,0:T(8,128)(2,1)}, u32[]{:S(2)}, u32[]{:S(2)}) async-start(bf16[32,8,2688]{2,1,0:T(8,128)(2,1)} %bitcast.26), calls=%async_computation | async-start | bytes 2752512 | tf_op jit(solution)/shard_map/dispatch/all_to_all | solution.py:301
  18.2 10.5 %collective-permute-start = (bf16[192,1024]{1,0:T(8,128)(2,1)}, bf16[192,1024]{1,0:T(8,128)(2,1)}, u32[]{:S(2)}, u32[]{:S(2)}) collective-permute-start(bf16[192,1024]{1,0:T(8,128)(2,1)} %get-tuple-element.29), channel_id=1, source_target_pairs={{0,1},{1,0},{2,3},{3,2},{4,5},{5,4},{6,7},{7,6},{8,9},{9,8},{10,11... | collective-permute-start | bytes 1179656 | tf_op jit(solution)/shard_map/route/ppermute | solution.py:298
  19.3 12.3 %collective-permute-start.1 = (bf16[192,1024]{1,0:T(8,128)(2,1)}, bf16[192,1024]{1,0:T(8,128)(2,1)S(1)}, u32[]{:S(2)}, u32[]{:S(2)}) collective-permute-start(bf16[192,1024]{1,0:T(8,128)(2,1)} %get-tuple-element.30), channel_id=1, source_target_pairs={{0,2},{1,3},{2,4},{3,5},{4,6},{5,7},{6,0},{7,1},{8,10},{9,11},{10,... | collective-permute-start | bytes 1179656 | tf_op jit(solution)/shard_map/route/ppermute | solution.py:298
  20.6 19.8 %collective-permute-start.2 = (bf16[192,1024]{1,0:T(8,128)(2,1)}, bf16[192,1024]{1,0:T(8,128)(2,1)S(1)}, u32[]{:S(2)}, u32[]{:S(2)}) collective-permute-start(bf16[192,1024]{1,0:T(8,128)(2,1)} %get-tuple-element.31), channel_id=1, source_target_pairs={{0,3},{1,2},{2,5},{3,4},{4,7},{5,6},{6,1},{7,0},{8,11},{9,10},{10,... | collective-permute-start | bytes 1179656 | tf_op jit(solution)/shard_map/route/ppermute | solution.py:298
  22.1 18.3 %collective-permute-start.3 = (bf16[192,1024]{1,0:T(8,128)(2,1)}, bf16[192,1024]{1,0:T(8,128)(2,1)S(1)}, u32[]{:S(2)}, u32[]{:S(2)}) collective-permute-start(bf16[192,1024]{1,0:T(8,128)(2,1)} %get-tuple-element.32), channel_id=1, source_target_pairs={{0,6},{1,7},{2,0},{3,1},{4,2},{5,3},{6,4},{7,5},{8,14},{9,15},{10,... | collective-permute-start | bytes 1179656 | tf_op jit(solution)/shard_map/route/ppermute | solution.py:298
  23.5 8.0 %copy-start.22 = (bf16[192,1024]{1,0:T(8,128)(2,1)S(1)}, bf16[192,1024]{1,0:T(8,128)(2,1)}, u32[]{:S(2)}) copy-start(bf16[192,1024]{1,0:T(8,128)(2,1)} %get-tuple-element.38) | copy-start | bytes 1179652
  23.5 4.8 %collective-permute-start.7 = (f32[2,192]{1,0:T(2,128)S(1)}, f32[2,192]{1,0:T(2,128)S(1)}, u32[]{:S(2)}, u32[]{:S(2)}) collective-permute-start(f32[2,192]{1,0:T(2,128)S(1)} %bitcast.28), channel_id=1, source_target_pairs={{0,1},{1,0},{2,3},{3,2},{4,5},{5,4},{6,7},{7,6},{8,9},{9,8},{10,11... | collective-permute-start | bytes 4616 | tf_op jit(solution)/shard_map/scales/ppermute | solution.py:309
  28.3 14.2 %collective-permute-start.4 = (bf16[192,1024]{1,0:T(8,128)(2,1)}, bf16[192,1024]{1,0:T(8,128)(2,1)S(1)}, u32[]{:S(2)}, u32[]{:S(2)}) collective-permute-start(bf16[192,1024]{1,0:T(8,128)(2,1)} %get-tuple-element.33), channel_id=1, source_target_pairs={{0,7},{1,6},{2,1},{3,0},{4,3},{5,2},{6,5},{7,4},{8,15},{9,14},{10,... | collective-permute-start | bytes 1179656 | tf_op jit(solution)/shard_map/route/ppermute | solution.py:298
  28.7 20.9 %collective-permute-start.5 = (bf16[192,1024]{1,0:T(8,128)(2,1)}, bf16[192,1024]{1,0:T(8,128)(2,1)}, u32[]{:S(2)}, u32[]{:S(2)}) collective-permute-start(bf16[192,1024]{1,0:T(8,128)(2,1)} %get-tuple-element.34), channel_id=1, source_target_pairs={{0,4},{1,5},{2,6},{3,7},{4,0},{5,1},{6,2},{7,3},{8,12},{9,13},{10,... | collective-permute-start | bytes 1179656 | tf_op jit(solution)/shard_map/route/ppermute | solution.py:298
  31.6 53.6 %copy-start = (bf16[192,1024]{1,0:T(8,128)(2,1)}, bf16[192,1024]{1,0:T(8,128)(2,1)S(1)}, u32[]{:S(2)}) copy-start(bf16[192,1024]{1,0:T(8,128)(2,1)S(1)} %collective-permute-done.1.refs_6_.refs_3_) | copy-start | bytes 1179652
  31.6 26.6 %collective-permute-start.6 = (bf16[192,1024]{1,0:T(8,128)(2,1)S(1)}, bf16[192,1024]{1,0:T(8,128)(2,1)}, u32[]{:S(2)}, u32[]{:S(2)}) collective-permute-start(bf16[192,1024]{1,0:T(8,128)(2,1)S(1)} %copy-done.22), channel_id=1, source_target_pairs={{0,5},{1,4},{2,7},{3,6},{4,1},{5,0},{6,3},{7,2},{8,13},{9,12},{10,... | collective-permute-start | bytes 1179656 | tf_op jit(solution)/shard_map/route/ppermute | solution.py:298
  40.4 44.8 %copy-start.2 = (bf16[192,1024]{1,0:T(8,128)(2,1)}, bf16[192,1024]{1,0:T(8,128)(2,1)S(1)}, u32[]{:S(2)}) copy-start(bf16[192,1024]{1,0:T(8,128)(2,1)S(1)} %collective-permute-done.2.refs_7_.refs_4_) | copy-start | bytes 1179652
  40.4 38.6 %collective-permute-start.10 = (bf16[1,192,4096]{2,1,0:T(8,128)(2,1)}, bf16[1,192,4096]{2,1,0:T(8,128)(2,1)}, u32[]{:S(2)}, u32[]{:S(2)}) collective-permute-start(bf16[1,192,4096]{2,1,0:T(8,128)(2,1)} %get-tuple-element.37), channel_id=1, source_target_pairs={{0,1},{1,0},{2,3},{3,2},{4,5},{5,4},{6,7},{7,6},{8,9},{9,8},{10,11... | collective-permute-start | bytes 4718600 | tf_op jit(solution)/shard_map/swap/ppermute | solution.py:331
  40.4 44.8 %copy-start.4 = (bf16[192,1024]{1,0:T(8,128)(2,1)}, bf16[192,1024]{1,0:T(8,128)(2,1)S(1)}, u32[]{:S(2)}) copy-start(bf16[192,1024]{1,0:T(8,128)(2,1)S(1)} %collective-permute-done.3.refs_8_.refs_5_) | copy-start | bytes 1179652
  40.4 38.6 %collective-permute-start.11 = (bf16[1,192,4096]{2,1,0:T(8,128)(2,1)}, bf16[1,192,4096]{2,1,0:T(8,128)(2,1)}, u32[]{:S(2)}, u32[]{:S(2)}) collective-permute-start(bf16[1,192,4096]{2,1,0:T(8,128)(2,1)} %get-tuple-element.41), channel_id=1, source_target_pairs={{0,1},{1,0},{2,3},{3,2},{4,5},{5,4},{6,7},{7,6},{8,9},{9,8},{10,11... | collective-permute-start | bytes 4718600 | tf_op jit(solution)/shard_map/swap/ppermute | solution.py:331
  42.6 42.6 %copy-start.6 = (bf16[192,1024]{1,0:T(8,128)(2,1)}, bf16[192,1024]{1,0:T(8,128)(2,1)S(1)}, u32[]{:S(2)}) copy-start(bf16[192,1024]{1,0:T(8,128)(2,1)S(1)} %collective-permute-done.4.refs_9_.refs_6_) | copy-start | bytes 1179652
  61.0 15.5 %collective-permute-start.8 = (bf16[256,1024]{1,0:T(8,128)(2,1)}, bf16[256,1024]{1,0:T(8,128)(2,1)}, u32[]{:S(2)}, u32[]{:S(2)}) collective-permute-start(bf16[256,1024]{1,0:T(8,128)(2,1)} %get-tuple-element.40.refs_0_), channel_id=1, source_target_pairs={{0,2},{2,4},{4,6},{6,0},{1,3},{3,5},{5,7},{7,1},{8,10},{10,12},{12... | collective-permute-start | bytes 1572872 | tf_op jit(solution)/shard_map/rows/ppermute | solution.py:321
  62.5 14.1 %collective-permute-start.12 = (bf16[256,1024]{1,0:T(8,128)(2,1)}, bf16[256,1024]{1,0:T(8,128)(2,1)}, u32[]{:S(2)}, u32[]{:S(2)}) collective-permute-start(bf16[256,1024]{1,0:T(8,128)(2,1)} %get-tuple-element.40.refs_0_), channel_id=1, source_target_pairs={{0,6},{2,0},{4,2},{6,4},{1,7},{3,1},{5,3},{7,5},{8,14},{10,8},{12,... | collective-permute-start | bytes 1572872 | tf_op jit(solution)/shard_map/rows/ppermute | solution.py:321
  76.5 22.7 %collective-permute-start.16 = (bf16[384,1024]{1,0:T(8,128)(2,1)}, bf16[384,1024]{1,0:T(8,128)(2,1)}, u32[]{:S(2)}, u32[]{:S(2)}) collective-permute-start(bf16[384,1024]{1,0:T(8,128)(2,1)} %get-tuple-element.47.refs_0_), channel_id=1, source_target_pairs={{0,6},{2,0},{4,2},{6,4},{1,7},{3,1},{5,3},{7,5},{8,14},{10,8},{12,... | collective-permute-start | bytes 2359304 | tf_op jit(solution)/shard_map/rows/ppermute | solution.py:321
  79.0 13.7 %collective-permute-start.9 = (bf16[256,1024]{1,0:T(8,128)(2,1)}, bf16[256,1024]{1,0:T(8,128)(2,1)}, u32[]{:S(2)}, u32[]{:S(2)}) collective-permute-start(bf16[256,1024]{1,0:T(8,128)(2,1)} %collective-permute-done.8.refs_1_), channel_id=1, source_target_pairs={{0,2},{2,4},{4,6},{6,0},{1,3},{3,5},{5,7},{7,1},{8,10},{10,12},{12... | collective-permute-start | bytes 1572872 | tf_op jit(solution)/shard_map/rows/ppermute | solution.py:321
  85.2 16.7 %copy-start.19 = (f32[2,4096]{1,0:T(2,128)S(1)}, f32[2,4096]{1,0:T(2,128)}, u32[]{:S(2)}) copy-start(f32[2,4096]{1,0:T(2,128)} %param.19) | copy-start | bytes 98308
  92.7 6.5 %copy-start.15 = (bf16[384,1024]{1,0:T(8,128)(2,1)S(1)}, bf16[384,1024]{1,0:T(8,128)(2,1)}, u32[]{:S(2)}) copy-start(bf16[384,1024]{1,0:T(8,128)(2,1)} %get-tuple-element.47.refs_0_) | copy-start | bytes 2359300
  96.6 11.4 %collective-permute-start.15 = (bf16[256,384]{1,0:T(8,128)(2,1)}, bf16[256,384]{1,0:T(8,128)(2,1)S(1)}, u32[]{:S(2)}, u32[]{:S(2)}) collective-permute-start(bf16[256,384]{1,0:T(8,128)(2,1)} %up.5.refs_0_), channel_id=1, source_target_pairs={{0,4},{2,6},{4,0},{6,2},{1,5},{3,7},{5,1},{7,3},{8,12},{10,14},{12... | collective-permute-start | bytes 589832 | tf_op jit(solution)/shard_map/down/ppermute | solution.py:321
  96.6 12.0 %collective-permute-start.13 = (bf16[256,384]{1,0:T(8,128)(2,1)}, bf16[256,384]{1,0:T(8,128)(2,1)S(1)}, u32[]{:S(2)}, u32[]{:S(2)}) collective-permute-start(bf16[256,384]{1,0:T(8,128)(2,1)} %up.5.refs_0_), channel_id=1, source_target_pairs={{0,2},{2,4},{4,6},{6,0},{1,3},{3,5},{5,7},{7,1},{8,10},{10,12},{12... | collective-permute-start | bytes 589832 | tf_op jit(solution)/shard_map/down/ppermute | solution.py:321
  96.6 12.0 %collective-permute-start.14 = (bf16[256,384]{1,0:T(8,128)(2,1)}, bf16[256,384]{1,0:T(8,128)(2,1)S(1)}, u32[]{:S(2)}, u32[]{:S(2)}) collective-permute-start(bf16[256,384]{1,0:T(8,128)(2,1)} %up.5.refs_0_), channel_id=1, source_target_pairs={{0,6},{2,0},{4,2},{6,4},{1,7},{3,1},{5,3},{7,5},{8,14},{10,8},{12,... | collective-permute-start | bytes 589832 | tf_op jit(solution)/shard_map/down/ppermute | solution.py:321
  99.2 26.2 %collective-permute-start.17 = (bf16[384,1024]{1,0:T(8,128)(2,1)S(1)}, bf16[384,1024]{1,0:T(8,128)(2,1)}, u32[]{:S(2)}, u32[]{:S(2)}) collective-permute-start(bf16[384,1024]{1,0:T(8,128)(2,1)S(1)} %copy-done.15), channel_id=1, source_target_pairs={{0,2},{2,4},{4,6},{6,0},{1,3},{3,5},{5,7},{7,1},{8,10},{10,12},{12... | collective-permute-start | bytes 2359304 | tf_op jit(solution)/shard_map/rows/ppermute | solution.py:321
  99.2 26.2 %collective-permute-start.18 = (bf16[384,1024]{1,0:T(8,128)(2,1)}, bf16[384,1024]{1,0:T(8,128)(2,1)}, u32[]{:S(2)}, u32[]{:S(2)}) collective-permute-start(bf16[384,1024]{1,0:T(8,128)(2,1)} %collective-permute-done.16.refs_1_), channel_id=1, source_target_pairs={{0,6},{2,0},{4,2},{6,4},{1,7},{3,1},{5,3},{7,5},{8,14},{10,8},{12,... | collective-permute-start | bytes 2359304 | tf_op jit(solution)/shard_map/rows/ppermute | solution.py:321
  108.5 0.7 copy-start.17
  109.2 0.7 copy-start.18
  114.8 34.2 %all-to-all-start.1 = ((bf16[32,8,1024]{2,1,0:T(8,128)(2,1)}), bf16[32,8,1024]{2,1,0:T(8,128)(2,1)S(1)}, u32[]{:S(2)}, u32[]{:S(2)}) async-start(bf16[32,8,1024]{2,1,0:T(8,128)(2,1)} %bitcast.25), calls=%async_computation.1 | async-start | bytes 1048576 | tf_op jit(solution)/shard_map/down/all_to_all | solution.py:301
  124.3 9.7 %copy-start.8 = (bf16[192,1024]{1,0:T(8,128)(2,1)S(1)}, bf16[192,1024]{1,0:T(8,128)(2,1)}, u32[]{:S(2)}) copy-start(bf16[192,1024]{1,0:T(8,128)(2,1)} %get-tuple-element.28.refs_4_.same_ref) | copy-start | bytes 1179652
  125.5 19.2 %copy-start.10 = (f32[2,1,4096]{2,1,0:T(1,128)S(1)}, f32[2,1,4096]{2,1,0:T(1,128)}, u32[]{:S(2)}) copy-start(f32[2,1,4096]{2,1,0:T(1,128)} %reshape.34.refs_12_.refs_10_) | copy-start | bytes 98308
  125.5 19.2 %copy-start.11 = (bf16[256,128]{1,0:T(8,128)(2,1)S(1)}, bf16[256,128]{1,0:T(8,128)(2,1)}, u32[]{:S(2)}) copy-start(bf16[256,128]{1,0:T(8,128)(2,1)} %get-tuple-element.48.refs_11_) | copy-start | bytes 196612
  125.5 19.2 %copy-start.12 = (s32[2]{0:T(128)S(1)}, s32[2]{0:T(128)}, u32[]{:S(2)}) copy-start(s32[2]{0:T(128)} %pad_add_fusion.place_ref) | copy-start | bytes 28
  131.2 13.5 %copy-start.1 = (bf16[192,1024]{1,0:T(8,128)(2,1)S(1)}, bf16[192,1024]{1,0:T(8,128)(2,1)}, u32[]{:S(2)}) copy-start(bf16[192,1024]{1,0:T(8,128)(2,1)} %copy-done) | copy-start | bytes 1179652
  131.2 13.5 %copy-start.3 = (bf16[192,1024]{1,0:T(8,128)(2,1)S(1)}, bf16[192,1024]{1,0:T(8,128)(2,1)}, u32[]{:S(2)}) copy-start(bf16[192,1024]{1,0:T(8,128)(2,1)} %copy-done.2) | copy-start | bytes 1179652
  131.2 13.5 %copy-start.5 = (bf16[192,1024]{1,0:T(8,128)(2,1)S(1)}, bf16[192,1024]{1,0:T(8,128)(2,1)}, u32[]{:S(2)}) copy-start(bf16[192,1024]{1,0:T(8,128)(2,1)} %copy-done.4) | copy-start | bytes 1179652
  131.2 13.5 %copy-start.7 = (bf16[192,1024]{1,0:T(8,128)(2,1)S(1)}, bf16[192,1024]{1,0:T(8,128)(2,1)}, u32[]{:S(2)}) copy-start(bf16[192,1024]{1,0:T(8,128)(2,1)} %copy-done.6) | copy-start | bytes 1179652
  131.2 9.1 %collective-permute-start.19 = (bf16[384,384]{1,0:T(8,128)(2,1)}, bf16[384,384]{1,0:T(8,128)(2,1)S(1)}, u32[]{:S(2)}, u32[]{:S(2)}) collective-permute-start(bf16[384,384]{1,0:T(8,128)(2,1)} %up.7.h_ref), channel_id=1, source_target_pairs={{0,2},{2,4},{4,6},{6,0},{1,3},{3,5},{5,7},{7,1},{8,10},{10,12},{12... | collective-permute-start | bytes 884744 | tf_op jit(solution)/shard_map/down/ppermute | solution.py:321
  131.3 9.0 %collective-permute-start.20 = (bf16[384,384]{1,0:T(8,128)(2,1)}, bf16[384,384]{1,0:T(8,128)(2,1)S(1)}, u32[]{:S(2)}, u32[]{:S(2)}) collective-permute-start(bf16[384,384]{1,0:T(8,128)(2,1)} %up.7.h_ref), channel_id=1, source_target_pairs={{0,6},{2,0},{4,2},{6,4},{1,7},{3,1},{5,3},{7,5},{8,14},{10,8},{12,... | collective-permute-start | bytes 884744 | tf_op jit(solution)/shard_map/down/ppermute | solution.py:321
  134.0 10.7 %collective-permute-start.21 = (bf16[384,384]{1,0:T(8,128)(2,1)}, bf16[384,384]{1,0:T(8,128)(2,1)S(1)}, u32[]{:S(2)}, u32[]{:S(2)}) collective-permute-start(bf16[384,384]{1,0:T(8,128)(2,1)} %up.7.h_ref), channel_id=1, source_target_pairs={{0,4},{2,6},{4,0},{6,2},{1,5},{3,7},{5,1},{7,3},{8,12},{10,14},{12... | collective-permute-start | bytes 884744 | tf_op jit(solution)/shard_map/down/ppermute | solution.py:321
  134.0 1.0 copy-start.9
  149.0 9.6 %copy-start.13 = (s32[128,8]{0,1:T(8,128)S(1)}, s32[128,8]{0,1:T(8,128)}, u32[]{:S(2)}) copy-start(s32[128,8]{0,1:T(8,128)} %param.12) | copy-start | bytes 12292
  149.0 9.6 %copy-start.14 = (f32[128,8]{0,1:T(8,128)S(1)}, f32[128,8]{0,1:T(8,128)}, u32[]{:S(2)}) copy-start(f32[128,8]{0,1:T(8,128)} %param.13) | copy-start | bytes 12292
  149.0 28.5 %all-to-all-start.2 = ((bf16[32,8,1664]{2,1,0:T(8,128)(2,1)}), bf16[32,8,1664]{2,1,0:T(8,128)(2,1)S(1)}, u32[]{:S(2)}, u32[]{:S(2)}) async-start(bf16[32,8,1664]{2,1,0:T(8,128)(2,1)} %bitcast.11), calls=%async_computation.2 | async-start | bytes 1703936 | tf_op jit(solution)/shard_map/down/all_to_all | solution.py:301
  179.1 7.5 %collective-permute-start.22 = (f32[128,512]{1,0:T(8,128)S(1)}, f32[128,512]{1,0:T(8,128)S(1)}, u32[]{:S(2)}, u32[]{:S(2)}) collective-permute-start(f32[128,512]{1,0:T(8,128)S(1)} %get-tuple-element.50), channel_id=1, source_target_pairs={{0,1},{1,0},{2,3},{3,2},{4,5},{5,4},{6,7},{7,6},{8,9},{9,8},{10,11... | collective-permute-start | bytes 786440 | tf_op jit(solution)/shard_map/combine/ppermute | solution.py:458
  (1 other events, 0.7 us)

commit v5 on v4

--- a/solution.py
+++ b/solution.py
@@ -315,12 +315,13 @@
             out_shape=[sds(rows, quarter), sds(rows + rows // 2, quarter), sds(rows, kv_cols)],
             compiler_params=PARAMS,
             cost_estimate=CHEAP,
-        )(after(arrived, *wd, scales), page_slots.reshape(1, -1))
+        )(after(arrived, *wd[:6], scales), page_slots.reshape(1, -1))
 
     def shift(v, by):
         return lax.ppermute(v, "y", [(i, (i + by) % n_y) for i in range(n_y)])
 
     with jax.named_scope("rows"):
+        x_p = after(x_p, x_q, *wd[6:])
         p_left, p_right = shift(x_p, 1), shift(x_p, -1)
         p_far = shift(p_left, 1)
         q_right = shift(after(x_q, p_right, p_left), -1)

time: 188 us -> 188 us (level)
  waiting for transfers between devices: 72.6 us -> 68.3 us
  starting transfers between devices: 61.9 us -> 65.9 us
    ppermute x7, waiting for transfers between devices: 24 us -> 11.1 us  [on_device(): wd.append(lax.ppermute(v, ('y', 'core'), pairs))]
    all_to_all x3, waiting for transfers between devices: 17.6 us -> 26.7 us  [exchange(): lax.all_to_all(v.reshape(n_dp, ROWS, v.shape[-1]), DP, 0, 0, tiled=True)]
    ppermute x12, starting transfers between devices: 13.6 us -> 17.4 us  [shift(): return lax.ppermute(v, 'y', [(i, (i + by) % n_y) for i in range(n_y)])]
  transfers between devices with their start and end apart: 26 -> 26, of which waited for: 13 -> 15; matrix products, arithmetic and copies ran while one was open for 1% -> 1% of each run, Pallas kernels for 21% -> 22%
where the time goes in v5:
time: 188 us; the launch traced here: 187 us
  waiting for transfers between devices  68.3 us (36%)
  starting transfers between devices  65.9 us (35%)
  Pallas kernels  46.9 us (25%)
  local copies, waits for them, and re-layouts  3.08 us (2%)
  other arithmetic  1.93 us (1%)
    all_to_all x3, starting transfers between devices, exchange(): lax.all_to_all(v.reshape(n_dp, ROWS, v.shape[-1]), DP, 0, 0, tiled=True)  30.9 us
    ppermute x12, waiting for transfers between devices, shift(): return lax.ppermute(v, 'y', [(i, (i + by) % n_y) for i in range(n_y)])  28.5 us
    all_to_all x3, waiting for transfers between devices, exchange(): lax.all_to_all(v.reshape(n_dp, ROWS, v.shape[-1]), DP, 0, 0, tiled=True)  26.7 us
    ppermute x12, starting transfers between devices, shift(): return lax.ppermute(v, 'y', [(i, (i + by) % n_y) for i in range(n_y)])  17.4 us
    ppermute x7, waiting for transfers between devices, on_device(): wd.append(lax.ppermute(v, ('y', 'core'), pairs))  11.1 us
    ppermute x7, starting transfers between devices, on_device(): wd.append(lax.ppermute(v, ('y', 'core'), pairs))  10.2 us
    ppermute x1, starting transfers between devices, on_device(): moe_out = (keep + lax.ppermute(send, 'core', [(0, 1), (1, 0)])).astype(BF)  6.38 us
    pallas_call x1, Pallas kernels, on_device(): call(up_first_kernel, 3, [whole(r, quarter)] * 3 + weight_specs(0, 3, 1),...  6.16 us
  transfers between devices with their start and end apart: 26, of which 15 were waited for; matrix products, arithmetic and copies ran while one was open for 1% of the time, Pallas kernels for 22%

profile of v5, /device:TPU:1, one launch (start us, length us, event | category | flops | bytes accessed | tf_op | source)
XLA Modules:
  0.0 186.9 jit_solution(4135384037942937317)
XLA Ops:
  1.2 5.0 %route.2 = (bf16[256,2688]{1,0:T(8,128)(2,1)}, bf16[192,1024]{1,0:T(8,128)(2,1)}, bf16[192,1024]{1,0:T(8,128)(2,1)}, bf16[192,1024]{1,0:T(8,128)(2,1)}, bf16[192...) custom-call(s32[2]{0:T(128)} %pad_add_fusion.place_ref, ...), custom_call_target="tpu_custom_call" | custom-call | flops 1000 | bytes 1000 | tf_op jit(solution)/shard_map/route/pallas_call | solution.py:271
  6.2 12.0 %all-to-all-start = ((bf16[32,8,2688]{2,1,0:T(8,128)(2,1)}), bf16[32,8,2688]{2,1,0:T(8,128)(2,1)}, u32[]{:S(2)}, u32[]{:S(2)}) async-start(bf16[32,8,2688]{2,1,0:T(8,128)(2,1)} %bitcast.26), calls=%async_computation | async-start | bytes 2752512 | tf_op jit(solution)/shard_map/dispatch/all_to_all | solution.py:301
  18.2 1.0 collective-permute-start
  19.3 1.3 collective-permute-start.1
  20.6 1.5 collective-permute-start.2
  22.1 1.4 collective-permute-start.3
  24.1 0.8 collective-permute-done.5
  25.3 4.2 %route.3 = (bf16[1,192,4096]{2,1,0:T(8,128)(2,1)}, bf16[1,192,4096]{2,1,0:T(8,128)(2,1)}) custom-call(s32[2]{0:T(128)} %pad_add_fusion.place_ref, bf16[2,192,4096]{2,1,0:T(8,128)(2,1)} %refs_2_.3, bf16[2,192,4096]{2,1,0:T(8,128)(2,1)} %refs_4_.3), custom_call_target="tpu_custom_call" | custom-call | flops 1000 | bytes 1000 | tf_op jit(solution)/shard_map/route/pallas_call | solution.py:280
  29.6 1.7 collective-permute-start.6
  31.6 2.7 %collective-permute-start.7 = (bf16[192,1024]{1,0:T(8,128)(2,1)S(1)}, bf16[192,1024]{1,0:T(8,128)(2,1)}, u32[]{:S(2)}, u32[]{:S(2)}) collective-permute-start(bf16[192,1024]{1,0:T(8,128)(2,1)S(1)} %copy-done.22), channel_id=1, source_target_pairs={{0,5},{1,4},{2,7},{3,6},{4,1},{5,0},{6,3},{7,2},{8,13},{9,12},{10,... | collective-permute-start | bytes 1179656 | tf_op jit(solution)/shard_map/route/ppermute | solution.py:298
  34.3 6.1 %collective-permute-done.2.refs_7_.refs_4_ = bf16[192,1024]{1,0:T(8,128)(2,1)S(1)} collective-permute-done((bf16[192,1024]{1,0:T(8,128)(2,1)}, bf16[192,1024]{1,0:T(8,128)(2,1)S(1)}, u32[]{:S(2)}, u32[]{:S(2)}) %collective-permute-start.2) | collective-permute-done | bytes 393248 | tf_op jit(solution)/shard_map/route/ppermute | solution.py:298
  40.9 0.7 pad_maximum_fusion.refs_6_.refs_7_
  41.6 1.0 collective-permute-done.4.refs_9_.refs_6_
  42.6 8.9 %all-to-all-done = bf16[32,8,2688]{2,1,0:T(8,128)(2,1)} async-done(((bf16[32,8,2688]{2,1,0:T(8,128)(2,1)}), bf16[32,8,2688]{2,1,0:T(8,128)(2,1)}, u32[]{:S(2)}, u32[]{:S(2)}) %all-to-all-start) | async-done | bytes 1376288 | tf_op jit(solution)/shard_map/dispatch/all_to_all | solution.py:301
  51.5 2.9 %unpack.1 = (bf16[256,1024]{1,0:T(8,128)(2,1)}, bf16[384,1024]{1,0:T(8,128)(2,1)}, bf16[256,128]{1,0:T(8,128)(2,1)}) custom-call(bf16[256,2688]{1,0:T(8,128)(2,1)} %bitcast.5.in_ref, s32[1,128]{1,0:T(1,128)} %bitcast.31), custom_call_target="tpu_custom_call" | custom-call | flops 1000 | bytes 1000 | tf_op jit(solution)/shard_map/unpack/pallas_call | solution.py:313
  54.4 3.8 %collective-permute-done.7.refs_11_.refs_8_ = bf16[192,1024]{1,0:T(8,128)(2,1)} collective-permute-done((bf16[192,1024]{1,0:T(8,128)(2,1)S(1)}, bf16[192,1024]{1,0:T(8,128)(2,1)}, u32[]{:S(2)}, u32[]{:S(2)}) %collective-permute-start.7) | collective-permute-done | bytes 393248 | tf_op jit(solution)/shard_map/route/ppermute | solution.py:298
  58.2 4.4 %collective-permute-start.8 = (bf16[256,1024]{1,0:T(8,128)(2,1)}, bf16[256,1024]{1,0:T(8,128)(2,1)}, u32[]{:S(2)}, u32[]{:S(2)}) collective-permute-start(bf16[256,1024]{1,0:T(8,128)(2,1)} %get-tuple-element.43.refs_0_), channel_id=1, source_target_pairs={{0,2},{2,4},{4,6},{6,0},{1,3},{3,5},{5,7},{7,1},{8,10},{10,12},{12... | collective-permute-start | bytes 1572872 | tf_op jit(solution)/shard_map/rows/ppermute | solution.py:321
  62.6 1.7 collective-permute-start.12
  64.2 9.8 %collective-permute-done.8.refs_1_ = bf16[256,1024]{1,0:T(8,128)(2,1)} collective-permute-done((bf16[256,1024]{1,0:T(8,128)(2,1)}, bf16[256,1024]{1,0:T(8,128)(2,1)}, u32[]{:S(2)}, u32[]{:S(2)}) %collective-permute-start.8) | collective-permute-done | bytes 524320 | tf_op jit(solution)/shard_map/rows/ppermute | solution.py:321
  74.0 1.6 collective-permute-done.12.refs_2_
  75.7 1.3 collective-permute-start.16
  77.5 6.2 %up.4.refs_5_ = f32[256,768]{1,0:T(8,128)} custom-call(s32[2]{0:T(128)} %pad_add_fusion.place_ref, bf16[256,1024]{1,0:T(8,128)(2,1)} %get-tuple-element.43.refs_0_, bf16[256,1024]{1,0:T(8,128)(2,1)} %collective-permute-done.8.refs_1_, bf16[256,1024]{1,0:T(8,128)(2,1)} %collective-permute-done.12.refs_2_, bf16[2,192,4096]{2,1,0:T(8,128)(2,1)} %refs_2_.3, ...), custom_call_target="tpu_custom_call" | custom-call | flops 1000 | bytes 1000 | tf_op jit(solution)/shard_map/up/pallas_call | solution.py:375
  83.7 7.4 %collective-permute-done.9.refs_0_ = bf16[256,1024]{1,0:T(8,128)(2,1)} collective-permute-done((bf16[256,1024]{1,0:T(8,128)(2,1)}, bf16[256,1024]{1,0:T(8,128)(2,1)}, u32[]{:S(2)}, u32[]{:S(2)}) %collective-permute-start.9) | collective-permute-done | bytes 524320 | tf_op jit(solution)/shard_map/rows/ppermute | solution.py:321
  91.1 3.9 %up.5.refs_0_ = bf16[256,384]{1,0:T(8,128)(2,1)} custom-call(s32[2]{0:T(128)} %pad_add_fusion.place_ref, bf16[256,1024]{1,0:T(8,128)(2,1)} %collective-permute-done.9.refs_0_, bf16[2,192,4096]{2,1,0:T(8,128)(2,1)} %refs_2_.3, bf16[1,192,4096]{2,1,0:T(8,128)(2,1)} %collective-permute-done.10.refs_4_.refs_2_.refs_3_, bf16[2,192,4096]{2,1,0:T(8,128)(2,1)} %refs_4_.3, ...), custom_call_target="tpu_custom_call" | custom-call | flops 1000 | bytes 1000 | tf_op jit(solution)/shard_map/up/pallas_call | solution.py:382
  95.0 1.2 collective-permute-start.15
  96.3 2.7 %collective-permute-start.14 = (bf16[256,384]{1,0:T(8,128)(2,1)}, bf16[256,384]{1,0:T(8,128)(2,1)S(1)}, u32[]{:S(2)}, u32[]{:S(2)}) collective-permute-start(bf16[256,384]{1,0:T(8,128)(2,1)} %up.5.refs_0_), channel_id=1, source_target_pairs={{0,6},{2,0},{4,2},{6,4},{1,7},{3,1},{5,3},{7,5},{8,14},{10,8},{12,... | collective-permute-start | bytes 589832 | tf_op jit(solution)/shard_map/down/ppermute | solution.py:321
  99.0 2.7 %collective-permute-start.18 = (bf16[384,1024]{1,0:T(8,128)(2,1)}, bf16[384,1024]{1,0:T(8,128)(2,1)}, u32[]{:S(2)}, u32[]{:S(2)}) collective-permute-start(bf16[384,1024]{1,0:T(8,128)(2,1)} %collective-permute-done.16.refs_1_), channel_id=1, source_target_pairs={{0,6},{2,0},{4,2},{6,4},{1,7},{3,1},{5,3},{7,5},{8,14},{10,8},{12,... | collective-permute-start | bytes 2359304 | tf_op jit(solution)/shard_map/rows/ppermute | solution.py:321
  101.6 0.6 reshape.34.refs_12_.refs_10_
  102.3 5.4 %up.6.refs_6_ = f32[384,768]{1,0:T(8,128)} custom-call(s32[2]{0:T(128)} %pad_add_fusion.place_ref, bf16[384,1024]{1,0:T(8,128)(2,1)} %get-tuple-element.49.refs_0_, bf16[384,1024]{1,0:T(8,128)(2,1)} %collective-permute-done.16.refs_1_, bf16[2,192,4096]{2,1,0:T(8,128)(2,1)} %refs_2_.3, bf16[1,192,4096]{2,1,0:T(8,128)(2,1)} %collective-permute-done.10.refs_4_.refs_2_.refs_3_, ...), custom_call_target="tpu_custom_call" | custom-call | flops 1000 | bytes 1000 | tf_op jit(solution)/shard_map/up/pallas_call | solution.py:393
  107.8 0.6 copy-done.16
  108.4 0.7 copy-done.18
  109.1 4.9 %down.3 = bf16[256,1024]{1,0:T(8,128)(2,1)} custom-call(s32[2]{0:T(128)} %pad_add_fusion.place_ref, bf16[256,384]{1,0:T(8,128)(2,1)} %up.5.refs_0_, bf16[256,384]{1,0:T(8,128)(2,1)} %copy-done.17, bf16[256,384]{1,0:T(8,128)(2,1)} %copy-done.18, bf16[256,384]{1,0:T(8,128)(2,1)} %copy-done.16, bf16[192,1024]{1,0:T(8,128)(2,1)} %get-tuple-element.29.refs_4_.same_ref, ...), custom_call_target="tpu_custom_call" | custom-call | flops 1000 | bytes 1000 | tf_op jit(solution)/shard_map/down/pallas_call | solution.py:404
  114.0 9.4 %all-to-all-start.1 = ((bf16[32,8,1024]{2,1,0:T(8,128)(2,1)}), bf16[32,8,1024]{2,1,0:T(8,128)(2,1)S(1)}, u32[]{:S(2)}, u32[]{:S(2)}) async-start(bf16[32,8,1024]{2,1,0:T(8,128)(2,1)} %bitcast.25), calls=%async_computation.1 | async-start | bytes 1048576 | tf_op jit(solution)/shard_map/down/all_to_all | solution.py:301
  123.5 1.2 collective-permute-done.17.refs_0_
  124.7 5.7 %up.7.h_ref = bf16[384,384]{1,0:T(8,128)(2,1)} custom-call(s32[2]{0:T(128)} %pad_add_fusion.place_ref, bf16[384,1024]{1,0:T(8,128)(2,1)} %collective-permute-done.17.refs_0_, bf16[384,1024]{1,0:T(8,128)(2,1)} %collective-permute-done.18.refs_1_, bf16[2,192,4096]{2,1,0:T(8,128)(2,1)} %refs_2_.3, ...), custom_call_target="tpu_custom_call" | custom-call | flops 1000 | bytes 1000 | tf_op jit(solution)/shard_map/up/pallas_call | solution.py:415
  130.6 2.7 %collective-permute-start.20 = (bf16[384,384]{1,0:T(8,128)(2,1)}, bf16[384,384]{1,0:T(8,128)(2,1)S(1)}, u32[]{:S(2)}, u32[]{:S(2)}) collective-permute-start(bf16[384,384]{1,0:T(8,128)(2,1)} %up.7.h_ref), channel_id=1, source_target_pairs={{0,6},{2,0},{4,2},{6,4},{1,7},{3,1},{5,3},{7,5},{8,14},{10,8},{12,... | collective-permute-start | bytes 884744 | tf_op jit(solution)/shard_map/down/ppermute | solution.py:321
  133.3 1.0 copy-done.9
  134.3 1.6 down.4.refs_9_
  135.9 3.2 %collective-permute-done.19.refs_0_ = bf16[384,384]{1,0:T(8,128)(2,1)S(1)} collective-permute-done((bf16[384,384]{1,0:T(8,128)(2,1)}, bf16[384,384]{1,0:T(8,128)(2,1)S(1)}, u32[]{:S(2)}, u32[]{:S(2)}) %collective-permute-start.19) | collective-permute-done | bytes 294944 | tf_op jit(solution)/shard_map/down/ppermute | solution.py:321
  139.1 5.1 %collective-permute-done.21.refs_2_ = bf16[384,384]{1,0:T(8,128)(2,1)S(1)} collective-permute-done((bf16[384,384]{1,0:T(8,128)(2,1)}, bf16[384,384]{1,0:T(8,128)(2,1)S(1)}, u32[]{:S(2)}, u32[]{:S(2)}) %collective-permute-start.21) | collective-permute-done | bytes 294944 | tf_op jit(solution)/shard_map/down/ppermute | solution.py:321
  144.2 4.3 %down.5 = bf16[256,1664]{1,0:T(8,128)(2,1)} custom-call(s32[2]{0:T(128)S(1)} %copy-done.12, bf16[384,384]{1,0:T(8,128)(2,1)S(1)} %collective-permute-done.19.refs_0_, bf16[384,384]{1,0:T(8,128)(2,1)S(1)} %collective-permute-done.20.refs_1_, bf16[384,384]{1,0:T(8,128)(2,1)S(1)} %collective-permute-done.21.refs_2_, bf16[192,1024]{1,0:T(8,128)(2,1)S(1)} %copy-done.1, ...), custom_call_target="tpu_custom_call" | custom-call | flops 1000 | bytes 1000 | tf_op jit(solution)/shard_map/down/pallas_call | solution.py:432
  148.5 9.5 %all-to-all-start.2 = ((bf16[32,8,1664]{2,1,0:T(8,128)(2,1)}), bf16[32,8,1664]{2,1,0:T(8,128)(2,1)S(1)}, u32[]{:S(2)}, u32[]{:S(2)}) async-start(bf16[32,8,1664]{2,1,0:T(8,128)(2,1)} %bitcast.11), calls=%async_computation.2 | async-start | bytes 1703936 | tf_op jit(solution)/shard_map/down/all_to_all | solution.py:301
  158.0 1.3 combine.2
  159.3 17.7 %all-to-all-done.2 = bf16[32,8,1664]{2,1,0:T(8,128)(2,1)S(1)} async-done(((bf16[32,8,1664]{2,1,0:T(8,128)(2,1)}), bf16[32,8,1664]{2,1,0:T(8,128)(2,1)S(1)}, u32[]{:S(2)}, u32[]{:S(2)}) %all-to-all-start.2) | async-done | bytes 852000 | tf_op jit(solution)/shard_map/down/all_to_all | solution.py:301
  177.1 1.6 combine.3
  178.7 6.4 %collective-permute-start.22 = (f32[128,512]{1,0:T(8,128)S(1)}, f32[128,512]{1,0:T(8,128)S(1)}, u32[]{:S(2)}, u32[]{:S(2)}) collective-permute-start(f32[128,512]{1,0:T(8,128)S(1)} %get-tuple-element.52), channel_id=1, source_target_pairs={{0,1},{1,0},{2,3},{3,2},{4,5},{5,4},{6,7},{7,6},{8,9},{9,8},{10,11... | collective-permute-start | bytes 786440 | tf_op jit(solution)/shard_map/combine/ppermute | solution.py:459
  185.1 1.2 collective-permute-done.22
  186.3 0.7 add_convert_fusion
  (69 shorter events, 3.3 us)
Async XLA Ops:
  6.2 17.3 %copy-start.20 = (f32[2,192]{1,0:T(2,128)S(1)}, f32[2,192]{1,0:T(2,128)}, u32[]{:S(2)}) copy-start(f32[2,192]{1,0:T(2,128)} %param.17) | copy-start | bytes 4612
  6.2 17.3 %copy-start.21 = (f32[2,192]{1,0:T(2,128)S(1)}, f32[2,192]{1,0:T(2,128)}, u32[]{:S(2)}) copy-start(f32[2,192]{1,0:T(2,128)} %param.18) | copy-start | bytes 4612
  6.2 45.3 %all-to-all-start = ((bf16[32,8,2688]{2,1,0:T(8,128)(2,1)}), bf16[32,8,2688]{2,1,0:T(8,128)(2,1)}, u32[]{:S(2)}, u32[]{:S(2)}) async-start(bf16[32,8,2688]{2,1,0:T(8,128)(2,1)} %bitcast.26), calls=%async_computation | async-start | bytes 2752512 | tf_op jit(solution)/shard_map/dispatch/all_to_all | solution.py:301
  18.2 11.4 %collective-permute-start = (bf16[192,1024]{1,0:T(8,128)(2,1)}, bf16[192,1024]{1,0:T(8,128)(2,1)}, u32[]{:S(2)}, u32[]{:S(2)}) collective-permute-start(bf16[192,1024]{1,0:T(8,128)(2,1)} %get-tuple-element.30), channel_id=1, source_target_pairs={{0,1},{1,0},{2,3},{3,2},{4,5},{5,4},{6,7},{7,6},{8,9},{9,8},{10,11... | collective-permute-start | bytes 1179656 | tf_op jit(solution)/shard_map/route/ppermute | solution.py:298
  19.3 12.3 %collective-permute-start.1 = (bf16[192,1024]{1,0:T(8,128)(2,1)}, bf16[192,1024]{1,0:T(8,128)(2,1)S(1)}, u32[]{:S(2)}, u32[]{:S(2)}) collective-permute-start(bf16[192,1024]{1,0:T(8,128)(2,1)} %get-tuple-element.31), channel_id=1, source_target_pairs={{0,2},{1,3},{2,4},{3,5},{4,6},{5,7},{6,0},{7,1},{8,10},{9,11},{10,... | collective-permute-start | bytes 1179656 | tf_op jit(solution)/shard_map/route/ppermute | solution.py:298
  20.6 19.8 %collective-permute-start.2 = (bf16[192,1024]{1,0:T(8,128)(2,1)}, bf16[192,1024]{1,0:T(8,128)(2,1)S(1)}, u32[]{:S(2)}, u32[]{:S(2)}) collective-permute-start(bf16[192,1024]{1,0:T(8,128)(2,1)} %get-tuple-element.32), channel_id=1, source_target_pairs={{0,3},{1,2},{2,5},{3,4},{4,7},{5,6},{6,1},{7,0},{8,11},{9,10},{10,... | collective-permute-start | bytes 1179656 | tf_op jit(solution)/shard_map/route/ppermute | solution.py:298
  22.1 18.3 %collective-permute-start.3 = (bf16[192,1024]{1,0:T(8,128)(2,1)}, bf16[192,1024]{1,0:T(8,128)(2,1)S(1)}, u32[]{:S(2)}, u32[]{:S(2)}) collective-permute-start(bf16[192,1024]{1,0:T(8,128)(2,1)} %get-tuple-element.33), channel_id=1, source_target_pairs={{0,6},{1,7},{2,0},{3,1},{4,2},{5,3},{6,4},{7,5},{8,14},{9,15},{10,... | collective-permute-start | bytes 1179656 | tf_op jit(solution)/shard_map/route/ppermute | solution.py:298
  23.5 1.4 collective-permute-start.5
  24.9 6.7 %copy-start.22 = (bf16[192,1024]{1,0:T(8,128)(2,1)S(1)}, bf16[192,1024]{1,0:T(8,128)(2,1)}, u32[]{:S(2)}) copy-start(bf16[192,1024]{1,0:T(8,128)(2,1)} %get-tuple-element.42) | copy-start | bytes 1179652
  24.9 17.7 %collective-permute-start.4 = (bf16[192,1024]{1,0:T(8,128)(2,1)}, bf16[192,1024]{1,0:T(8,128)(2,1)S(1)}, u32[]{:S(2)}, u32[]{:S(2)}) collective-permute-start(bf16[192,1024]{1,0:T(8,128)(2,1)} %get-tuple-element.34), channel_id=1, source_target_pairs={{0,7},{1,6},{2,1},{3,0},{4,3},{5,2},{6,5},{7,4},{8,15},{9,14},{10,... | collective-permute-start | bytes 1179656 | tf_op jit(solution)/shard_map/route/ppermute | solution.py:298
  29.6 24.8 %collective-permute-start.6 = (bf16[192,1024]{1,0:T(8,128)(2,1)}, bf16[192,1024]{1,0:T(8,128)(2,1)}, u32[]{:S(2)}, u32[]{:S(2)}) collective-permute-start(bf16[192,1024]{1,0:T(8,128)(2,1)} %get-tuple-element.38), channel_id=1, source_target_pairs={{0,4},{1,5},{2,6},{3,7},{4,0},{5,1},{6,2},{7,3},{8,12},{9,13},{10,... | collective-permute-start | bytes 1179656 | tf_op jit(solution)/shard_map/route/ppermute | solution.py:298
  31.6 52.1 %copy-start = (bf16[192,1024]{1,0:T(8,128)(2,1)}, bf16[192,1024]{1,0:T(8,128)(2,1)S(1)}, u32[]{:S(2)}) copy-start(bf16[192,1024]{1,0:T(8,128)(2,1)S(1)} %collective-permute-done.1.refs_6_.refs_3_) | copy-start | bytes 1179652
  31.6 26.6 %collective-permute-start.7 = (bf16[192,1024]{1,0:T(8,128)(2,1)S(1)}, bf16[192,1024]{1,0:T(8,128)(2,1)}, u32[]{:S(2)}, u32[]{:S(2)}) collective-permute-start(bf16[192,1024]{1,0:T(8,128)(2,1)S(1)} %copy-done.22), channel_id=1, source_target_pairs={{0,5},{1,4},{2,7},{3,6},{4,1},{5,0},{6,3},{7,2},{8,13},{9,12},{10,... | collective-permute-start | bytes 1179656 | tf_op jit(solution)/shard_map/route/ppermute | solution.py:298
  40.4 43.3 %copy-start.2 = (bf16[192,1024]{1,0:T(8,128)(2,1)}, bf16[192,1024]{1,0:T(8,128)(2,1)S(1)}, u32[]{:S(2)}) copy-start(bf16[192,1024]{1,0:T(8,128)(2,1)S(1)} %collective-permute-done.2.refs_7_.refs_4_) | copy-start | bytes 1179652
  40.4 37.1 %collective-permute-start.10 = (bf16[1,192,4096]{2,1,0:T(8,128)(2,1)}, bf16[1,192,4096]{2,1,0:T(8,128)(2,1)}, u32[]{:S(2)}, u32[]{:S(2)}) collective-permute-start(bf16[1,192,4096]{2,1,0:T(8,128)(2,1)} %get-tuple-element.41), channel_id=1, source_target_pairs={{0,1},{1,0},{2,3},{3,2},{4,5},{5,4},{6,7},{7,6},{8,9},{9,8},{10,11... | collective-permute-start | bytes 4718600 | tf_op jit(solution)/shard_map/swap/ppermute | solution.py:332
  40.4 43.3 %copy-start.4 = (bf16[192,1024]{1,0:T(8,128)(2,1)}, bf16[192,1024]{1,0:T(8,128)(2,1)S(1)}, u32[]{:S(2)}) copy-start(bf16[192,1024]{1,0:T(8,128)(2,1)S(1)} %collective-permute-done.3.refs_8_.refs_5_) | copy-start | bytes 1179652
  40.4 37.1 %collective-permute-start.11 = (bf16[1,192,4096]{2,1,0:T(8,128)(2,1)}, bf16[1,192,4096]{2,1,0:T(8,128)(2,1)}, u32[]{:S(2)}, u32[]{:S(2)}) collective-permute-start(bf16[1,192,4096]{2,1,0:T(8,128)(2,1)} %get-tuple-element.44), channel_id=1, source_target_pairs={{0,1},{1,0},{2,3},{3,2},{4,5},{5,4},{6,7},{7,6},{8,9},{9,8},{10,11... | collective-permute-start | bytes 4718600 | tf_op jit(solution)/shard_map/swap/ppermute | solution.py:332
  42.6 41.1 %copy-start.6 = (bf16[192,1024]{1,0:T(8,128)(2,1)}, bf16[192,1024]{1,0:T(8,128)(2,1)S(1)}, u32[]{:S(2)}) copy-start(bf16[192,1024]{1,0:T(8,128)(2,1)S(1)} %collective-permute-done.4.refs_9_.refs_6_) | copy-start | bytes 1179652
  58.2 15.9 %collective-permute-start.8 = (bf16[256,1024]{1,0:T(8,128)(2,1)}, bf16[256,1024]{1,0:T(8,128)(2,1)}, u32[]{:S(2)}, u32[]{:S(2)}) collective-permute-start(bf16[256,1024]{1,0:T(8,128)(2,1)} %get-tuple-element.43.refs_0_), channel_id=1, source_target_pairs={{0,2},{2,4},{4,6},{6,0},{1,3},{3,5},{5,7},{7,1},{8,10},{10,12},{12... | collective-permute-start | bytes 1572872 | tf_op jit(solution)/shard_map/rows/ppermute | solution.py:321
  62.6 13.1 %collective-permute-start.12 = (bf16[256,1024]{1,0:T(8,128)(2,1)}, bf16[256,1024]{1,0:T(8,128)(2,1)}, u32[]{:S(2)}, u32[]{:S(2)}) collective-permute-start(bf16[256,1024]{1,0:T(8,128)(2,1)} %get-tuple-element.43.refs_0_), channel_id=1, source_target_pairs={{0,6},{2,0},{4,2},{6,4},{1,7},{3,1},{5,3},{7,5},{8,14},{10,8},{12,... | collective-permute-start | bytes 1572872 | tf_op jit(solution)/shard_map/rows/ppermute | solution.py:321
  75.7 23.3 %collective-permute-start.16 = (bf16[384,1024]{1,0:T(8,128)(2,1)}, bf16[384,1024]{1,0:T(8,128)(2,1)}, u32[]{:S(2)}, u32[]{:S(2)}) collective-permute-start(bf16[384,1024]{1,0:T(8,128)(2,1)} %get-tuple-element.49.refs_0_), channel_id=1, source_target_pairs={{0,6},{2,0},{4,2},{6,4},{1,7},{3,1},{5,3},{7,5},{8,14},{10,8},{12,... | collective-permute-start | bytes 2359304 | tf_op jit(solution)/shard_map/rows/ppermute | solution.py:321
  77.0 14.2 %collective-permute-start.9 = (bf16[256,1024]{1,0:T(8,128)(2,1)}, bf16[256,1024]{1,0:T(8,128)(2,1)}, u32[]{:S(2)}, u32[]{:S(2)}) collective-permute-start(bf16[256,1024]{1,0:T(8,128)(2,1)} %collective-permute-done.8.refs_1_), channel_id=1, source_target_pairs={{0,2},{2,4},{4,6},{6,0},{1,3},{3,5},{5,7},{7,1},{8,10},{10,12},{12... | collective-permute-start | bytes 1572872 | tf_op jit(solution)/shard_map/rows/ppermute | solution.py:321
  83.7 17.9 %copy-start.19 = (f32[2,4096]{1,0:T(2,128)S(1)}, f32[2,4096]{1,0:T(2,128)}, u32[]{:S(2)}) copy-start(f32[2,4096]{1,0:T(2,128)} %param.19) | copy-start | bytes 98308
  91.1 7.8 %copy-start.15 = (bf16[384,1024]{1,0:T(8,128)(2,1)S(1)}, bf16[384,1024]{1,0:T(8,128)(2,1)}, u32[]{:S(2)}) copy-start(bf16[384,1024]{1,0:T(8,128)(2,1)} %get-tuple-element.49.refs_0_) | copy-start | bytes 2359300
  95.0 12.6 %collective-permute-start.15 = (bf16[256,384]{1,0:T(8,128)(2,1)}, bf16[256,384]{1,0:T(8,128)(2,1)S(1)}, u32[]{:S(2)}, u32[]{:S(2)}) collective-permute-start(bf16[256,384]{1,0:T(8,128)(2,1)} %up.5.refs_0_), channel_id=1, source_target_pairs={{0,4},{2,6},{4,0},{6,2},{1,5},{3,7},{5,1},{7,3},{8,12},{10,14},{12... | collective-permute-start | bytes 589832 | tf_op jit(solution)/shard_map/down/ppermute | solution.py:321
  96.3 11.5 %collective-permute-start.13 = (bf16[256,384]{1,0:T(8,128)(2,1)}, bf16[256,384]{1,0:T(8,128)(2,1)S(1)}, u32[]{:S(2)}, u32[]{:S(2)}) collective-permute-start(bf16[256,384]{1,0:T(8,128)(2,1)} %up.5.refs_0_), channel_id=1, source_target_pairs={{0,2},{2,4},{4,6},{6,0},{1,3},{3,5},{5,7},{7,1},{8,10},{10,12},{12... | collective-permute-start | bytes 589832 | tf_op jit(solution)/shard_map/down/ppermute | solution.py:321
  96.3 11.5 %collective-permute-start.14 = (bf16[256,384]{1,0:T(8,128)(2,1)}, bf16[256,384]{1,0:T(8,128)(2,1)S(1)}, u32[]{:S(2)}, u32[]{:S(2)}) collective-permute-start(bf16[256,384]{1,0:T(8,128)(2,1)} %up.5.refs_0_), channel_id=1, source_target_pairs={{0,6},{2,0},{4,2},{6,4},{1,7},{3,1},{5,3},{7,5},{8,14},{10,8},{12,... | collective-permute-start | bytes 589832 | tf_op jit(solution)/shard_map/down/ppermute | solution.py:321
  98.9 25.8 %collective-permute-start.17 = (bf16[384,1024]{1,0:T(8,128)(2,1)S(1)}, bf16[384,1024]{1,0:T(8,128)(2,1)}, u32[]{:S(2)}, u32[]{:S(2)}) collective-permute-start(bf16[384,1024]{1,0:T(8,128)(2,1)S(1)} %copy-done.15), channel_id=1, source_target_pairs={{0,2},{2,4},{4,6},{6,0},{1,3},{3,5},{5,7},{7,1},{8,10},{10,12},{12... | collective-permute-start | bytes 2359304 | tf_op jit(solution)/shard_map/rows/ppermute | solution.py:321
  99.0 25.8 %collective-permute-start.18 = (bf16[384,1024]{1,0:T(8,128)(2,1)}, bf16[384,1024]{1,0:T(8,128)(2,1)}, u32[]{:S(2)}, u32[]{:S(2)}) collective-permute-start(bf16[384,1024]{1,0:T(8,128)(2,1)} %collective-permute-done.16.refs_1_), channel_id=1, source_target_pairs={{0,6},{2,0},{4,2},{6,4},{1,7},{3,1},{5,3},{7,5},{8,14},{10,8},{12,... | collective-permute-start | bytes 2359304 | tf_op jit(solution)/shard_map/rows/ppermute | solution.py:321
  107.7 0.7 copy-start.16
  108.4 0.7 copy-start.18
  114.0 34.5 %all-to-all-start.1 = ((bf16[32,8,1024]{2,1,0:T(8,128)(2,1)}), bf16[32,8,1024]{2,1,0:T(8,128)(2,1)S(1)}, u32[]{:S(2)}, u32[]{:S(2)}) async-start(bf16[32,8,1024]{2,1,0:T(8,128)(2,1)} %bitcast.25), calls=%async_computation.1 | async-start | bytes 1048576 | tf_op jit(solution)/shard_map/down/all_to_all | solution.py:301
  123.5 9.8 %copy-start.8 = (bf16[192,1024]{1,0:T(8,128)(2,1)S(1)}, bf16[192,1024]{1,0:T(8,128)(2,1)}, u32[]{:S(2)}) copy-start(bf16[192,1024]{1,0:T(8,128)(2,1)} %get-tuple-element.29.refs_4_.same_ref) | copy-start | bytes 1179652
  124.7 19.5 %copy-start.10 = (f32[2,1,4096]{2,1,0:T(1,128)S(1)}, f32[2,1,4096]{2,1,0:T(1,128)}, u32[]{:S(2)}) copy-start(f32[2,1,4096]{2,1,0:T(1,128)} %reshape.34.refs_12_.refs_10_) | copy-start | bytes 98308
  124.7 19.5 %copy-start.11 = (bf16[256,128]{1,0:T(8,128)(2,1)S(1)}, bf16[256,128]{1,0:T(8,128)(2,1)}, u32[]{:S(2)}) copy-start(bf16[256,128]{1,0:T(8,128)(2,1)} %get-tuple-element.50.refs_11_) | copy-start | bytes 196612
  124.7 19.5 %copy-start.12 = (s32[2]{0:T(128)S(1)}, s32[2]{0:T(128)}, u32[]{:S(2)}) copy-start(s32[2]{0:T(128)} %pad_add_fusion.place_ref) | copy-start | bytes 28
  130.4 13.8 %copy-start.1 = (bf16[192,1024]{1,0:T(8,128)(2,1)S(1)}, bf16[192,1024]{1,0:T(8,128)(2,1)}, u32[]{:S(2)}) copy-start(bf16[192,1024]{1,0:T(8,128)(2,1)} %copy-done) | copy-start | bytes 1179652
  130.4 13.8 %copy-start.3 = (bf16[192,1024]{1,0:T(8,128)(2,1)S(1)}, bf16[192,1024]{1,0:T(8,128)(2,1)}, u32[]{:S(2)}) copy-start(bf16[192,1024]{1,0:T(8,128)(2,1)} %copy-done.2) | copy-start | bytes 1179652
  130.4 13.8 %copy-start.5 = (bf16[192,1024]{1,0:T(8,128)(2,1)S(1)}, bf16[192,1024]{1,0:T(8,128)(2,1)}, u32[]{:S(2)}) copy-start(bf16[192,1024]{1,0:T(8,128)(2,1)} %copy-done.4) | copy-start | bytes 1179652
  130.5 13.8 %copy-start.7 = (bf16[192,1024]{1,0:T(8,128)(2,1)S(1)}, bf16[192,1024]{1,0:T(8,128)(2,1)}, u32[]{:S(2)}) copy-start(bf16[192,1024]{1,0:T(8,128)(2,1)} %copy-done.6) | copy-start | bytes 1179652
  130.5 8.7 %collective-permute-start.19 = (bf16[384,384]{1,0:T(8,128)(2,1)}, bf16[384,384]{1,0:T(8,128)(2,1)S(1)}, u32[]{:S(2)}, u32[]{:S(2)}) collective-permute-start(bf16[384,384]{1,0:T(8,128)(2,1)} %up.7.h_ref), channel_id=1, source_target_pairs={{0,2},{2,4},{4,6},{6,0},{1,3},{3,5},{5,7},{7,1},{8,10},{10,12},{12... | collective-permute-start | bytes 884744 | tf_op jit(solution)/shard_map/down/ppermute | solution.py:321
  130.6 8.6 %collective-permute-start.20 = (bf16[384,384]{1,0:T(8,128)(2,1)}, bf16[384,384]{1,0:T(8,128)(2,1)S(1)}, u32[]{:S(2)}, u32[]{:S(2)}) collective-permute-start(bf16[384,384]{1,0:T(8,128)(2,1)} %up.7.h_ref), channel_id=1, source_target_pairs={{0,6},{2,0},{4,2},{6,4},{1,7},{3,1},{5,3},{7,5},{8,14},{10,8},{12,... | collective-permute-start | bytes 884744 | tf_op jit(solution)/shard_map/down/ppermute | solution.py:321
  133.2 11.0 %collective-permute-start.21 = (bf16[384,384]{1,0:T(8,128)(2,1)}, bf16[384,384]{1,0:T(8,128)(2,1)S(1)}, u32[]{:S(2)}, u32[]{:S(2)}) collective-permute-start(bf16[384,384]{1,0:T(8,128)(2,1)} %up.7.h_ref), channel_id=1, source_target_pairs={{0,4},{2,6},{4,0},{6,2},{1,5},{3,7},{5,1},{7,3},{8,12},{10,14},{12... | collective-permute-start | bytes 884744 | tf_op jit(solution)/shard_map/down/ppermute | solution.py:321
  133.3 1.0 copy-start.9
  148.5 9.5 %copy-start.13 = (s32[128,8]{0,1:T(8,128)S(1)}, s32[128,8]{0,1:T(8,128)}, u32[]{:S(2)}) copy-start(s32[128,8]{0,1:T(8,128)} %param.12) | copy-start | bytes 12292
  148.5 9.5 %copy-start.14 = (f32[128,8]{0,1:T(8,128)S(1)}, f32[128,8]{0,1:T(8,128)}, u32[]{:S(2)}) copy-start(f32[128,8]{0,1:T(8,128)} %param.13) | copy-start | bytes 12292
  148.5 28.6 %all-to-all-start.2 = ((bf16[32,8,1664]{2,1,0:T(8,128)(2,1)}), bf16[32,8,1664]{2,1,0:T(8,128)(2,1)S(1)}, u32[]{:S(2)}, u32[]{:S(2)}) async-start(bf16[32,8,1664]{2,1,0:T(8,128)(2,1)} %bitcast.11), calls=%async_computation.2 | async-start | bytes 1703936 | tf_op jit(solution)/shard_map/down/all_to_all | solution.py:301
  178.7 7.5 %collective-permute-start.22 = (f32[128,512]{1,0:T(8,128)S(1)}, f32[128,512]{1,0:T(8,128)S(1)}, u32[]{:S(2)}, u32[]{:S(2)}) collective-permute-start(f32[128,512]{1,0:T(8,128)S(1)} %get-tuple-element.52), channel_id=1, source_target_pairs={{0,1},{1,0},{2,3},{3,2},{4,5},{5,4},{6,7},{7,6},{8,9},{9,8},{10,11... | collective-permute-start | bytes 786440 | tf_op jit(solution)/shard_map/combine/ppermute | solution.py:459
  (1 other events, 0.7 us)
